TPU v7x, 256 devices: a whole 4x4x8 slice. The times are simulated.
256 devices in a mesh: grp: 16 (over z, core), voc: 16 (over y, x).
Axes of the slice: x: 4, y: 4, z: 8, core: 2. Of those that a mesh axis runs over, the one named last changes fastest.
Arguments:
- student_hidden: bfloat16 [384, 4096], P('grp', 'voc')
- norm_gain: float32 [4096], P('voc'), may hold values from 0.5 to 1.5
- teacher_hidden: bfloat16 [384, 5120], P('grp', 'voc')
- student_head: bfloat16 [4096, 98304], P(None, ('grp', 'voc'))
- teacher_head: bfloat16 [5120, 98304], P(None, ('grp', 'voc'))
- episode_source: int32 [192], replicated, may hold values from 0 to 191, as said below
- lengths: int32 [192], replicated, may hold values from 1 to 2, 240 in all
Outputs:
- loss: float32 [], replicated
- grad_hidden: bfloat16 [384, 4096], P('grp', 'voc')
- grad_gain: float32 [4096], P('voc')
- grad_head: bfloat16 [4096, 98304], P(None, ('grp', 'voc'))
Inputs may be any that keep to these rules, and one draw needn't show every extreme that they name: `episode_source`: A permutation of the episodes. Student episodes 12 * s to 12 * s + 11 form group s, teacher episodes likewise form teacher group t; at most 2 episodes of one student group come from one teacher group, and that many in some pair.
All inputs are finite; a program needn't handle non-finite values.
Results may differ from a plain program's by a relative error of at most 0.04.
Values may be sent and summed in bfloat16 or wider, within the bound.
No kernel may reach another device: no remote copies, remote signals or barrier semaphores. Data moves between devices by JAX's collectives and lax.ppermute only.
A program may use at most 64 MiB of HBM per device.

v0:
```python
import jax
import jax.numpy as jnp
from jax import lax
from jax.sharding import PartitionSpec as P

DS = 4096
SEQ = 2
MOST = 2


EPSILON = 1e-06


def realign(teacher_hidden, table, group_index, per_group):
    groups = table.shape[0]
    source_group = table // per_group
    source_local = table % per_group
    mine = (source_group == group_index).astype(jnp.int32)
    earlier = jnp.cumsum(mine, axis=1) - mine
    slot_ids = jnp.arange(MOST, dtype=jnp.int32)
    matches = mine[:, :, None] * (earlier[:, :, None] == slot_ids[None, None, :]).astype(jnp.int32)
    send_index = jnp.sum(matches * source_local[:, :, None], axis=1)
    features = teacher_hidden.shape[1]
    episodes = teacher_hidden.reshape(per_group, SEQ, features)
    outgoing = jnp.take(episodes, send_index, axis=0)
    incoming = lax.all_to_all(outgoing, "grp", split_axis=0, concat_axis=0, tiled=True)
    own_groups = lax.dynamic_index_in_dim(source_group, group_index, 0, keepdims=False)
    matching = (own_groups[:, None] == own_groups[None, :]).astype(jnp.int32)
    position = jnp.sum(jnp.tril(matching, -1), axis=1)
    flat_index = own_groups * MOST + position
    received = incoming.reshape(groups * MOST, SEQ, features)
    return jnp.take(received, flat_index, axis=0).reshape(per_group * SEQ, features)


def local(
    student_hidden, norm_gain, teacher_hidden, student_head, teacher_head, episode_source, lengths
):
    groups = lax.axis_size("grp")
    group_index = lax.axis_index("grp")
    rows_group = student_hidden.shape[0]
    per_group = rows_group // SEQ
    hidden_f32 = student_hidden.astype(jnp.float32)
    squares = lax.psum(jnp.sum(hidden_f32 * hidden_f32, axis=1), "voc")
    inverse_rms = lax.rsqrt(squares / DS + EPSILON)
    normed = (hidden_f32 * inverse_rms[:, None] * norm_gain[None, :]).astype(jnp.bfloat16)
    table = episode_source.reshape(groups, per_group)
    aligned = realign(teacher_hidden, table, group_index, per_group)
    teacher_rows, student_rows = (
        lax.all_gather(aligned, "voc", axis=1, tiled=True),
        lax.all_gather(normed, "voc", axis=1, tiled=True),
    )
    teacher_logits = jnp.dot(
        lax.all_gather(teacher_rows, "grp", axis=0, tiled=True),
        teacher_head,
        preferred_element_type=jnp.float32,
    )
    positions = jnp.arange(SEQ, dtype=jnp.int32)
    all_rows = lax.all_gather(student_rows, "grp", axis=0, tiled=True)
    student_logits = jnp.dot(all_rows, student_head, preferred_element_type=jnp.float32)
    lengths_f32 = lengths.astype(jnp.float32)
    valid = positions[None, :] < lengths[:, None]
    token_weight = jnp.where(
        valid, 1.0 / lengths_f32[:, None], jnp.zeros_like(lengths_f32)[:, None]
    ).reshape(-1)
    top_student, top_teacher = lax.pmax(
        (jnp.max(student_logits, axis=1), jnp.max(teacher_logits, axis=1)), ("grp", "voc")
    )
    exp_student = jnp.exp(student_logits - top_student[:, None])
    exp_teacher = jnp.exp(teacher_logits - top_teacher[:, None])
    total_student, total_teacher = lax.psum(
        (jnp.sum(exp_student, axis=1), jnp.sum(exp_teacher, axis=1)), ("grp", "voc")
    )
    log_student = student_logits - (top_student + jnp.log(total_student))[:, None]
    log_teacher = teacher_logits - (top_teacher + jnp.log(total_teacher))[:, None]
    prob_student = jnp.exp(log_student)
    log_ratio = log_student - log_teacher
    divergence = lax.psum(jnp.sum(prob_student * log_ratio, axis=1), ("grp", "voc"))
    loss = jnp.sum(token_weight * divergence)
    logit_grad = (token_weight[:, None] * prob_student * (log_ratio - divergence[:, None])).astype(
        jnp.bfloat16
    )
    grad_head = lax.dot_general(
        all_rows, logit_grad, (((0,), (0,)), ((), ())), preferred_element_type=jnp.float32
    ).astype(jnp.bfloat16)
    full_term = lax.dot_general(
        logit_grad, student_head, (((1,), (1,)), ((), ())), preferred_element_type=jnp.float32
    )
    feature_part = lax.psum_scatter(
        full_term.astype(jnp.bfloat16), "voc", scatter_dimension=1, tiled=True
    )
    normed_grad = lax.psum_scatter(feature_part, "grp", scatter_dimension=0, tiled=True).astype(
        jnp.float32
    )
    scaled = normed_grad * norm_gain[None, :]
    inner = lax.psum(jnp.sum(scaled * hidden_f32, axis=1), "voc")
    grad_hidden = (
        inverse_rms[:, None] * scaled - hidden_f32 * (inverse_rms**3)[:, None] * inner[:, None] / DS
    )
    grad_gain = lax.psum(jnp.sum(normed_grad * hidden_f32 * inverse_rms[:, None], axis=0), "grp")
    return (loss, grad_hidden.astype(jnp.bfloat16), grad_gain, grad_head)


def solution(mesh):
    placed = (
        P("grp", "voc"),
        P("voc"),
        P("grp", "voc"),
        P(None, ("grp", "voc")),
        P(None, ("grp", "voc")),
        P(),
        P(),
    )
    return jax.shard_map(
        local,
        mesh=mesh,
        in_specs=placed,
        out_specs=(P(), P("grp", "voc"), P("voc"), P(None, ("grp", "voc"))),
        check_vma=False,
    )
```

profile of v0, /device:TPU:1, one launch (start us, length us, event | category | flops | bytes accessed | tf_op | source)
XLA Modules:
  0.0 604.3 jit_solution(17065896833166777343)
XLA Ops:
  7.2 1.0 fusion.4
  8.2 34.3 %psum.42 = f32[24]{0:T(128)S(1)} all-reduce(f32[24]{0:T(128)S(1)} %fusion.4), channel_id=1, replica_groups=mesh['grp'=16,'voc'=16] {'voc'}, use_global_device_ids=true, to_apply=%region_1.0 | all-reduce | flops 24 | bytes 192 | tf_op jit(solution)/shard_map/psum | solution.py:43
  43.2 17.4 %all_gather.12 = bf16[24,4096]{1,0:T(8,128)(2,1)} all-gather(bf16[24,256]{1,0:T(8,128)(2,1)S(1)} %fusion.6), channel_id=1, replica_groups=mesh['grp'=16,'voc'=16] {'voc'}, dimensions={1}, use_global_device_ids=true | all-gather | bytes 208896 | tf_op jit(solution)/shard_map/all_gather | solution.py:50
  65.2 21.3 %all-to-all-start = ((bf16[16,2,2,320]{3,2,1,0:T(2,128)(2,1)}), bf16[16,2,2,320]{3,2,1,0:T(2,128)(2,1)S(1)}, u32[]{:S(2)}, u32[]{:S(2)}) async-start(bf16[16,2,2,320]{3,2,1,0:T(2,128)(2,1)} %broadcast_select_fusion), calls=%async_computation | async-start | bytes 98304 | tf_op jit(solution)/shard_map/all_to_all | solution.py:26
  87.0 7.4 %all-to-all-done = bf16[16,2,2,320]{3,2,1,0:T(2,128)(2,1)S(1)} async-done(((bf16[16,2,2,320]{3,2,1,0:T(2,128)(2,1)}), bf16[16,2,2,320]{3,2,1,0:T(2,128)(2,1)S(1)}, u32[]{:S(2)}, u32[]{:S(2)}) %all-to-all-start) | async-done | bytes 40992 | tf_op jit(solution)/shard_map/all_to_all | solution.py:26
  95.1 20.8 %all-gather = bf16[16,320,24]{1,2,0:T(8,128)(2,1)S(1)} all-gather(bf16[1,320,24]{1,2,0:T(8,128)(2,1)S(1)} %select_bitcast_fusion), channel_id=1, replica_groups=mesh['grp'=16,'voc'=16] {'voc'}, dimensions={0}, use_global_device_ids=true | all-gather | bytes 261120 | tf_op jit(solution)/shard_map/all_gather | solution.py:49
  116.0 1.0 reshape.201
  118.7 4.5 fusion.17
  123.2 36.1 %all-gather.6.cloned.1.call-done = bf16[384,5120]{1,0:T(8,128)(2,1)} async-done(((bf16[24,5120]{1,0:T(8,128)(2,1)}), bf16[384,5120]{1,0:T(8,128)(2,1)}) %all-gather.6.cloned.1.call-update) | async-done | bytes 3932176 | tf_op jit(solution)/shard_map/all_gather | solution.py:53
  159.3 6.4 %fusion.16 = (f32[384]{0:T(512)S(1)}, f32[384,384]{0,1:T(8,128)}) fusion(bf16[384,5120]{1,0:T(8,128)(2,1)} %all-gather.6.cloned.1.call-done, bf16[5120,384]{1,0:T(8,128)(2,1)} %param.11), kind=kOutput, calls=%fused_computation.61 | convolution fusion | flops 1510096512 | bytes 8455680 | tf_op jit(solution)/shard_map/dot_general | solution.py:52
  165.7 76.1 %all-reduce.1 = (f32[384]{0:T(512)S(1)}, f32[384]{0:T(512)S(1)}) all-reduce(f32[384]{0:T(512)S(1)} %get-tuple-element.16, f32[384]{0:T(512)S(1)} %get-tuple-element.18), channel_id=1, replica_groups=mesh['grp'=16,'voc'=16] {'grp','voc'}, use_global_device_ids=true, to_apply=%region_10.11 | all-reduce | flops 768 | bytes 6144 | tf_op jit(solution)/shard_map/pmax | solution.py:65
  241.8 1.4 exponential_reduce_fusion
  243.2 72.5 %all-reduce = (f32[384]{0:T(512)S(1)}, f32[384]{0:T(512)S(1)}) all-reduce(f32[384]{0:T(512)S(1)} %get-tuple-element.20, f32[384]{0:T(512)S(1)} %get-tuple-element.21), channel_id=1, replica_groups=mesh['grp'=16,'voc'=16] {'grp','voc'}, use_global_device_ids=true, to_apply=%region_12.13 | all-reduce | flops 768 | bytes 6144 | tf_op jit(solution)/shard_map/psum | solution.py:70
  315.7 1.4 multiply_reduce_fusion
  317.1 73.9 %psum.45 = f32[384]{0:T(512)S(1)} all-reduce(f32[384]{0:T(512)S(1)} %multiply_reduce_fusion), channel_id=1, replica_groups=mesh['grp'=16,'voc'=16] {'grp','voc'}, use_global_device_ids=true, to_apply=%region_14.15 | all-reduce | flops 384 | bytes 3072 | tf_op jit(solution)/shard_map/psum | solution.py:77
  391.0 1.4 multiply_convert_fusion
  392.4 3.5 convolution_convert_fusion.1
  396.2 75.2 %reduce-scatter.3.cloned.1.call-done = bf16[384,256]{1,0:T(8,128)(2,1)} async-done(((bf16[384,4096]{1,0:T(8,128)(2,1)}), bf16[384,256]{1,0:T(8,128)(2,1)}) %reduce-scatter.3.cloned.1.call-update) | async-done | bytes 196624 | tf_op jit(solution)/shard_map/reduce_scatter | solution.py:88
  472.1 5.7 convolution_convert_fusion
  477.8 50.2 %reduce-scatter.5.cloned.1.call-done = bf16[24,256]{1,0:T(8,128)(2,1)} async-done(((bf16[384,256]{1,0:T(8,128)(2,1)}), bf16[24,256]{1,0:T(8,128)(2,1)}) %reduce-scatter.5.cloned.1.call-update) | async-done | bytes 12304 | tf_op jit(solution)/shard_map/reduce_scatter | solution.py:91
  528.0 0.9 fusion.11
  528.9 33.3 %psum.46 = f32[24]{0:T(128)S(1)} all-reduce(f32[24]{0:T(128)S(1)} %get-tuple-element.5), channel_id=1, replica_groups=mesh['grp'=16,'voc'=16] {'voc'}, use_global_device_ids=true, to_apply=%region_19.20 | all-reduce | flops 24 | bytes 192 | tf_op jit(solution)/shard_map/psum | solution.py:95
  562.3 34.1 %psum.47 = f32[256]{0:T(256)} all-reduce(f32[256]{0:T(256)S(1)} %get-tuple-element.4), channel_id=1, replica_groups=mesh['grp'=16,'voc'=16] {'grp'}, use_global_device_ids=true, to_apply=%region_21.22 | all-reduce | flops 256 | bytes 2048 | tf_op jit(solution)/shard_map/psum | solution.py:99
  596.4 1.4 fusion.3
  (57 shorter events, 9.1 us)
Async XLA Ops:
  7.2 111.5 %copy-start = (bf16[4096,384]{1,0:T(8,128)(2,1)S(1)}, bf16[4096,384]{1,0:T(8,128)(2,1)}, u32[]{:S(2)}) copy-start(bf16[4096,384]{1,0:T(8,128)(2,1)} %param.10) | copy-start | bytes 9437188
  7.2 111.5 %all-gather.4.cloned.1.call-start = ((), (), s32[]{:S(2)}) async-start(), calls=%async_computation.3 | async-start | bytes 3342336 | tf_op jit(solution)/shard_map/all_gather | solution.py:58
  65.2 29.2 %all-to-all-start = ((bf16[16,2,2,320]{3,2,1,0:T(2,128)(2,1)}), bf16[16,2,2,320]{3,2,1,0:T(2,128)(2,1)S(1)}, u32[]{:S(2)}, u32[]{:S(2)}) async-start(bf16[16,2,2,320]{3,2,1,0:T(2,128)(2,1)} %broadcast_select_fusion), calls=%async_computation | async-start | bytes 98304 | tf_op jit(solution)/shard_map/all_to_all | solution.py:26
  86.5 72.8 %all-gather.6.cloned.1.call-start = ((), (), s32[]{:S(2)}) async-start(), calls=%async_computation.4 | async-start | bytes 4177920 | tf_op jit(solution)/shard_map/all_gather | solution.py:53
  117.0 354.5 %reduce-scatter.3.cloned.1.call-start = ((), (), s32[]{:S(2)}) async-start(), calls=%async_computation.5 | async-start | bytes 3342336 | tf_op jit(solution)/shard_map/reduce_scatter | solution.py:88
  396.0 132.0 %reduce-scatter.5.cloned.1.call-start = ((), (), s32[]{:S(2)}) async-start(), calls=%async_computation.6 | async-start | bytes 208896 | tf_op jit(solution)/shard_map/reduce_scatter | solution.py:91
  472.1 55.9 %copy-start.1 = (bf16[24,256]{1,0:T(8,128)(2,1)S(1)}, bf16[24,256]{1,0:T(8,128)(2,1)}, u32[]{:S(2)}) copy-start(bf16[24,256]{1,0:T(8,128)(2,1)} %param.7) | copy-start | bytes 36868
  472.1 55.9 %copy-start.2 = (f32[256]{0:T(256)S(1)}, f32[256]{0:T(256)}, u32[]{:S(2)}) copy-start(f32[256]{0:T(256)} %param.8) | copy-start | bytes 3076
Sparse Core Ops, SparseCore 0:
  60.7 55.4 all-gather.3
  118.1 41.2 all-gather.5
  396.1 75.3 reduce-scatter.2
  473.8 54.1 reduce-scatter.4
where the time goes:
time: 606 us; the launch traced here: 604 us
  blocking collectives  362 us (60%)
  waiting for transfers between devices  169 us (28%)
  starting transfers between devices  21.6 us (4%)
  matrix products  20.1 us (3%)
  between operations  13.9 us (2%)
  other arithmetic  13 us (2%)
    pmax x1, blocking collectives, local(): lax.pmax((jnp.max(student_logits, axis=1), jnp.max(teacher_logits, axis=1...  76.1 us
    reduce_scatter x1, waiting for transfers between devices, local(): lax.psum_scatter(full_term.astype(jnp.bfloat16), 'voc', scatter_dimension...  75.2 us
    psum x1, blocking collectives, local(): lax.psum(jnp.sum(prob_student * log_ratio, axis=1), ('grp', 'voc'))  73.9 us
    psum x1, blocking collectives, local(): lax.psum((jnp.sum(exp_student, axis=1), jnp.sum(exp_teacher, axis=1)), ('...  72.5 us
    reduce_scatter x1, waiting for transfers between devices, local(): lax.psum_scatter(feature_part, 'grp', scatter_dimension=0, tiled=True)  50.2 us
    all_gather x1, waiting for transfers between devices, local(): lax.all_gather(teacher_rows, 'grp', axis=0, tiled=True)  36.1 us
    psum x1, blocking collectives, local(): squares = lax.psum(jnp.sum(hidden_f32 * hidden_f32, axis=1), 'voc')  34.3 us
    psum x1, blocking collectives, local(): lax.psum(jnp.sum(normed_grad * hidden_f32 * inverse_rms[:, None], axis=0)...  34.1 us
  transfers between devices with their start and end apart: 5, of which 4 were waited for; matrix products, arithmetic and copies ran while one was open for 3% of the time, Pallas kernels for 0%

commit v1 on v0

v1 whole, which is shorter than its diff:
```python
import jax
import jax.numpy as jnp
from jax import lax
from jax.sharding import PartitionSpec as P

DS = 4096
SEQ = 2
VALID = 240
LANES = 256
EPSILON = 1e-06
BF = jnp.bfloat16
F32 = jnp.float32
CORE_SWAP = [(i, i ^ 1) for i in range(16)]


def rounded(x):
    return lax.reduce_precision(x, 8, 7)


def lane_tables(episode_source, lengths):
    episodes = lengths.shape[0]
    two = (lengths == 2).astype(jnp.int32)
    before = jnp.arange(episodes)[None, :] < jnp.arange(episodes)[:, None]
    rank = jnp.sum(jnp.where(before, two[None, :], 0), axis=1)
    lane = jnp.arange(LANES, dtype=jnp.int32)
    number = jnp.arange(episodes, dtype=jnp.int32)
    first = lane[None, :] == number[:, None]
    second = (two[:, None] == 1) & (lane[None, :] == episodes + rank[:, None])
    pick = first | second
    position = (lane >= episodes).astype(jnp.int32)
    inside = lane < VALID
    episode = jnp.sum(jnp.where(pick, number[:, None], 0), axis=0)
    source = jnp.sum(jnp.where(pick, episode_source[:, None], 0), axis=0)
    length = jnp.sum(jnp.where(pick, lengths[:, None], 0), axis=0)
    student_row = jnp.where(inside, episode * SEQ + position, -1)
    teacher_row = jnp.where(inside, source * SEQ + position, -1)
    weight = jnp.where(inside, 1.0 / jnp.maximum(length, 1).astype(F32), 0.0)
    return student_row, teacher_row, weight


def combine(stats):
    top_s, sum_s, top_t, sum_t, mean_d, mean_u, mean_du = [stats[:, k] for k in range(7)]
    all_s = jnp.max(top_s, axis=0)
    all_t = jnp.max(top_t, axis=0)
    shift_s = top_s - all_s[None]
    shift_t = top_t - all_t[None]
    scale_s = jnp.exp(shift_s)
    scale_t = jnp.exp(shift_t)
    shift_d = shift_s - shift_t
    out = [
        all_s,
        jnp.sum(scale_s * sum_s, axis=0),
        all_t,
        jnp.sum(scale_t * sum_t, axis=0),
        jnp.sum(scale_s * (mean_d + shift_d * sum_s), axis=0),
        jnp.sum(scale_s * (mean_u + shift_s * sum_s), axis=0),
        jnp.sum(
            scale_s
            * (mean_du + shift_s * mean_d + shift_d * mean_u + shift_s * shift_d * sum_s),
            axis=0,
        ),
    ]
    return jnp.stack(out + [jnp.zeros_like(all_s)])


def spread(x, axis):
    count = lax.axis_size(axis)
    return lax.all_to_all(jnp.broadcast_to(x[None], (count,) + x.shape), axis, 0, 0, tiled=True)


def with_gain(total):
    gain = total[..., VALID : VALID + 1] + total[..., VALID + 1 : VALID + 2]
    high = rounded(gain)
    lane = lax.broadcasted_iota(jnp.int32, total.shape, total.ndim - 1)
    kept = jnp.where(lane == VALID, high, jnp.where(lane == VALID + 1, gain - high, total))
    return kept.astype(BF)


def local(
    student_hidden, norm_gain, teacher_hidden, student_head, teacher_head, episode_source, lengths
):
    groups = lax.axis_size("grp")
    voc = lax.axis_size("voc")
    group_index = lax.axis_index("grp")
    core = group_index % 2
    rows = student_hidden.shape[0]
    half_s = student_hidden.shape[1] // 2
    half_t = teacher_hidden.shape[1] // 2
    half = half_s + half_t
    student_row, teacher_row, weight = lane_tables(episode_source, lengths)
    row_ids = jnp.arange(groups * rows, dtype=jnp.int32)
    lane = jnp.arange(LANES, dtype=jnp.int32)
    select_s = (row_ids[:, None] == student_row[None, :]).astype(BF)
    select_t = (row_ids[:, None] == teacher_row[None, :]).astype(BF)

    both = jnp.stack(
        [
            jnp.concatenate([student_hidden[:, :half_s], teacher_hidden[:, :half_t]], axis=1),
            jnp.concatenate([student_hidden[:, half_s:], teacher_hidden[:, half_t:]], axis=1),
        ]
    )
    outgoing = jnp.broadcast_to(both[None], (groups // 2, 2, rows, half)).reshape(groups, rows, half)
    held = lax.all_to_all(outgoing, "grp", 0, 0, tiled=True).reshape(groups * rows, half)

    transposed = (((0,), (0,)), ((), ()))
    block_s = lax.dot_general(
        held[:, :half_s], select_s, transposed, preferred_element_type=F32
    )
    block_t = lax.dot_general(
        held[:, half_s:], select_t, transposed, preferred_element_type=F32
    )
    gain_half = lax.dynamic_slice_in_dim(norm_gain, core * half_s, half_s)[:, None]
    gain_high = rounded(gain_half)
    gain_mid = rounded(gain_half - gain_high)
    gain_low = gain_half - gain_high - gain_mid
    block_s = jnp.where(
        lane == VALID,
        gain_high,
        jnp.where(lane == VALID + 1, gain_mid, jnp.where(lane == VALID + 2, gain_low, block_s)),
    )
    block = jnp.concatenate([block_s.astype(BF), block_t.astype(BF)], axis=0)
    mine = spread(block, "voc")
    other = lax.ppermute(mine, "grp", CORE_SWAP)
    ordered = jnp.stack(
        [jnp.where(core == 0, mine, other), jnp.where(core == 0, other, mine)], axis=1
    )
    hidden_t = ordered[:, :, :half_s].reshape(DS, LANES).astype(F32)
    teacher_t = ordered[:, :, half_s:].reshape(-1, LANES)

    gain = jnp.sum(hidden_t[:, VALID : VALID + 3], axis=1, keepdims=True)
    inverse_rms = lax.rsqrt(jnp.sum(hidden_t * hidden_t, axis=0) / DS + EPSILON)
    inside = lane < VALID
    scaled_rows = jnp.where(inside, hidden_t * inverse_rms, 0.0)
    normed_t = (scaled_rows * gain).astype(BF)

    student = lax.dot_general(student_head, normed_t, transposed, preferred_element_type=F32)
    teacher = lax.dot_general(teacher_head, teacher_t, transposed, preferred_element_type=F32)
    top_s = jnp.max(student, axis=0)
    top_t = jnp.max(teacher, axis=0)
    below = student - top_s
    exp_s = jnp.exp(below)
    below_t = teacher - top_t
    ratio = below - below_t
    stats = jnp.stack(
        [
            top_s,
            jnp.sum(exp_s, axis=0),
            top_t,
            jnp.sum(jnp.exp(below_t), axis=0),
            jnp.sum(exp_s * ratio, axis=0),
            jnp.sum(exp_s * below, axis=0),
            jnp.sum(exp_s * ratio * below, axis=0),
            jnp.zeros_like(top_s),
        ]
    )
    stats = combine(spread(stats, "voc"))
    stats = combine(spread(stats, "grp"))
    all_s, total_s, all_t, total_t = stats[0], stats[1], stats[2], stats[3]
    mean_d = stats[4] / total_s
    mean_u = stats[5] / total_s
    covariance = stats[6] / total_s - mean_d * mean_u
    divergence = mean_d - jnp.log(total_s) + jnp.log(total_t)
    loss = jnp.sum(weight * divergence)
    factor = weight * jnp.exp(top_s - all_s) / total_s
    offset = (top_s - all_s) - (top_t - all_t) - mean_d
    grad_t = (factor * exp_s * (ratio + offset)).astype(BF)

    term = lax.dot_general(
        student_head, grad_t, (((1,), (0,)), ((), ())), preferred_element_type=F32
    )
    gain_term = jnp.sum(term * scaled_rows, axis=1, keepdims=True)
    gain_top = rounded(gain_term)
    term = jnp.where(
        lane == VALID, gain_top, jnp.where(lane == VALID + 1, gain_term - gain_top, term)
    ).astype(BF)
    term = term.reshape(voc, 2, half_s, LANES)
    away = lax.dynamic_index_in_dim(term, 1 - core, 1, keepdims=False)
    stay = lax.dynamic_index_in_dim(term, core, 1, keepdims=False)
    arrived = lax.ppermute(away, "grp", CORE_SWAP)
    grad_head = lax.dot_general(
        normed_t, grad_t, (((1,), (1,)), ((), ())), preferred_element_type=F32
    ).astype(BF)
    pair = with_gain(stay.astype(F32) + arrived.astype(F32))
    pieces = lax.all_to_all(pair, "voc", 0, 0, tiled=True)
    feature_sum = with_gain(jnp.sum(pieces.astype(F32), axis=0))

    extra = 8
    slot = jnp.arange(rows + extra, dtype=jnp.int32)
    wanted = jnp.where(
        slot[None, :] < rows,
        jnp.arange(groups, dtype=jnp.int32)[:, None] * rows + slot[None, :],
        -2,
    )
    lane_row = jnp.where(inside, student_row, -1)
    select_out = (wanted[:, :, None] == lane_row) | (
        (slot[None, :, None] >= rows) & (lane == slot[None, :, None] - rows + VALID) & (lane < VALID + 2)
    )
    outgoing = lax.dot_general(
        select_out.reshape(-1, LANES).astype(BF),
        feature_sum,
        (((1,), (1,)), ((), ())),
        preferred_element_type=F32,
    ).astype(BF).reshape(groups, rows + extra, half_s)
    pieces = lax.all_to_all(outgoing, "grp", 0, 0, tiled=True)
    total = jnp.sum(pieces.reshape(groups // 2, 2, rows + extra, half_s).astype(F32), axis=0)
    total = jnp.concatenate([total[0], total[1]], axis=1)
    normed_grad = total[:rows]
    grad_gain = total[rows] + total[rows + 1]

    own = (group_index * rows + jnp.arange(rows, dtype=jnp.int32))[:, None] == student_row[None, :]
    own_rms = jnp.sum(jnp.where(own, inverse_rms, 0.0), axis=1, keepdims=True)
    pull = weight * covariance * inverse_rms * inverse_rms / DS
    own_pull = jnp.sum(jnp.where(own, pull, 0.0), axis=1, keepdims=True)
    grad_hidden = own_rms * (normed_grad * norm_gain) - student_hidden.astype(F32) * own_pull
    return (loss, grad_hidden.astype(BF), grad_gain, grad_head)


def solution(mesh):
    placed = (
        P("grp", "voc"),
        P("voc"),
        P("grp", "voc"),
        P(None, ("grp", "voc")),
        P(None, ("grp", "voc")),
        P(),
        P(),
    )
    return jax.shard_map(
        local,
        mesh=mesh,
        in_specs=placed,
        out_specs=(P(), P("grp", "voc"), P("voc"), P(None, ("grp", "voc"))),
        check_vma=False,
    )
```

time: 606 us -> 214 us (0.35)
  blocking collectives: 362 us -> 47.9 us
  waiting for transfers between devices: 169 us -> 40 us
  local copies, waits for them, and re-layouts: 4.13 us -> 47.6 us
  other arithmetic: 13 us -> 32.1 us
  between operations: 13.9 us -> 1.04 us
    psum x5 -> x0, blocking collectives: 248 us -> none  [the longest x1 73.9 us: local(): lax.psum(jnp.sum(prob_student * log_ratio, axis=1), ('grp', 'voc'))]
    reduce_scatter x2 -> x0, waiting for transfers between devices: 125 us -> none  [the longest x1 75.2 us: local(): lax.psum_scatter(full_term.astype(jnp.bfloat16), 'voc', scatter_dimension...]
    pmax x1 -> x0, blocking collectives: 76.1 us -> none  [local(): lax.pmax((jnp.max(student_logits, axis=1), jnp.max(teacher_logits, axis=1...]
    all_to_all x0 -> x2, blocking collectives: none -> 47.9 us  [spread(): lax.all_to_all(jnp.broadcast_to(x[None], (count,) + x.shape), axis, 0, 0,...]
    all_gather x2 -> x0, blocking collectives: 38.2 us -> none  [the longest x1 20.8 us: local(): lax.all_gather(aligned, 'voc', axis=1, tiled=True)]
    all_gather x2 -> x0, waiting for transfers between devices: 36.1 us -> none  [the longest x1 36.1 us: local(): lax.all_gather(teacher_rows, 'grp', axis=0, tiled=True)]
    all_to_all x1 -> x4, waiting for transfers between devices: 7.38 us -> 35.5 us  [the longest x1 13 us: local(): pieces = lax.all_to_all(pair, 'voc', 0, 0, tiled=True)]
    convert_element_type x1 -> x2, local copies, waits for them, and re-layouts: 0.08 us -> 13.8 us  [local(): hidden_t = ordered[:, :, :half_s].reshape(DS, LANES).astype(F32)]
  transfers between devices with their start and end apart: 5 -> 6, of which waited for: 4 -> 5; matrix products, arithmetic and copies ran while one was open for 3% -> 9% of each run, Pallas kernels for 0% -> 0%
where the time goes in v1:
time: 214 us; the launch traced here: 213 us
  blocking collectives  47.9 us (22%)
  local copies, waits for them, and re-layouts  47.6 us (22%)
  waiting for transfers between devices  40 us (19%)
  other arithmetic  32.1 us (15%)
  starting transfers between devices  27.1 us (13%)
  matrix products  16.9 us (8%)
    all_to_all x2, blocking collectives, spread(): lax.all_to_all(jnp.broadcast_to(x[None], (count,) + x.shape), axis, 0, 0,...  47.9 us
    convert_element_type x2, local copies, waits for them, and re-layouts, local(): hidden_t = ordered[:, :, :half_s].reshape(DS, LANES).astype(F32)  13.8 us
    all_to_all x1, waiting for transfers between devices, local(): pieces = lax.all_to_all(pair, 'voc', 0, 0, tiled=True)  13 us
    unnamed x48, local copies, waits for them, and re-layouts  12.4 us
    all_to_all x1, starting transfers between devices, local(): lax.all_to_all(outgoing, 'grp', 0, 0, tiled=True)  9.98 us
    all_to_all x1, waiting for transfers between devices, spread(): lax.all_to_all(jnp.broadcast_to(x[None], (count,) + x.shape), axis, 0, 0,...  9.32 us
    all_to_all x1, waiting for transfers between devices, local(): lax.all_to_all(outgoing, 'grp', 0, 0, tiled=True)  8.77 us
    dynamic_slice x1, local copies, waits for them, and re-layouts, local(): stay = lax.dynamic_index_in_dim(term, core, 1, keepdims=False)  8.58 us
  transfers between devices with their start and end apart: 6, of which 5 were waited for; matrix products, arithmetic and copies ran while one was open for 9% of the time, Pallas kernels for 0%

profile of v1, /device:TPU:1, one launch (start us, length us, event | category | flops | bytes accessed | tf_op | source)
XLA Modules:
  0.0 212.7 jit_solution(2350051229566878183)
XLA Ops:
  3.1 10.0 %all-to-all-start = ((bf16[16,24,288]{2,1,0:T(8,128)(2,1)}), bf16[16,24,288]{2,1,0:T(8,128)(2,1)S(1)}, u32[]{:S(2)}, u32[]{:S(2)}) async-start(bf16[16,24,288]{2,1,0:T(8,128)(2,1)} %bitcast.2), calls=%async_computation | async-start | bytes 589824 | tf_op jit(solution)/shard_map/all_to_all | solution.py:103
  16.7 8.8 %all-to-all-done = bf16[16,24,288]{2,1,0:T(8,128)(2,1)S(1)} async-done(((bf16[16,24,288]{2,1,0:T(8,128)(2,1)}), bf16[16,24,288]{2,1,0:T(8,128)(2,1)S(1)}, u32[]{:S(2)}, u32[]{:S(2)}) %all-to-all-start) | async-done | bytes 221216 | tf_op jit(solution)/shard_map/all_to_all | solution.py:103
  26.2 38.5 %all_to_all.30 = bf16[16,288,256]{2,1,0:T(8,128)(2,1)} all-to-all(bf16[16,288,256]{2,1,0:T(8,128)(2,1)S(1)} %broadcast_in_dim.244), channel_id=1, replica_groups=mesh['grp'=16,'voc'=16] {'voc'}, dimensions={0} | all-to-all | bytes 4718592 | tf_op jit(solution)/shard_map/all_to_all | solution.py:68
  65.7 4.5 %collective-permute-done = bf16[16,288,256]{2,1,0:T(8,128)(2,1)} collective-permute-done((bf16[16,288,256]{2,1,0:T(8,128)(2,1)}, bf16[16,288,256]{2,1,0:T(8,128)(2,1)}, u32[]{:S(2)}, u32[]{:S(2)}) %collective-permute-start) | collective-permute-done | bytes 2359328 | tf_op jit(solution)/shard_map/ppermute | solution.py:123
  70.2 2.7 %select_bitcast_fusion.1 = (bf16[16,1,288,256]{3,2,0,1:T(8,128)(2,1)S(1)}, bf16[16,1,288,256]{3,2,0,1:T(8,128)(2,1)S(1)}) fusion(bf16[16,288,256]{2,1,0:T(8,128)(2,1)} %all_to_all.30, bf16[16,288,256]{2,1,0:T(8,128)(2,1)} %collective-permute-done, pred[]{:T(512)S(6)} %eq.163), kind=kLoop, calls=%fused_computation.9 | loop fusion | flops 2359296 | bytes 9437185 | tf_op jit(solution)/shard_map/stack | solution.py:124
  73.1 2.5 %multiply_reduce_fusion.1 = (f32[256]{0:T(256)S(1)}, f32[16,2,128,256]{3,2,0,1:T(8,128)}) fusion(bf16[16,1,288,256]{3,2,0,1:T(8,128)(2,1)S(1)} %get-tuple-element.37, bf16[16,1,288,256]{3,2,0,1:T(8,128)(2,1)S(1)} %get-tuple-element.36), kind=kLoop, calls=%fused_computation.6 | loop fusion | flops 6291200 | bytes 8913920 | tf_op jit(solution)/shard_map/reduce_sum | solution.py:131
  77.3 7.4 %copy.61 = f32[16,2,128,256]{2,1,0,3:T(2,128)} copy(f32[16,2,128,256]{3,2,0,1:T(8,128)} %get-tuple-element.35) | data formatting | bytes 8388608 | tf_op jit(solution)/shard_map/convert_element_type | solution.py:127
  84.7 6.4 %reshape.266 = f32[4096,256]{0,1:T(8,128)} reshape(f32[16,2,128,256]{2,1,0,3:T(2,128)} %copy.61) | data formatting | bytes 8388608 | tf_op jit(solution)/shard_map/convert_element_type | solution.py:127
  92.1 4.7 %fusion.56 = (f32[256]{0:T(256)S(1)}, f32[256,384]{1,0:T(8,128)S(1)}) fusion(bf16[5120,256]{1,0:T(8,128)(2,1)} %bitcast.215, bf16[5120,384]{1,0:T(8,128)(2,1)} %param.11), kind=kOutput, calls=%fused_computation.168 | convolution fusion | flops 1006731008 | bytes 6947840 | tf_op jit(solution)/shard_map/dot_general | solution.py:137
  102.2 9.4 %all_to_all.31 = f32[16,8,256]{2,1,0:T(8,128)S(1)} all-to-all(f32[16,8,256]{2,1,0:T(8,128)S(1)} %broadcast_in_dim.246), channel_id=1, replica_groups=mesh['grp'=16,'voc'=16] {'voc'}, dimensions={0} | all-to-all | bytes 262144 | tf_op jit(solution)/shard_map/all_to_all | solution.py:68
  113.8 5.5 %all-to-all-start.3 = ((f32[16,8,256]{2,1,0:T(8,128)}), f32[16,8,256]{2,1,0:T(8,128)}, u32[]{:S(2)}, u32[]{:S(2)}) async-start(f32[16,8,256]{2,1,0:T(8,128)} %broadcast_in_dim.247), calls=%async_computation.3 | async-start | bytes 262144 | tf_op jit(solution)/shard_map/all_to_all | solution.py:68
  119.3 9.3 %all-to-all-done.3 = f32[16,8,256]{2,1,0:T(8,128)} async-done(((f32[16,8,256]{2,1,0:T(8,128)}), f32[16,8,256]{2,1,0:T(8,128)}, u32[]{:S(2)}, u32[]{:S(2)}) %all-to-all-start.3) | async-done | bytes 131104 | tf_op jit(solution)/shard_map/all_to_all | solution.py:68
  133.0 3.7 %multiply_reduce_fusion = (f32[4096]{0:T(1024)S(1)}, bf16[4096,256]{0,1:T(8,128)(2,1)S(1)}) fusion(f32[4096,256]{0,1:T(8,128)} %reshape.266, f32[256]{0:T(256)} %copy-done.7, pred[256]{0:T(512)(128)(4,1)} %copy-done.22, bf16[4096,384]{1,0:T(8,128)(2,1)S(1)} %copy-done, f32[256,384]{1,0:T(8,128)S(1)} %get-tuple-element.75, f32[256,384]{1,0:T(8,128)} %copy-done.4, ...), kind=kOutput, calls=%fused_computation.3 | convolution fusion | flops 811233280 | bytes 10245376 | tf_op jit(solution)/shard_map/dot_general | solution.py:168
  138.4 4.4 %reshape.264 = bf16[16,2,128,256]{2,1,0,3:T(2,128)(2,1)} reshape(bf16[4096,256]{0,1:T(8,128)(2,1)} %select_convert_fusion) | data formatting | bytes 4194304 | tf_op jit(solution)/shard_map/reshape | solution.py:176
  142.8 8.6 %constant_dynamic-slice_fusion = (bf16[16,1,128,256]{2,1,0,3:T(2,128)(2,1)}, bf16[16,1,128,256]{2,1,0,3:T(2,128)(2,1)}) fusion(bf16[16,2,128,256]{2,1,0,3:T(2,128)(2,1)} %reshape.264, s32[]{:T(128)S(6)} %select_n.148, s32[]{:T(128)S(6)} %select_n.149), kind=kLoop, calls=%fused_computation.154 | loop fusion | bytes 4194312 | tf_op jit(solution)/shard_map/jit(dynamic_index_in_dim)/dynamic_slice | solution.py:178
  151.4 5.8 %copy.91 = bf16[16,1,128,256]{3,2,0,1:T(8,128)(2,1)} copy(bf16[16,1,128,256]{2,1,0,3:T(2,128)(2,1)} %get-tuple-element.39) | data formatting | bytes 2097152
  158.5 5.8 %copy.90 = bf16[16,1,128,256]{3,2,0,1:T(8,128)(2,1)} copy(bf16[16,1,128,256]{2,1,0,3:T(2,128)(2,1)} %get-tuple-element.38) | data formatting | bytes 2097152
  164.3 1.9 convert_add_fusion
  167.5 2.5 %select_convert_fusion.1 = bf16[16,128,256]{2,1,0:T(8,128)(2,1)} fusion(bf16[16,128]{1,0:T(8,128)(2,1)S(1)} %get-tuple-element.5, bf16[16,128]{1,0:T(8,128)(2,1)S(1)} %get-tuple-element.4, pred[256]{0:T(512)(128)(4,1)S(1)} %copy-done.16, pred[256]{0:T(512)(128)(4,1)S(1)} %copy-done.20, bf16[16,128,256]{2,1,0:T(8,128)(2,1)} %collective-permute-done.1, ...), kind=kLoop, calls=%fused_computation.13 | loop fusion | flops 2621440 | bytes 3154432 | tf_op jit(solution)/shard_map/convert_element_type | solution.py:76
  170.0 4.5 %all-to-all-start.4 = ((bf16[16,128,256]{2,1,0:T(8,128)(2,1)}), bf16[16,128,256]{2,1,0:T(8,128)(2,1)}, u32[]{:S(2)}, u32[]{:S(2)}) async-start(bf16[16,128,256]{2,1,0:T(8,128)(2,1)} %select_convert_fusion.1), calls=%async_computation.4 | async-start | bytes 2097152 | tf_op jit(solution)/shard_map/all_to_all | solution.py:184
  178.0 13.0 %all-to-all-done.4 = bf16[16,128,256]{2,1,0:T(8,128)(2,1)} async-done(((bf16[16,128,256]{2,1,0:T(8,128)(2,1)}), bf16[16,128,256]{2,1,0:T(8,128)(2,1)}, u32[]{:S(2)}, u32[]{:S(2)}) %all-to-all-start.4) | async-done | bytes 1048608 | tf_op jit(solution)/shard_map/all_to_all | solution.py:184
  194.5 6.1 %all-to-all-start.5 = ((bf16[16,32,128]{2,1,0:T(8,128)(2,1)}), bf16[16,32,128]{2,1,0:T(8,128)(2,1)}, u32[]{:S(2)}, u32[]{:S(2)}) async-start(bf16[16,32,128]{2,1,0:T(8,128)(2,1)} %bitcast.217), calls=%async_computation.5 | async-start | bytes 262144 | tf_op jit(solution)/shard_map/all_to_all | solution.py:204
  200.6 4.8 %convolution_convert_fusion = bf16[4096,384]{1,0:T(8,128)(2,1)} fusion(bf16[4096,256]{0,1:T(8,128)(2,1)} %copy-done.2, f32[256,384]{1,0:T(8,128)S(1)} %get-tuple-element.75, f32[256,384]{1,0:T(8,128)} %copy-done.4, f32[256]{0:T(256)} %copy-done.12, f32[256]{0:T(256)} %copy-done.11, f32[256]{0:T(256)S(1)} %get-tuple-element.74, f32[256]{0:T(256)} %copy-done.6), kind=kOutput, calls=%fused_computation | convolution fusion | flops 807567360 | bytes 6033408 | tf_op jit(solution)/shard_map/dot_general | solution.py:180
  205.4 4.4 %all-to-all-done.5 = bf16[16,32,128]{2,1,0:T(8,128)(2,1)} async-done(((bf16[16,32,128]{2,1,0:T(8,128)(2,1)}), bf16[16,32,128]{2,1,0:T(8,128)(2,1)}, u32[]{:S(2)}, u32[]{:S(2)}) %all-to-all-start.5) | async-done | bytes 131104 | tf_op jit(solution)/shard_map/all_to_all | solution.py:204
  (109 shorter events, 36.4 us)
Async XLA Ops:
  0.6 97.0 %copy-start = (bf16[4096,384]{1,0:T(8,128)(2,1)S(1)}, bf16[4096,384]{1,0:T(8,128)(2,1)}, u32[]{:S(2)}) copy-start(bf16[4096,384]{1,0:T(8,128)(2,1)} %param.10) | copy-start | bytes 9437188
  3.1 22.3 %all-to-all-start = ((bf16[16,24,288]{2,1,0:T(8,128)(2,1)}), bf16[16,24,288]{2,1,0:T(8,128)(2,1)S(1)}, u32[]{:S(2)}, u32[]{:S(2)}) async-start(bf16[16,24,288]{2,1,0:T(8,128)(2,1)} %bitcast.2), calls=%async_computation | async-start | bytes 589824 | tf_op jit(solution)/shard_map/all_to_all | solution.py:103
  13.1 51.6 %copy-start.14 = (pred[256]{0:T(512)(128)(4,1)}, pred[256]{0:T(512)(128)(4,1)S(1)}, u32[]{:S(2)}) copy-start(pred[256]{0:T(512)(128)(4,1)S(1)} %get-tuple-element.82) | copy-start | bytes 772
  14.7 50.0 %copy-start.18 = (pred[256]{0:T(512)(128)(4,1)}, pred[256]{0:T(512)(128)(4,1)S(1)}, u32[]{:S(2)}) copy-start(pred[256]{0:T(512)(128)(4,1)S(1)} %iota_compare_fusion.11) | copy-start | bytes 772
  16.7 48.0 %copy-start.21 = (s32[256]{0:T(256)}, s32[256]{0:T(256)S(1)}, u32[]{:S(2)}) copy-start(s32[256]{0:T(256)S(1)} %get-tuple-element.66) | copy-start | bytes 3076
  64.7 5.5 %collective-permute-start = (bf16[16,288,256]{2,1,0:T(8,128)(2,1)}, bf16[16,288,256]{2,1,0:T(8,128)(2,1)}, u32[]{:S(2)}, u32[]{:S(2)}) collective-permute-start(bf16[16,288,256]{2,1,0:T(8,128)(2,1)} %all_to_all.30), channel_id=1, source_target_pairs={{0,16},{16,0},{32,48},{48,32},{64,80},{80,64},{96,112},{112,96},{1... | collective-permute-start | bytes 7077896 | tf_op jit(solution)/shard_map/ppermute | solution.py:123
  65.7 31.1 %copy-start.22 = (pred[256]{0:T(512)(128)(4,1)}, pred[256]{0:T(512)(128)(4,1)S(1)}, u32[]{:S(2)}) copy-start(pred[256]{0:T(512)(128)(4,1)S(1)} %iota_compare_fusion.12) | copy-start | bytes 772
  75.6 16.5 %copy-start.13 = (f32[256]{0:T(256)}, f32[256]{0:T(256)S(1)}, u32[]{:S(2)}) copy-start(f32[256]{0:T(256)S(1)} %get-tuple-element.34) | copy-start | bytes 3076
  92.1 4.7 %copy-start.7 = (f32[256]{0:T(256)}, f32[256]{0:T(256)S(1)}, u32[]{:S(2)}) copy-start(f32[256]{0:T(256)S(1)} %add_rsqrt_fusion) | copy-start | bytes 3076
  92.1 4.7 %copy-start.1 = (f32[4096,256]{0,1:T(8,128)S(1)}, f32[4096,256]{0,1:T(8,128)}, u32[]{:S(2)}) copy-start(f32[4096,256]{0,1:T(8,128)} %reshape.266) | copy-start | bytes 12582916
  99.0 37.6 %copy-start.6 = (f32[256]{0:T(256)}, f32[256]{0:T(256)S(1)}, u32[]{:S(2)}) copy-start(f32[256]{0:T(256)S(1)} %get-tuple-element.72) | copy-start | bytes 3076
  113.8 14.8 %all-to-all-start.3 = ((f32[16,8,256]{2,1,0:T(8,128)}), f32[16,8,256]{2,1,0:T(8,128)}, u32[]{:S(2)}, u32[]{:S(2)}) async-start(f32[16,8,256]{2,1,0:T(8,128)} %broadcast_in_dim.247), calls=%async_computation.3 | async-start | bytes 262144 | tf_op jit(solution)/shard_map/all_to_all | solution.py:68
  133.0 3.7 %copy-start.11 = (f32[256]{0:T(256)}, f32[256]{0:T(256)S(1)}, u32[]{:S(2)}) copy-start(f32[256]{0:T(256)S(1)} %get-tuple-element.62) | copy-start | bytes 3076
  133.0 3.7 %copy-start.12 = (f32[256]{0:T(256)}, f32[256]{0:T(256)S(1)}, u32[]{:S(2)}) copy-start(f32[256]{0:T(256)S(1)} %get-tuple-element.63) | copy-start | bytes 3076
  133.0 3.7 %copy-start.15 = (pred[256]{0:T(512)(128)(4,1)S(1)}, pred[256]{0:T(512)(128)(4,1)}, u32[]{:S(2)}) copy-start(pred[256]{0:T(512)(128)(4,1)} %copy-done.14) | copy-start | bytes 772
  133.0 3.7 %copy-start.19 = (pred[256]{0:T(512)(128)(4,1)S(1)}, pred[256]{0:T(512)(128)(4,1)}, u32[]{:S(2)}) copy-start(pred[256]{0:T(512)(128)(4,1)} %copy-done.18) | copy-start | bytes 772
  157.2 7.2 %collective-permute-start.1 = (bf16[16,128,256]{2,1,0:T(8,128)(2,1)}, bf16[16,128,256]{2,1,0:T(8,128)(2,1)}, u32[]{:S(2)}, u32[]{:S(2)}) collective-permute-start(bf16[16,128,256]{2,1,0:T(8,128)(2,1)} %bitcast.216), channel_id=1, source_target_pairs={{0,16},{16,0},{32,48},{48,32},{64,80},{80,64},{96,112},{112,96},{1... | collective-permute-start | bytes 3145736 | tf_op jit(solution)/shard_map/ppermute | solution.py:179
  164.3 3.1 %copy-start.16 = (pred[256]{0:T(512)(128)(4,1)S(1)}, pred[256]{0:T(512)(128)(4,1)}, u32[]{:S(2)}) copy-start(pred[256]{0:T(512)(128)(4,1)} %copy-done.14) | copy-start | bytes 772
  164.3 3.1 %copy-start.20 = (pred[256]{0:T(512)(128)(4,1)S(1)}, pred[256]{0:T(512)(128)(4,1)}, u32[]{:S(2)}) copy-start(pred[256]{0:T(512)(128)(4,1)} %copy-done.18) | copy-start | bytes 772
  167.5 9.3 %copy-start.8 = (f32[256]{0:T(256)S(1)}, f32[256]{0:T(256)}, u32[]{:S(2)}) copy-start(f32[256]{0:T(256)} %copy-done.7) | copy-start | bytes 3076
  170.0 22.6 %copy-start.17 = (pred[256]{0:T(512)(128)(4,1)S(1)}, pred[256]{0:T(512)(128)(4,1)}, u32[]{:S(2)}) copy-start(pred[256]{0:T(512)(128)(4,1)} %copy-done.14) | copy-start | bytes 772
  170.0 21.0 %all-to-all-start.4 = ((bf16[16,128,256]{2,1,0:T(8,128)(2,1)}), bf16[16,128,256]{2,1,0:T(8,128)(2,1)}, u32[]{:S(2)}, u32[]{:S(2)}) async-start(bf16[16,128,256]{2,1,0:T(8,128)(2,1)} %select_convert_fusion.1), calls=%async_computation.4 | async-start | bytes 2097152 | tf_op jit(solution)/shard_map/all_to_all | solution.py:184
  194.5 15.4 %all-to-all-start.5 = ((bf16[16,32,128]{2,1,0:T(8,128)(2,1)}), bf16[16,32,128]{2,1,0:T(8,128)(2,1)}, u32[]{:S(2)}, u32[]{:S(2)}) async-start(bf16[16,32,128]{2,1,0:T(8,128)(2,1)} %bitcast.217), calls=%async_computation.5 | async-start | bytes 262144 | tf_op jit(solution)/shard_map/all_to_all | solution.py:204
  200.6 10.8 %copy-start.5 = (bf16[24,256]{1,0:T(8,128)(2,1)S(1)}, bf16[24,256]{1,0:T(8,128)(2,1)}, u32[]{:S(2)}) copy-start(bf16[24,256]{1,0:T(8,128)(2,1)} %param.7) | copy-start | bytes 36868
  (5 other events, 6.6 us)

commit v2 on v0

v2 whole, which is shorter than its diff:
```python
import jax
import jax.numpy as jnp
from jax import lax
from jax.experimental import pallas as pl
from jax.experimental.pallas import tpu as pltpu
from jax.sharding import PartitionSpec as P

DS = 4096
SEQ = 2
VALID = 240
LANES = 256
EPSILON = 1e-06
GROUPS = 16
VOC = 16
ROWS = 24
HALF_S = 128
HALF_T = 160
HALF = HALF_S + HALF_T
VOC_DEV = 384
STATS = 8
SEND = 32
CHUNKS = 4
PER = VOC // CHUNKS
BF = jnp.bfloat16
F32 = jnp.float32
CORE_SWAP = [(i, i ^ 1) for i in range(GROUPS)]
TN = (((0,), (0,)), ((), ()))
NT = (((1,), (1,)), ((), ()))
NN = (((1,), (0,)), ((), ()))


def rounded(x):
    return lax.reduce_precision(x, 8, 7)


def dot(a, b, dims):
    return lax.dot_general(a, b, dims, preferred_element_type=F32)


def lane_tables(episode_source, lengths):
    episodes = lengths.shape[0]
    two = (lengths == 2).astype(jnp.int32)
    before = jnp.arange(episodes)[None, :] < jnp.arange(episodes)[:, None]
    rank = jnp.sum(jnp.where(before, two[None, :], 0), axis=1)
    lane = jnp.arange(LANES, dtype=jnp.int32)
    number = jnp.arange(episodes, dtype=jnp.int32)
    first = lane[None, :] == number[:, None]
    second = (two[:, None] == 1) & (lane[None, :] == episodes + rank[:, None])
    pick = first | second
    position = (lane >= episodes).astype(jnp.int32)
    inside = lane < VALID
    episode = jnp.sum(jnp.where(pick, number[:, None], 0), axis=0)
    source = jnp.sum(jnp.where(pick, episode_source[:, None], 0), axis=0)
    length = jnp.sum(jnp.where(pick, lengths[:, None], 0), axis=0)
    student_row = jnp.where(inside, episode * SEQ + position, -1)
    teacher_row = jnp.where(inside, source * SEQ + position, -1)
    weight = jnp.where(inside, 1.0 / jnp.maximum(length, 1).astype(F32), 0.0)
    return student_row[None], teacher_row[None], weight[None]


def own_core():
    return lax.rem(lax.axis_index("grp"), 2)


def lane_iota(shape):
    return lax.broadcasted_iota(jnp.int32, shape, len(shape) - 1)


def pack_kernel(student, teacher, out):
    for c in range(2):
        half = jnp.concatenate(
            [
                student[:, c * HALF_S : (c + 1) * HALF_S],
                teacher[:, c * HALF_T : (c + 1) * HALF_T],
            ],
            axis=1,
        )
        for z in range(GROUPS // 2):
            out[2 * z + c] = half


def compact_kernel(held, student_row, teacher_row, gain, out):
    rows = jnp.concatenate([held[g].astype(F32) for g in range(GROUPS)], axis=0).astype(BF)
    ids = lax.broadcasted_iota(jnp.int32, (GROUPS * ROWS, LANES), 0)
    pick_s = jnp.where(ids == student_row[...], 1.0, 0.0).astype(BF)
    pick_t = jnp.where(ids == teacher_row[...], 1.0, 0.0).astype(BF)
    part = lax.broadcasted_iota(jnp.int32, (16, LANES), 0)
    place = jnp.where(lane_iota((16, LANES)) == part + VALID, 1.0, 0.0).astype(BF)
    block_s = dot(rows[:, :HALF_S], pick_s, TN) + dot(gain[...].astype(BF), place, TN)
    block_t = dot(rows[:, HALF_S:], pick_t, TN)
    block_s = block_s.astype(BF)
    block_t = block_t.astype(BF)
    for v in range(VOC):
        out[v, :HALF_S, :] = block_s
        out[v, HALF_S:, :] = block_t


def stack_rows(values):
    row = lax.broadcasted_iota(jnp.int32, (STATS, LANES), 0)
    out = jnp.zeros((STATS, LANES), F32)
    for k, value in enumerate(values):
        out = jnp.where(row == k, value, out)
    return out


def combined(stats):
    top_s, sum_s, top_t, sum_t, mean_d, mean_u, mean_du = [
        stats[:, k, :] for k in range(7)
    ]
    all_s = jnp.max(top_s, axis=0, keepdims=True)
    all_t = jnp.max(top_t, axis=0, keepdims=True)
    shift_s = top_s - all_s
    shift_t = top_t - all_t
    scale_s = jnp.exp(shift_s)
    scale_t = jnp.exp(shift_t)
    shift_d = shift_s - shift_t

    def total(x):
        return jnp.sum(x, axis=0, keepdims=True)

    return (
        all_s,
        total(scale_s * sum_s),
        all_t,
        total(scale_t * sum_t),
        total(scale_s * (mean_d + shift_d * sum_s)),
        total(scale_s * (mean_u + shift_s * sum_s)),
        total(
            scale_s
            * (mean_du + shift_s * mean_d + shift_d * mean_u + shift_s * shift_d * sum_s)
        ),
    )


def forward_kernel(
    mine, other, student_head, teacher_head,
    normed, exp_out, ratio_out, stats_out, inverse_out,
    rows_s, rows_t, head_s, head_t, row_sems, head_sems,
):
    core = own_core()
    copies = []
    for k, (block, place) in enumerate(((mine, core), (other, 1 - core))):
        copies.append(
            pltpu.make_async_copy(
                block.at[:, pl.ds(0, HALF_S), :], rows_s.at[:, place], row_sems.at[2 * k]
            )
        )
        copies.append(
            pltpu.make_async_copy(
                block.at[:, pl.ds(HALF_S, HALF_T), :], rows_t.at[:, place], row_sems.at[2 * k + 1]
            )
        )
    for copy in copies:
        copy.start()
    heads = []
    for j in range(CHUNKS):
        span_s = pl.ds(j * (DS // CHUNKS), DS // CHUNKS)
        span_t = pl.ds(j * (VOC * 2 * HALF_T // CHUNKS), VOC * 2 * HALF_T // CHUNKS)
        heads.append(
            (
                pltpu.make_async_copy(
                    student_head.at[span_s], head_s.at[span_s], head_sems.at[0, j]
                ),
                pltpu.make_async_copy(
                    teacher_head.at[span_t], head_t.at[span_t], head_sems.at[1, j]
                ),
            )
        )
    for copy_s, _ in heads:
        copy_s.start()
    for _, copy_t in heads:
        copy_t.start()
    for copy in copies:
        copy.wait()

    squares = jnp.zeros((1, LANES), F32)
    for v in range(VOC):
        part = rows_s[v].reshape(2 * HALF_S, LANES).astype(F32)
        squares = squares + jnp.sum(part * part, axis=0, keepdims=True)
    inverse = lax.rsqrt(squares / DS + EPSILON)
    inverse_out[...] = inverse
    kept = jnp.where(lane_iota((1, LANES)) < VALID, inverse, 0.0)
    for v in range(VOC):
        part = rows_s[v].reshape(2 * HALF_S, LANES).astype(F32)
        gain = (
            part[:, VALID : VALID + 1]
            + part[:, VALID + 1 : VALID + 2]
            + part[:, VALID + 2 : VALID + 3]
        )
        normed[pl.ds(v * 2 * HALF_S, 2 * HALF_S), :] = (part * kept * gain).astype(BF)

    student = jnp.zeros((VOC_DEV, LANES), F32)
    for j in range(CHUNKS):
        span = pl.ds(j * (DS // CHUNKS), DS // CHUNKS)
        heads[j][0].wait()
        student = student + dot(head_s[span, :], normed[span, :], TN)
    teacher = jnp.zeros((VOC_DEV, LANES), F32)
    for j in range(CHUNKS):
        size = VOC * 2 * HALF_T // CHUNKS
        heads[j][1].wait()
        rows = rows_t[pl.ds(j * PER, PER)].reshape(size, LANES)
        teacher = teacher + dot(head_t[pl.ds(j * size, size), :], rows, TN)

    top_s = jnp.max(student, axis=0, keepdims=True)
    top_t = jnp.max(teacher, axis=0, keepdims=True)
    below = student - top_s
    exp_s = jnp.exp(below)
    below_t = teacher - top_t
    ratio = below - below_t
    exp_out[...] = exp_s
    ratio_out[...] = ratio

    def total(x):
        return jnp.sum(x, axis=0, keepdims=True)

    weighted = exp_s * ratio
    stats = stack_rows(
        [
            top_s,
            total(exp_s),
            top_t,
            total(jnp.exp(below_t)),
            total(weighted),
            total(exp_s * below),
            total(weighted * below),
        ]
    )
    for v in range(VOC):
        stats_out[v] = stats


def combine_kernel(stats, out):
    tile = stack_rows(combined(stats))
    for g in range(GROUPS):
        out[g] = tile


def with_gain(total):
    lane = lane_iota(total.shape)
    gain = total[:, VALID : VALID + 1] + total[:, VALID + 1 : VALID + 2]
    return place_gain(total, gain, lane)


def place_gain(total, gain, lane):
    high = gain.astype(BF).astype(F32)
    low = gain - high
    return jnp.where(lane == VALID, high, jnp.where(lane == VALID + 1, low, total)).astype(BF)


def backward_kernel(
    stats, local_stats, exp_in, ratio_in, weight, inverse, student_head, normed,
    grad_out, stay, away, pull_out, loss_out,
    head_s, rows, sems,
):
    core = own_core()
    size = DS // CHUNKS
    copies = []
    for j in range(CHUNKS):
        span = pl.ds(j * size, size)
        copies.append(
            (
                pltpu.make_async_copy(student_head.at[span], head_s.at[span], sems.at[0, j]),
                pltpu.make_async_copy(normed.at[span], rows.at[span], sems.at[1, j]),
            )
        )
    for pair in copies:
        pair[0].start()
        pair[1].start()
    all_s, total_s, all_t, total_t, sum_d, sum_u, sum_du = combined(stats)
    mean_d = sum_d / total_s
    mean_u = sum_u / total_s
    covariance = sum_du / total_s - mean_d * mean_u
    divergence = mean_d - jnp.log(total_s) + jnp.log(total_t)
    loss_out[...] = jnp.sum(weight[...] * divergence, axis=1, keepdims=True)
    pull_out[...] = weight[...] * covariance * inverse[...] * inverse[...] / DS
    shift_s = local_stats[0:1, :] - all_s
    shift_t = local_stats[2:3, :] - all_t
    factor = weight[...] * jnp.exp(shift_s) / total_s
    offset = shift_s - shift_t - mean_d
    grad = (factor * exp_in[...] * (ratio_in[...] + offset)).astype(BF)
    grad_out[...] = grad
    lane = lane_iota((2 * HALF_S, LANES))
    for j in range(CHUNKS):
        copies[j][0].wait()
        copies[j][1].wait()
        for i in range(PER):
            v = j * PER + i
            span = pl.ds(v * 2 * HALF_S, 2 * HALF_S)
            term = dot(head_s[span, :], grad, NN)
            gain = jnp.sum(term * rows[span, :].astype(F32), axis=1, keepdims=True)
            term = place_gain(term, gain, lane)
            first, second = term[:HALF_S], term[HALF_S:]
            stay[v] = jnp.where(core == 0, first, second)
            away[v] = jnp.where(core == 0, second, first)


def pair_kernel(stay, arrived, out):
    for v in range(VOC):
        out[v] = with_gain(stay[v].astype(F32) + arrived[v].astype(F32))


def send_kernel(pieces, student_row, out):
    total = pieces[0].astype(F32)
    for v in range(1, VOC):
        total = total + pieces[v].astype(F32)
    total = with_gain(total)
    slot = lax.broadcasted_iota(jnp.int32, (SEND, LANES), 0)
    extra = (slot >= ROWS) & (slot < ROWS + 2) & (lane_iota((SEND, LANES)) == slot - ROWS + VALID)
    for g in range(GROUPS):
        pick = ((slot < ROWS) & (student_row[...] == slot + g * ROWS)) | extra
        out[g] = dot(jnp.where(pick, 1.0, 0.0).astype(BF), total, NT).astype(BF)


def finish_kernel(pieces, hidden, gain, student_row, inverse, pull, grad_hidden, grad_gain):
    halves = []
    for c in range(2):
        total = pieces[c].astype(F32)
        for z in range(1, GROUPS // 2):
            total = total + pieces[2 * z + c].astype(F32)
        halves.append(total)
    total = jnp.concatenate(halves, axis=1)
    grad_gain[...] = (total[ROWS : ROWS + 1] + total[ROWS + 1 : ROWS + 2]) / gain[...]
    first = lax.axis_index("grp") * ROWS
    own = lax.broadcasted_iota(jnp.int32, (ROWS, LANES), 0) + first == student_row[...]
    own_rms = jnp.sum(jnp.where(own, inverse[...], 0.0), axis=1, keepdims=True)
    own_pull = jnp.sum(jnp.where(own, pull[...], 0.0), axis=1, keepdims=True)
    normed_grad = total[:ROWS]
    result = own_rms * (normed_grad * gain[...]) - hidden[...].astype(F32) * own_pull
    grad_hidden[...] = result.astype(BF)


def shape(dims, dtype):
    return jax.ShapeDtypeStruct(dims, dtype)


def params(mib):
    return pltpu.CompilerParams(vmem_limit_bytes=mib * 1024 * 1024)


def exchange(x, axis):
    return lax.all_to_all(x, axis, 0, 0, tiled=True)


ANY = pl.BlockSpec(memory_space=pl.ANY)
VMEM = pl.BlockSpec(memory_space=pltpu.VMEM)


def local(
    student_hidden, norm_gain, teacher_hidden, student_head, teacher_head, episode_source, lengths
):
    core = own_core()
    width_t = VOC * 2 * HALF_T
    row = shape((1, LANES), F32)
    student_row, teacher_row, weight = lane_tables(episode_source, lengths)

    packed = pl.pallas_call(
        pack_kernel, out_shape=shape((GROUPS, ROWS, HALF), BF), compiler_params=params(16)
    )(student_hidden, teacher_hidden)
    held = exchange(packed, "grp")

    gain_half = lax.dynamic_slice_in_dim(norm_gain, core * HALF_S, HALF_S)
    gain_high = rounded(gain_half)
    gain_mid = rounded(gain_half - gain_high)
    gain_low = gain_half - gain_high - gain_mid
    gain_parts = jnp.concatenate(
        [jnp.stack([gain_high, gain_mid, gain_low]), jnp.zeros((13, HALF_S), F32)], axis=0
    )
    block = pl.pallas_call(
        compact_kernel, out_shape=shape((VOC, HALF, LANES), BF), compiler_params=params(16)
    )(held, student_row, teacher_row, gain_parts)
    mine = exchange(block, "voc")
    other = lax.ppermute(mine, "grp", CORE_SWAP)

    normed, exp_s, ratio, stats, inverse = pl.pallas_call(
        forward_kernel,
        out_shape=(
            shape((DS, LANES), BF),
            shape((VOC_DEV, LANES), F32),
            shape((VOC_DEV, LANES), F32),
            shape((VOC, STATS, LANES), F32),
            row,
        ),
        in_specs=[ANY] * 4,
        scratch_shapes=[
            pltpu.VMEM((VOC, 2, HALF_S, LANES), BF),
            pltpu.VMEM((VOC, 2, HALF_T, LANES), BF),
            pltpu.VMEM((DS, VOC_DEV), BF),
            pltpu.VMEM((width_t, VOC_DEV), BF),
            pltpu.SemaphoreType.DMA((4,)),
            pltpu.SemaphoreType.DMA((2, CHUNKS)),
        ],
        compiler_params=params(32),
    )(mine, other, student_head, teacher_head)

    from_voc = exchange(stats, "voc")
    spread = pl.pallas_call(
        combine_kernel, out_shape=shape((GROUPS, STATS, LANES), F32), compiler_params=params(16)
    )(from_voc)
    from_grp = exchange(spread, "grp")

    grad, stay, away, pull, loss = pl.pallas_call(
        backward_kernel,
        out_shape=(
            shape((VOC_DEV, LANES), BF),
            shape((VOC, HALF_S, LANES), BF),
            shape((VOC, HALF_S, LANES), BF),
            row,
            shape((1, 1), F32),
        ),
        in_specs=[VMEM] * 6 + [ANY] * 2,
        scratch_shapes=[
            pltpu.VMEM((DS, VOC_DEV), BF),
            pltpu.VMEM((DS, LANES), BF),
            pltpu.SemaphoreType.DMA((2, CHUNKS)),
        ],
        compiler_params=params(32),
    )(from_grp, stats[0], exp_s, ratio, weight, inverse, student_head, normed)

    arrived = lax.ppermute(away, "grp", CORE_SWAP)
    grad_head = dot(normed, grad, NT).astype(BF)
    pair = pl.pallas_call(
        pair_kernel, out_shape=shape((VOC, HALF_S, LANES), BF), compiler_params=params(16)
    )(stay, arrived)
    pieces = exchange(pair, "voc")
    outgoing = pl.pallas_call(
        send_kernel, out_shape=shape((GROUPS, SEND, HALF_S), BF), compiler_params=params(16)
    )(pieces, student_row)
    pieces = exchange(outgoing, "grp")
    grad_hidden, grad_gain = pl.pallas_call(
        finish_kernel, out_shape=(shape((ROWS, 2 * HALF_S), BF), row), compiler_params=params(16)
    )(pieces, student_hidden, norm_gain[None], student_row, inverse, pull)
    return (loss.reshape(()), grad_hidden, grad_gain.reshape(-1), grad_head)


def solution(mesh):
    placed = (
        P("grp", "voc"),
        P("voc"),
        P("grp", "voc"),
        P(None, ("grp", "voc")),
        P(None, ("grp", "voc")),
        P(),
        P(),
    )
    return jax.shard_map(
        local,
        mesh=mesh,
        in_specs=placed,
        out_specs=(P(), P("grp", "voc"), P("voc"), P(None, ("grp", "voc"))),
        check_vma=False,
    )
```

time: 606 us -> 149 us (0.25)
  blocking collectives: 362 us -> 58 us
  waiting for transfers between devices: 169 us -> 38.1 us
  Pallas kernels: 0 us -> 17.4 us
  matrix products: 20.1 us -> 2.95 us
  between operations: 13.9 us -> 0.78 us
  other arithmetic: 13 us -> 2.53 us
    psum x5 -> x0, blocking collectives: 248 us -> none  [the longest x1 73.9 us: local(): lax.psum(jnp.sum(prob_student * log_ratio, axis=1), ('grp', 'voc'))]
    reduce_scatter x2 -> x0, waiting for transfers between devices: 125 us -> none  [the longest x1 75.2 us: local(): lax.psum_scatter(full_term.astype(jnp.bfloat16), 'voc', scatter_dimension...]
    pmax x1 -> x0, blocking collectives: 76.1 us -> none  [local(): lax.pmax((jnp.max(student_logits, axis=1), jnp.max(teacher_logits, axis=1...]
    all_to_all x0 -> x2, blocking collectives: none -> 58 us  [exchange(): return lax.all_to_all(x, axis, 0, 0, tiled=True)]
    all_gather x2 -> x0, blocking collectives: 38.2 us -> none  [the longest x1 20.8 us: local(): lax.all_gather(aligned, 'voc', axis=1, tiled=True)]
    all_gather x2 -> x0, waiting for transfers between devices: 36.1 us -> none  [the longest x1 36.1 us: local(): lax.all_gather(teacher_rows, 'grp', axis=0, tiled=True)]
    all_to_all x1 -> x4, waiting for transfers between devices: 7.38 us -> 31.3 us  [exchange(): return lax.all_to_all(x, axis, 0, 0, tiled=True)]
    pallas_call x0 -> x8, Pallas kernels: none -> 17.4 us  [the longest x1 8.93 us: local(): pl.pallas_call(forward_kernel, out_shape=(shape((DS, LANES), BF), shape((...]
  transfers between devices with their start and end apart: 5 -> 6, of which waited for: 4 -> 6; matrix products, arithmetic and copies ran while one was open for 3% -> 4% of each run, Pallas kernels for 0% -> 0%
where the time goes in v2:
time: 149 us; the launch traced here: 148 us
  blocking collectives  58 us (39%)
  waiting for transfers between devices  38.1 us (26%)
  starting transfers between devices  24.2 us (16%)
  Pallas kernels  17.4 us (12%)
  local copies, waits for them, and re-layouts  4.11 us (3%)
  matrix products  2.95 us (2%)
  other arithmetic  2.53 us (2%)
    all_to_all x2, blocking collectives, exchange(): return lax.all_to_all(x, axis, 0, 0, tiled=True)  58 us
    all_to_all x4, waiting for transfers between devices, exchange(): return lax.all_to_all(x, axis, 0, 0, tiled=True)  31.3 us
    all_to_all x4, starting transfers between devices, exchange(): return lax.all_to_all(x, axis, 0, 0, tiled=True)  23.2 us
    pallas_call x1, Pallas kernels, local(): pl.pallas_call(forward_kernel, out_shape=(shape((DS, LANES), BF), shape((...  8.93 us
    ppermute x1, waiting for transfers between devices, local(): other = lax.ppermute(mine, 'grp', CORE_SWAP)  4.16 us
    unnamed x14, local copies, waits for them, and re-layouts  3.33 us
  transfers between devices with their start and end apart: 6, of which 6 were waited for; matrix products, arithmetic and copies ran while one was open for 4% of the time, Pallas kernels for 0%

profile of v2, /device:TPU:1, one launch (start us, length us, event | category | flops | bytes accessed | tf_op | source)
XLA Modules:
  0.0 148.1 jit_solution(12982409681460159649)
XLA Ops:
  1.3 0.7 copy-done.5
  2.1 0.8 shard_map.102
  2.9 10.0 %all-to-all-start = ((bf16[16,24,288]{2,1,0:T(8,128)(2,1)}), bf16[16,24,288]{2,1,0:T(8,128)(2,1)S(1)}, u32[]{:S(2)}, u32[]{:S(2)}) async-start(bf16[16,24,288]{2,1,0:T(8,128)(2,1)} %shard_map.102), calls=%async_computation | async-start | bytes 589824 | tf_op jit(solution)/shard_map/all_to_all | solution.py:341
  13.7 0.9 select_reduce_fusion
  14.7 0.8 reduce-precision_bitcast_fusion.1
  15.5 9.7 %all-to-all-done.held = bf16[16,24,288]{2,1,0:T(8,128)(2,1)S(1)} async-done(((bf16[16,24,288]{2,1,0:T(8,128)(2,1)}), bf16[16,24,288]{2,1,0:T(8,128)(2,1)S(1)}, u32[]{:S(2)}, u32[]{:S(2)}) %all-to-all-start) | async-done | bytes 221216 | tf_op jit(solution)/shard_map/all_to_all | solution.py:341
  25.8 38.7 %all_to_all.30.mine = bf16[16,288,256]{2,1,0:T(8,128)(2,1)S(1)} all-to-all(bf16[16,288,256]{2,1,0:T(8,128)(2,1)S(1)} %shard_map.103), channel_id=1, replica_groups=mesh['grp'=16,'voc'=16] {'voc'}, dimensions={0} | all-to-all | bytes 4718592 | tf_op jit(solution)/shard_map/all_to_all | solution.py:341
  64.4 0.9 collective-permute-start
  65.4 4.2 %collective-permute-done.other = bf16[16,288,256]{2,1,0:T(8,128)(2,1)S(1)} collective-permute-done((bf16[16,288,256]{2,1,0:T(8,128)(2,1)S(1)}, bf16[16,288,256]{2,1,0:T(8,128)(2,1)S(1)}, u32[]{:S(2)}, u32[]{:S(2)}) %collective-permute-start) | collective-permute-done | bytes 2359328 | tf_op jit(solution)/shard_map/ppermute | solution.py:372
  69.5 8.9 %shard_map.104 = (bf16[4096,256]{1,0:T(8,128)(2,1)S(1)}, f32[384,256]{1,0:T(8,128)S(1)}, f32[384,256]{1,0:T(8,128)S(1)}, f32[16,8,256]{2,1,0:T(8,128)}, f32[1,256]{1,0:T(1,128)S(1)}) custom-call(bf16[16,288,256]{2,1,0:T(8,128)(2,1)S(1)} %all_to_all.30.mine, bf16[16,288,256]{2,1,0:T(8,128)(2,1)S(1)} %collective-permute-done.other, ...), custom_call_target="tpu_custom_call" | custom-call | tf_op jit(solution)/shard_map/pallas_call | solution.py:374
  78.5 3.5 %all-to-all-start.2 = ((f32[16,8,256]{2,1,0:T(8,128)}), f32[16,8,256]{2,1,0:T(8,128)S(1)}, u32[]{:S(2)}, u32[]{:S(2)}) async-start(f32[16,8,256]{2,1,0:T(8,128)} %get-tuple-element.16), calls=%async_computation.2 | async-start | bytes 262144 | tf_op jit(solution)/shard_map/all_to_all | solution.py:341
  82.0 6.8 %all-to-all-done.2.stats = f32[16,8,256]{2,1,0:T(8,128)S(1)} async-done(((f32[16,8,256]{2,1,0:T(8,128)}), f32[16,8,256]{2,1,0:T(8,128)S(1)}, u32[]{:S(2)}, u32[]{:S(2)}) %all-to-all-start.2) | async-done | bytes 131104 | tf_op jit(solution)/shard_map/all_to_all | solution.py:341
  88.8 0.8 shard_map.105
  89.6 4.8 %all-to-all-start.3 = ((f32[16,8,256]{2,1,0:T(8,128)}), f32[16,8,256]{2,1,0:T(8,128)S(1)}, u32[]{:S(2)}, u32[]{:S(2)}) async-start(f32[16,8,256]{2,1,0:T(8,128)} %shard_map.105), calls=%async_computation.3 | async-start | bytes 262144 | tf_op jit(solution)/shard_map/all_to_all | solution.py:341
  95.1 8.5 %all-to-all-done.3.stats = f32[16,8,256]{2,1,0:T(8,128)S(1)} async-done(((f32[16,8,256]{2,1,0:T(8,128)}), f32[16,8,256]{2,1,0:T(8,128)S(1)}, u32[]{:S(2)}, u32[]{:S(2)}) %all-to-all-start.3) | async-done | bytes 131104 | tf_op jit(solution)/shard_map/all_to_all | solution.py:341
  103.6 1.9 %copy-done.1 = bf16[4096,384]{1,0:T(8,128)(2,1)S(1)} copy-done((bf16[4096,384]{1,0:T(8,128)(2,1)S(1)}, bf16[4096,384]{1,0:T(8,128)(2,1)}, u32[]{:S(2)}) %copy-start.1) | copy-done | bytes 3145752
  105.5 2.8 %shard_map.106 = (bf16[384,256]{1,0:T(8,128)(2,1)S(1)}, bf16[16,128,256]{2,1,0:T(8,128)(2,1)S(1)}, bf16[16,128,256]{2,1,0:T(8,128)(2,1)S(1)}, f32[1,256]{1,0:T(1,128)S(1)}, f32[1,1]{1,0:T(1,128)}) custom-call(f32[16,8,256]{2,1,0:T(8,128)S(1)} %all-to-all-done.3.stats, f32[8,256]{1,0:T(8,128)S(1)} %slice_bitcast_fusion.local_stats, ...), custom_call_target="tpu_custom_call" | custom-call | tf_op jit(solution)/shard_map/pallas_call | solution.py:401
  108.4 2.6 %collective-permute-done.1.arrived = bf16[16,128,256]{2,1,0:T(8,128)(2,1)S(1)} collective-permute-done((bf16[16,128,256]{2,1,0:T(8,128)(2,1)S(1)}, bf16[16,128,256]{2,1,0:T(8,128)(2,1)S(1)}, u32[]{:S(2)}, u32[]{:S(2)}) %collective-permute-start.1) | collective-permute-done | bytes 1048608 | tf_op jit(solution)/shard_map/ppermute | solution.py:419
  111.0 1.6 %shard_map.107 = bf16[16,128,256]{2,1,0:T(8,128)(2,1)S(1)} custom-call(bf16[16,128,256]{2,1,0:T(8,128)(2,1)S(1)} %get-tuple-element.22.stay, bf16[16,128,256]{2,1,0:T(8,128)(2,1)S(1)} %collective-permute-done.1.arrived), custom_call_target="tpu_custom_call" | custom-call | tf_op jit(solution)/shard_map/pallas_call | solution.py:421
  112.6 19.4 %all_to_all.31.pieces = bf16[16,128,256]{2,1,0:T(8,128)(2,1)S(1)} all-to-all(bf16[16,128,256]{2,1,0:T(8,128)(2,1)S(1)} %shard_map.107), channel_id=1, replica_groups=mesh['grp'=16,'voc'=16] {'voc'}, dimensions={0} | all-to-all | bytes 2097152 | tf_op jit(solution)/shard_map/all_to_all | solution.py:341
  132.0 1.4 shard_map.108
  133.3 4.9 %all-to-all-start.5 = ((bf16[16,32,128]{2,1,0:T(8,128)(2,1)}), bf16[16,32,128]{2,1,0:T(8,128)(2,1)S(1)}, u32[]{:S(2)}, u32[]{:S(2)}) async-start(bf16[16,32,128]{2,1,0:T(8,128)(2,1)} %shard_map.108), calls=%async_computation.5 | async-start | bytes 262144 | tf_op jit(solution)/shard_map/all_to_all | solution.py:341
  138.2 2.9 %convolution_convert_fusion = bf16[4096,384]{1,0:T(8,128)(2,1)} fusion(bf16[4096,256]{1,0:T(8,128)(2,1)S(1)} %get-tuple-element.20.normed, bf16[384,256]{1,0:T(8,128)(2,1)S(1)} %get-tuple-element.27), kind=kOutput, calls=%fused_computation | convolution fusion | flops 806879232 | bytes 5439488 | tf_op jit(solution)/shard_map/dot_general | solution.py:37
  141.2 6.2 %all-to-all-done.5.pieces = bf16[16,32,128]{2,1,0:T(8,128)(2,1)S(1)} async-done(((bf16[16,32,128]{2,1,0:T(8,128)(2,1)}), bf16[16,32,128]{2,1,0:T(8,128)(2,1)S(1)}, u32[]{:S(2)}, u32[]{:S(2)}) %all-to-all-start.5) | async-done | bytes 131104 | tf_op jit(solution)/shard_map/all_to_all | solution.py:341
  (27 shorter events, 3.7 us)
Async XLA Ops:
  0.6 0.7 copy-start.3
  1.3 0.7 copy-start.5
  2.9 22.3 %all-to-all-start = ((bf16[16,24,288]{2,1,0:T(8,128)(2,1)}), bf16[16,24,288]{2,1,0:T(8,128)(2,1)S(1)}, u32[]{:S(2)}, u32[]{:S(2)}) async-start(bf16[16,24,288]{2,1,0:T(8,128)(2,1)} %shard_map.102), calls=%async_computation | async-start | bytes 589824 | tf_op jit(solution)/shard_map/all_to_all | solution.py:341
  25.2 44.3 %copy-start.2 = (bf16[5120,384]{1,0:T(8,128)(2,1)S(1)}, bf16[5120,384]{1,0:T(8,128)(2,1)}, u32[]{:S(2)}) copy-start(bf16[5120,384]{1,0:T(8,128)(2,1)} %teacher_head.1) | copy-start | bytes 11796484
  25.7 43.8 %copy-start = (bf16[4096,384]{1,0:T(8,128)(2,1)S(1)}, bf16[4096,384]{1,0:T(8,128)(2,1)}, u32[]{:S(2)}) copy-start(bf16[4096,384]{1,0:T(8,128)(2,1)} %student_head.3) | copy-start | bytes 9437188
  64.4 5.1 %collective-permute-start = (bf16[16,288,256]{2,1,0:T(8,128)(2,1)S(1)}, bf16[16,288,256]{2,1,0:T(8,128)(2,1)S(1)}, u32[]{:S(2)}, u32[]{:S(2)}) collective-permute-start(bf16[16,288,256]{2,1,0:T(8,128)(2,1)S(1)} %all_to_all.30.mine), channel_id=1, source_target_pairs={{0,16},{16,0},{32,48},{48,32},{64,80},{80,64},{96,112},{112,96},{1... | collective-permute-start | bytes 7077896 | tf_op jit(solution)/shard_map/ppermute | solution.py:372
  78.5 10.3 %all-to-all-start.2 = ((f32[16,8,256]{2,1,0:T(8,128)}), f32[16,8,256]{2,1,0:T(8,128)S(1)}, u32[]{:S(2)}, u32[]{:S(2)}) async-start(f32[16,8,256]{2,1,0:T(8,128)} %get-tuple-element.16), calls=%async_computation.2 | async-start | bytes 262144 | tf_op jit(solution)/shard_map/all_to_all | solution.py:341
  89.6 14.0 %all-to-all-start.3 = ((f32[16,8,256]{2,1,0:T(8,128)}), f32[16,8,256]{2,1,0:T(8,128)S(1)}, u32[]{:S(2)}, u32[]{:S(2)}) async-start(f32[16,8,256]{2,1,0:T(8,128)} %shard_map.105), calls=%async_computation.3 | async-start | bytes 262144 | tf_op jit(solution)/shard_map/all_to_all | solution.py:341
  103.6 1.9 %copy-start.1 = (bf16[4096,384]{1,0:T(8,128)(2,1)S(1)}, bf16[4096,384]{1,0:T(8,128)(2,1)}, u32[]{:S(2)}) copy-start(bf16[4096,384]{1,0:T(8,128)(2,1)} %student_head.3) | copy-start | bytes 9437188
  108.3 2.7 %collective-permute-start.1 = (bf16[16,128,256]{2,1,0:T(8,128)(2,1)S(1)}, bf16[16,128,256]{2,1,0:T(8,128)(2,1)S(1)}, u32[]{:S(2)}, u32[]{:S(2)}) collective-permute-start(bf16[16,128,256]{2,1,0:T(8,128)(2,1)S(1)} %get-tuple-element.23), channel_id=1, source_target_pairs={{0,16},{16,0},{32,48},{48,32},{64,80},{80,64},{96,112},{112,96},{1... | collective-permute-start | bytes 3145736 | tf_op jit(solution)/shard_map/ppermute | solution.py:419
  133.3 14.1 %all-to-all-start.5 = ((bf16[16,32,128]{2,1,0:T(8,128)(2,1)}), bf16[16,32,128]{2,1,0:T(8,128)(2,1)S(1)}, u32[]{:S(2)}, u32[]{:S(2)}) async-start(bf16[16,32,128]{2,1,0:T(8,128)(2,1)} %shard_map.108), calls=%async_computation.5 | async-start | bytes 262144 | tf_op jit(solution)/shard_map/all_to_all | solution.py:341
  138.2 9.2 %copy-start.4 = (bf16[24,256]{1,0:T(8,128)(2,1)S(1)}, bf16[24,256]{1,0:T(8,128)(2,1)}, u32[]{:S(2)}) copy-start(bf16[24,256]{1,0:T(8,128)(2,1)} %hidden.1) | copy-start | bytes 36868
  138.2 9.2 %copy-start.6 = (f32[256]{0:T(256)S(1)}, f32[256]{0:T(256)}, u32[]{:S(2)}) copy-start(f32[256]{0:T(256)} %param.8) | copy-start | bytes 3076

commit v3 on v2

v3 whole, which is shorter than its diff:
```python
import jax
import jax.numpy as jnp
from jax import lax
from jax.experimental import pallas as pl
from jax.experimental.pallas import tpu as pltpu
from jax.sharding import PartitionSpec as P

DS = 4096
SEQ = 2
VALID = 240
LANES = 256
EPSILON = 1e-06
GROUPS = 16
VOC = 16
ROWS = 24
HALF_S = 128
HALF_T = 160
HALF = HALF_S + HALF_T
VOC_DEV = 384
STATS = 8
SEND = 32
PER = 4
SPARE = 16
BF = jnp.bfloat16
F32 = jnp.float32
CORE_SWAP = [(i, i ^ 1) for i in range(GROUPS)]
TN = (((0,), (0,)), ((), ()))
NT = (((1,), (1,)), ((), ()))
NN = (((1,), (0,)), ((), ()))


def rounded(x):
    return lax.reduce_precision(x, 8, 7)


def dot(a, b, dims):
    return lax.dot_general(a, b, dims, preferred_element_type=F32)


def lane_tables(episode_source, lengths):
    episodes = lengths.shape[0]
    two = (lengths == 2).astype(jnp.int32)
    before = jnp.arange(episodes)[None, :] < jnp.arange(episodes)[:, None]
    rank = jnp.sum(jnp.where(before, two[None, :], 0), axis=1)
    lane = jnp.arange(LANES, dtype=jnp.int32)
    number = jnp.arange(episodes, dtype=jnp.int32)
    first = lane[None, :] == number[:, None]
    second = (two[:, None] == 1) & (lane[None, :] == episodes + rank[:, None])
    pick = first | second
    position = (lane >= episodes).astype(jnp.int32)
    inside = lane < VALID
    episode = jnp.sum(jnp.where(pick, number[:, None], 0), axis=0)
    source = jnp.sum(jnp.where(pick, episode_source[:, None], 0), axis=0)
    length = jnp.sum(jnp.where(pick, lengths[:, None], 0), axis=0)
    student_row = jnp.where(inside, episode * SEQ + position, -1)
    teacher_row = jnp.where(inside, source * SEQ + position, -1)
    weight = jnp.where(inside, 1.0 / jnp.maximum(length, 1).astype(F32), 0.0)
    return student_row[None], teacher_row[None], weight[None]


def own_core():
    return lax.rem(lax.axis_index("grp"), 2)


def lane_iota(shape):
    return lax.broadcasted_iota(jnp.int32, shape, len(shape) - 1)


def pack_kernel(student_in, teacher_in, out, student, teacher, sems):
    copies = [
        pltpu.make_async_copy(student_in, student, sems.at[0]),
        pltpu.make_async_copy(teacher_in, teacher, sems.at[1]),
    ]
    for copy in copies:
        copy.start()
    for copy in copies:
        copy.wait()
    for c in range(2):
        half = jnp.concatenate(
            [
                student[:, c * HALF_S : (c + 1) * HALF_S],
                teacher[:, c * HALF_T : (c + 1) * HALF_T],
            ],
            axis=1,
        )
        for z in range(GROUPS // 2):
            out[2 * z + c] = half


def spare_lanes():
    source = lax.broadcasted_iota(jnp.int32, (LANES, LANES), 0)
    lane = lane_iota((LANES, LANES))
    return jnp.where(lane == VALID + lax.rem(source, SPARE), 1.0, 0.0).astype(BF)


def spare_rows():
    row = lax.broadcasted_iota(jnp.int32, (SPARE, LANES), 0)
    return lax.div(lane_iota((SPARE, LANES)), SPARE) == row


def split(x, parts):
    out = []
    for _ in range(parts):
        out.append(x.astype(BF))
        x = x - out[-1].astype(F32)
    return out


def compact_kernel(held, student_row, teacher_row, gain, out):
    rows = jnp.concatenate([held[g].astype(F32) for g in range(GROUPS)], axis=0).astype(BF)
    ids = lax.broadcasted_iota(jnp.int32, (GROUPS * ROWS, LANES), 0)
    pick_s = jnp.where(ids == student_row[...], 1.0, 0.0).astype(BF)
    pick_t = jnp.where(ids == teacher_row[...], 1.0, 0.0).astype(BF)
    block_s = dot(rows[:, :HALF_S], pick_s, TN)
    block_t = dot(rows[:, HALF_S:], pick_t, TN).astype(BF)
    spread_gain = dot(gain[...].astype(BF), jnp.ones((16, LANES), BF), TN)
    squares = jnp.sum(block_s * block_s, axis=0, keepdims=True)
    parts = split(jnp.where(spare_rows(), squares, 0.0), 2)
    lanes = spare_lanes()
    spare = jnp.concatenate([dot(part, lanes, NN) for part in parts], axis=0)
    block_s = block_s * spread_gain
    block_s = jnp.concatenate([block_s[: 2 * SPARE] + spare, block_s[2 * SPARE :]], axis=0)
    block_s = block_s.astype(BF)
    for v in range(VOC):
        out[v, :HALF_S, :] = block_s
        out[v, HALF_S:, :] = block_t


def stack_rows(values):
    row = lax.broadcasted_iota(jnp.int32, (STATS, LANES), 0)
    out = jnp.zeros((STATS, LANES), F32)
    for k, value in enumerate(values):
        out = jnp.where(row == k, value, out)
    return out


def total(x):
    return jnp.sum(x, axis=0, keepdims=True)


def combined(stats):
    top_s, sum_s, top_t, sum_t, mean_d, mean_u, mean_du = [stats[:, k, :] for k in range(7)]
    all_s = jnp.max(top_s, axis=0, keepdims=True)
    all_t = jnp.max(top_t, axis=0, keepdims=True)
    shift_s = top_s - all_s
    shift_t = top_t - all_t
    scale_s = jnp.exp(shift_s)
    scale_t = jnp.exp(shift_t)
    shift_d = shift_s - shift_t
    return (
        all_s,
        total(scale_s * sum_s),
        all_t,
        total(scale_t * sum_t),
        total(scale_s * (mean_d + shift_d * sum_s)),
        total(scale_s * (mean_u + shift_s * sum_s)),
        total(
            scale_s
            * (mean_du + shift_s * mean_d + shift_d * mean_u + shift_s * shift_d * sum_s)
        ),
    )


def span_of(v, core, half):
    return pl.ds(pl.multiple_of(v * 2 * half + core * half, 32), half)


def logits_of(rows, student_head, teacher_head, core):
    student = jnp.zeros((VOC_DEV, LANES), F32)
    teacher = jnp.zeros((VOC_DEV, LANES), F32)
    squares = jnp.zeros((SPARE, LANES), F32)
    for j in range(0, VOC, PER):
        group = range(j, j + PER)
        head_s = jnp.concatenate([student_head[span_of(v, core, HALF_S), :] for v in group], axis=0)
        head_t = jnp.concatenate([teacher_head[span_of(v, core, HALF_T), :] for v in group], axis=0)
        rows_s = jnp.concatenate([rows[v, :HALF_S, :] for v in group], axis=0)
        rows_t = jnp.concatenate([rows[v, HALF_S:, :] for v in group], axis=0)
        student = student + dot(head_s, rows_s, TN)
        teacher = teacher + dot(head_t, rows_t, TN)
        for v in group:
            squares = squares + rows[v, :SPARE, :].astype(F32)
            squares = squares + rows[v, SPARE : 2 * SPARE, :].astype(F32)
    return student, teacher, squares


def forward_one(mine, student_head, teacher_head, student_out, teacher_out, squares_out):
    student, teacher, squares = logits_of(mine, student_head, teacher_head, own_core())
    student_out[...] = student
    teacher_out[...] = teacher
    squares_out[...] = squares


def forward_two(
    other, student_head, teacher_head, student_in, teacher_in, squares_in,
    exp_out, ratio_out, stats_out, tops_out, inverse_out,
):
    student, teacher, squares = logits_of(other, student_head, teacher_head, 1 - own_core())
    squares = squares + squares_in[...]
    squares = jnp.where(lane_iota((SPARE, LANES)) >= VALID, squares, 0.0)
    lanes = spare_lanes()
    by_row = sum(dot(part, lanes, NT) for part in split(squares, 3))
    squares = total(jnp.where(spare_rows(), by_row, 0.0))
    inverse = lax.rsqrt(squares / DS + EPSILON)
    inverse_out[...] = inverse
    student = (student + student_in[...]) * inverse
    teacher = teacher + teacher_in[...]

    top_s = jnp.max(student, axis=0, keepdims=True)
    top_t = jnp.max(teacher, axis=0, keepdims=True)
    below = student - top_s
    exp_s = jnp.exp(below)
    below_t = teacher - top_t
    ratio = below - below_t
    exp_out[...] = exp_s
    ratio_out[...] = ratio
    weighted = exp_s * ratio
    stats = stack_rows(
        [
            top_s,
            total(exp_s),
            top_t,
            total(jnp.exp(below_t)),
            total(weighted),
            total(exp_s * below),
            total(weighted * below),
        ]
    )
    tops_out[...] = stats
    for v in range(VOC):
        stats_out[v] = stats


def combine_kernel(stats, out):
    tile = stack_rows(combined(stats))
    for g in range(GROUPS):
        out[g] = tile


def terms_of(rows, student_head, grad, kept, core, out):
    source = lax.broadcasted_iota(jnp.int32, (LANES, LANES), 0)
    to_gain = jnp.where(
        (lane_iota((LANES, LANES)) == VALID) & (source < VALID), 1.0, 0.0
    ).astype(BF)
    for j in range(0, VOC, PER):
        group = range(j, j + PER)
        head = jnp.concatenate([student_head[span_of(v, core, HALF_S), :] for v in group], axis=0)
        term = dot(head, grad, NN)
        part = jnp.concatenate([rows[v, :HALF_S, :] for v in group], axis=0).astype(F32)
        term = term + dot((term * (part * kept)).astype(BF), to_gain, NN)
        term = term.astype(BF)
        for i, v in enumerate(group):
            out[v] = term[i * HALF_S : (i + 1) * HALF_S]


def backward_one(
    stats, tops, exp_in, ratio_in, weight, inverse, student_head, other,
    grad_out, scaled_out, away, pull_out, loss_out,
):
    all_s, total_s, all_t, total_t, sum_d, sum_u, sum_du = combined(stats)
    inside = lane_iota((1, LANES)) < VALID
    mean_d = sum_d / total_s
    mean_u = sum_u / total_s
    covariance = sum_du / total_s - mean_d * mean_u
    divergence = mean_d - jnp.log(total_s) + jnp.log(total_t)
    loss_out[...] = jnp.sum(
        jnp.where(inside, weight[...] * divergence, 0.0), axis=1, keepdims=True
    )
    pull_out[...] = weight[...] * covariance * inverse[...] * inverse[...] / DS
    shift_s = tops[0:1, :] - all_s
    shift_t = tops[2:3, :] - all_t
    factor = weight[...] * jnp.exp(shift_s) / total_s
    offset = shift_s - shift_t - mean_d
    grad = jnp.where(inside, factor * exp_in[...] * (ratio_in[...] + offset), 0.0)
    kept = jnp.where(inside, inverse[...], 0.0)
    scaled_out[...] = (grad * kept).astype(BF)
    grad = grad.astype(BF)
    grad_out[...] = grad
    terms_of(other, student_head, grad, kept, 1 - own_core(), away)


def backward_two(grad, inverse, student_head, mine, stay):
    kept = jnp.where(lane_iota((1, LANES)) < VALID, inverse[...], 0.0)
    terms_of(mine, student_head, grad[...], kept, own_core(), stay)


def head_kernel(mine, other, scaled, out):
    core = own_core()
    first = pl.program_id(0) * PER
    for rows, which in ((mine, core), (other, 1 - core)):
        block = jnp.concatenate([rows[first + i, :HALF_S, :] for i in range(PER)], axis=0)
        result = dot(block, scaled[...], NT).astype(BF)
        for i in range(PER):
            out[span_of(i, which, HALF_S), :] = result[i * HALF_S : (i + 1) * HALF_S]


def pair_kernel(stay, arrived, out):
    for v in range(VOC):
        out[v] = (stay[v].astype(F32) + arrived[v].astype(F32)).astype(BF)


def send_kernel(pieces, student_row, out):
    summed = pieces[0].astype(F32)
    for v in range(1, VOC):
        summed = summed + pieces[v].astype(F32)
    summed = summed.astype(BF)
    slot = lax.broadcasted_iota(jnp.int32, (SEND, LANES), 0)
    extra = (slot == ROWS) & (lane_iota((SEND, LANES)) == VALID)
    for g in range(GROUPS):
        pick = ((slot < ROWS) & (student_row[...] == slot + g * ROWS)) | extra
        out[g] = dot(jnp.where(pick, 1.0, 0.0).astype(BF), summed, NT).astype(BF)


def finish_kernel(pieces, hidden, gain, student_row, inverse, pull, grad_hidden, grad_gain):
    halves = []
    for c in range(2):
        summed = pieces[c].astype(F32)
        for z in range(1, GROUPS // 2):
            summed = summed + pieces[2 * z + c].astype(F32)
        halves.append(summed)
    summed = jnp.concatenate(halves, axis=1)
    grad_gain[...] = summed[ROWS : ROWS + 1] / gain[...]
    first = lax.axis_index("grp") * ROWS
    own = lax.broadcasted_iota(jnp.int32, (ROWS, LANES), 0) + first == student_row[...]
    own_rms = jnp.sum(jnp.where(own, inverse[...], 0.0), axis=1, keepdims=True)
    own_pull = jnp.sum(jnp.where(own, pull[...], 0.0), axis=1, keepdims=True)
    normed_grad = summed[:ROWS]
    result = own_rms * (normed_grad * gain[...]) - hidden[...].astype(F32) * own_pull
    grad_hidden[...] = result.astype(BF)


def shape(dims, dtype):
    return jax.ShapeDtypeStruct(dims, dtype)


def params(mib):
    return pltpu.CompilerParams(vmem_limit_bytes=mib * 1024 * 1024)


def cost(flops):
    return pl.CostEstimate(flops=flops, bytes_accessed=4 * 1024 * 1024, transcendentals=0)


def exchange(x, axis):
    return lax.all_to_all(x, axis, 0, 0, tiled=True)


ANY = pl.BlockSpec(memory_space=pl.ANY)
VMEM = pl.BlockSpec(memory_space=pltpu.VMEM)


def local(
    student_hidden, norm_gain, teacher_hidden, student_head, teacher_head, episode_source, lengths
):
    core = own_core()
    row = shape((1, LANES), F32)
    logits = shape((VOC_DEV, LANES), F32)
    half_rows = shape((VOC, HALF_S, LANES), BF)
    student_row, teacher_row, weight = lane_tables(episode_source, lengths)

    packed = pl.pallas_call(
        pack_kernel,
        out_shape=shape((GROUPS, ROWS, HALF), BF),
        in_specs=[ANY] * 2,
        scratch_shapes=[
            pltpu.VMEM((ROWS, 2 * HALF_S), BF),
            pltpu.VMEM((ROWS, 2 * HALF_T), BF),
            pltpu.SemaphoreType.DMA((2,)),
        ],
        compiler_params=params(4),
    )(student_hidden, teacher_hidden)
    held = exchange(packed, "grp")

    gain_half = lax.dynamic_slice_in_dim(norm_gain, core * HALF_S, HALF_S)
    gain_high = rounded(gain_half)
    gain_mid = rounded(gain_half - gain_high)
    gain_low = gain_half - gain_high - gain_mid
    gain_parts = jnp.concatenate(
        [jnp.stack([gain_high, gain_mid, gain_low]), jnp.zeros((13, HALF_S), F32)], axis=0
    )
    block = pl.pallas_call(
        compact_kernel, out_shape=shape((VOC, HALF, LANES), BF), compiler_params=params(8)
    )(held, student_row, teacher_row, gain_parts)
    mine = exchange(block, "voc")
    other = lax.ppermute(mine, "grp", CORE_SWAP)

    student, teacher, squares = pl.pallas_call(
        forward_one,
        out_shape=(logits, logits, shape((SPARE, LANES), F32)),
        compiler_params=params(12),
        cost_estimate=cost(VOC * HALF * VOC_DEV * LANES * 2),
    )(mine, student_head, teacher_head)
    exp_s, ratio, stats, tops, inverse = pl.pallas_call(
        forward_two,
        out_shape=(
            logits,
            logits,
            shape((VOC, STATS, LANES), F32),
            shape((STATS, LANES), F32),
            row,
        ),
        compiler_params=params(12),
        cost_estimate=cost(VOC * HALF * VOC_DEV * LANES * 2),
    )(other, student_head, teacher_head, student, teacher, squares)

    from_voc = exchange(stats, "voc")
    spread = pl.pallas_call(
        combine_kernel, out_shape=shape((GROUPS, STATS, LANES), F32), compiler_params=params(4)
    )(from_voc)
    from_grp = exchange(spread, "grp")

    grad, scaled, away, pull, loss = pl.pallas_call(
        backward_one,
        out_shape=(
            shape((VOC_DEV, LANES), BF),
            shape((VOC_DEV, LANES), BF),
            half_rows,
            row,
            shape((1, 1), F32),
        ),
        compiler_params=params(8),
        cost_estimate=cost(DS * VOC_DEV * LANES),
    )(from_grp, tops, exp_s, ratio, weight, inverse, student_head, other)
    arrived = lax.ppermute(away, "grp", CORE_SWAP)
    stay = pl.pallas_call(
        backward_two,
        out_shape=half_rows,
        compiler_params=params(8),
        cost_estimate=cost(DS * VOC_DEV * LANES),
    )(grad, inverse, student_head, mine)
    pair = pl.pallas_call(pair_kernel, out_shape=half_rows, compiler_params=params(8))(
        stay, arrived
    )
    pieces = exchange(pair, "voc")
    grad_head = pl.pallas_call(
        head_kernel,
        out_shape=shape((DS, VOC_DEV), BF),
        grid=(VOC // PER,),
        in_specs=[VMEM] * 3,
        out_specs=pl.BlockSpec((DS * PER // VOC, VOC_DEV), lambda i: (i, 0)),
        compiler_params=params(12),
        cost_estimate=cost(DS * VOC_DEV * LANES * 2),
    )(mine, other, scaled)
    outgoing = pl.pallas_call(
        send_kernel, out_shape=shape((GROUPS, SEND, HALF_S), BF), compiler_params=params(8)
    )(pieces, student_row)
    pieces = exchange(outgoing, "grp")
    grad_hidden, grad_gain = pl.pallas_call(
        finish_kernel, out_shape=(shape((ROWS, 2 * HALF_S), BF), row), compiler_params=params(4)
    )(pieces, student_hidden, norm_gain[None], student_row, inverse, pull)
    return (loss.reshape(()), grad_hidden, grad_gain.reshape(-1), grad_head)


def solution(mesh):
    placed = (
        P("grp", "voc"),
        P("voc"),
        P("grp", "voc"),
        P(None, ("grp", "voc")),
        P(None, ("grp", "voc")),
        P(),
        P(),
    )
    return jax.shard_map(
        local,
        mesh=mesh,
        in_specs=placed,
        out_specs=(P(), P("grp", "voc"), P("voc"), P(None, ("grp", "voc"))),
        check_vma=False,
    )
```

time: 149 us -> 142 us (0.953)
  waiting for transfers between devices: 38.1 us -> 27.3 us
  blocking collectives: 58 us -> 67.3 us
  local copies, waits for them, and re-layouts: 4.11 us -> 8.36 us
  starting transfers between devices: 24.2 us -> 20.7 us
  Pallas kernels: 17.4 us -> 14.1 us
  matrix products: 2.95 us -> 0 us
    all_to_all x2 -> x3, blocking collectives: 58 us -> 67.3 us  [exchange(): return lax.all_to_all(x, axis, 0, 0, tiled=True)]
    all_to_all x4 -> x3, waiting for transfers between devices: 31.3 us -> 23.3 us  [exchange(): return lax.all_to_all(x, axis, 0, 0, tiled=True)]
    unnamed x14 -> x32, local copies, waits for them, and re-layouts: 3.33 us -> 8.28 us
    all_to_all x4 -> x3, starting transfers between devices: 23.2 us -> 19.8 us  [exchange(): return lax.all_to_all(x, axis, 0, 0, tiled=True)]
    pallas_call x4 -> x7, Pallas kernels: 14.1 us -> 10.9 us  [the longest x1 3.09 us: local(): pl.pallas_call(head_kernel, out_shape=shape((DS, VOC_DEV), BF), grid=(VOC...]
    dot_general x1 -> x0, matrix products: 2.95 us -> none  [dot(): return lax.dot_general(a, b, dims, preferred_element_type=F32)]
    ppermute x1, waiting for transfers between devices: 2.65 us -> 1.04 us  [local(): arrived = lax.ppermute(away, 'grp', CORE_SWAP)]
  transfers between devices with their start and end apart: 6 -> 5, of which waited for: 6 -> 5; matrix products, arithmetic and copies ran while one was open for 4% -> 2% of each run, Pallas kernels for 0% -> 4%
where the time goes in v3:
time: 142 us; the launch traced here: 141 us
  blocking collectives  67.3 us (47%)
  waiting for transfers between devices  27.3 us (19%)
  starting transfers between devices  20.7 us (15%)
  Pallas kernels  14.1 us (10%)
  local copies, waits for them, and re-layouts  8.36 us (6%)
  other arithmetic  2.55 us (2%)
    all_to_all x3, blocking collectives, exchange(): return lax.all_to_all(x, axis, 0, 0, tiled=True)  67.3 us
    all_to_all x3, waiting for transfers between devices, exchange(): return lax.all_to_all(x, axis, 0, 0, tiled=True)  23.3 us
    all_to_all x3, starting transfers between devices, exchange(): return lax.all_to_all(x, axis, 0, 0, tiled=True)  19.8 us
    unnamed x32, local copies, waits for them, and re-layouts  8.28 us
    pallas_call x1, Pallas kernels, local(): pl.pallas_call(head_kernel, out_shape=shape((DS, VOC_DEV), BF), grid=(VOC...  3.09 us
    ppermute x1, waiting for transfers between devices, local(): other = lax.ppermute(mine, 'grp', CORE_SWAP)  2.89 us
  transfers between devices with their start and end apart: 5, of which 5 were waited for; matrix products, arithmetic and copies ran while one was open for 2% of the time, Pallas kernels for 4%

profile of v3, /device:TPU:1, one launch (start us, length us, event | category | flops | bytes accessed | tf_op | source)
XLA Modules:
  0.0 141.1 jit_solution(2521067188800387395)
XLA Ops:
  2.1 0.8 shard_map.102
  2.9 10.0 %all-to-all-start = ((bf16[16,24,288]{2,1,0:T(8,128)(2,1)}), bf16[16,24,288]{2,1,0:T(8,128)(2,1)S(1)}, u32[]{:S(2)}, u32[]{:S(2)}) async-start(bf16[16,24,288]{2,1,0:T(8,128)(2,1)} %shard_map.102), calls=%async_computation | async-start | bytes 589824 | tf_op jit(solution)/shard_map/all_to_all | solution.py:344
  13.7 0.9 select_reduce_fusion
  15.6 9.7 %all-to-all-done.held = bf16[16,24,288]{2,1,0:T(8,128)(2,1)S(1)} async-done(((bf16[16,24,288]{2,1,0:T(8,128)(2,1)}), bf16[16,24,288]{2,1,0:T(8,128)(2,1)S(1)}, u32[]{:S(2)}, u32[]{:S(2)}) %all-to-all-start) | async-done | bytes 221216 | tf_op jit(solution)/shard_map/all_to_all | solution.py:344
  25.7 38.5 %all_to_all.30.mine = bf16[16,288,256]{2,1,0:T(8,128)(2,1)S(1)} all-to-all(bf16[16,288,256]{2,1,0:T(8,128)(2,1)S(1)} %shard_map.103), channel_id=1, replica_groups=mesh['grp'=16,'voc'=16] {'voc'}, dimensions={0} | all-to-all | bytes 4718592 | tf_op jit(solution)/shard_map/all_to_all | solution.py:344
  64.3 0.9 collective-permute-start
  65.2 1.2 shard_map.104
  66.5 2.9 %collective-permute-done.other = bf16[16,288,256]{2,1,0:T(8,128)(2,1)S(1)} collective-permute-done((bf16[16,288,256]{2,1,0:T(8,128)(2,1)S(1)}, bf16[16,288,256]{2,1,0:T(8,128)(2,1)S(1)}, u32[]{:S(2)}, u32[]{:S(2)}) %collective-permute-start) | collective-permute-done | bytes 2359328 | tf_op jit(solution)/shard_map/ppermute | solution.py:384
  69.4 1.7 %shard_map.105 = (f32[384,256]{1,0:T(8,128)S(1)}, f32[384,256]{1,0:T(8,128)S(1)}, f32[16,8,256]{2,1,0:T(8,128)S(1)}, f32[8,256]{1,0:T(8,128)S(1)}, f32[1,256]{1,0:T(1,128)S(1)}) custom-call(bf16[16,288,256]{2,1,0:T(8,128)(2,1)S(1)} %collective-permute-done.other, bf16[4096,384]{1,0:T(8,128)(2,1)S(1)} %copy-done, bf16[5120,384]{1,0:T(8,128)(2,1)S(1)} %copy-done.7, ...), custom_call_target="tpu_custom_call" | custom-call | flops 905969664 | bytes 4194304 | tf_op jit(solution)/shard_map/pallas_call | solution.py:392
  72.6 9.4 %all_to_all.31.stats = f32[16,8,256]{2,1,0:T(8,128)S(1)} all-to-all(f32[16,8,256]{2,1,0:T(8,128)S(1)} %get-tuple-element.22), channel_id=1, replica_groups=mesh['grp'=16,'voc'=16] {'voc'}, dimensions={0} | all-to-all | bytes 262144 | tf_op jit(solution)/shard_map/all_to_all | solution.py:344
  82.8 4.9 %all-to-all-start.3 = ((f32[16,8,256]{2,1,0:T(8,128)}), f32[16,8,256]{2,1,0:T(8,128)S(1)}, u32[]{:S(2)}, u32[]{:S(2)}) async-start(f32[16,8,256]{2,1,0:T(8,128)} %shard_map.106), calls=%async_computation.3 | async-start | bytes 262144 | tf_op jit(solution)/shard_map/all_to_all | solution.py:344
  87.8 9.2 %all-to-all-done.3.stats = f32[16,8,256]{2,1,0:T(8,128)S(1)} async-done(((f32[16,8,256]{2,1,0:T(8,128)}), f32[16,8,256]{2,1,0:T(8,128)S(1)}, u32[]{:S(2)}, u32[]{:S(2)}) %all-to-all-start.3) | async-done | bytes 131104 | tf_op jit(solution)/shard_map/all_to_all | solution.py:344
  97.0 1.7 %copy-done.5 = bf16[16,288,256]{2,1,0:T(8,128)(2,1)S(1)} copy-done((bf16[16,288,256]{2,1,0:T(8,128)(2,1)S(1)}, bf16[16,288,256]{2,1,0:T(8,128)(2,1)}, u32[]{:S(2)}) %copy-start.5) | copy-done | bytes 2359320
  98.7 1.0 copy-done.9
  99.6 1.0 copy-done.11
  100.6 2.2 %shard_map.107 = (bf16[384,256]{1,0:T(8,128)(2,1)S(1)}, bf16[384,256]{1,0:T(8,128)(2,1)S(1)}, bf16[16,128,256]{2,1,0:T(8,128)(2,1)S(1)}, f32[1,256]{1,0:T(1,128)S(1)}, f32[1,1]{1,0:T(1,128)}) custom-call(f32[16,8,256]{2,1,0:T(8,128)S(1)} %all-to-all-done.3.stats, f32[8,256]{1,0:T(8,128)S(1)} %get-tuple-element.23.tops, f32[384,256]{1,0:T(8,128)S(1)} %copy-done.9, ...), custom_call_target="tpu_custom_call" | custom-call | flops 402653184 | bytes 4194304 | tf_op jit(solution)/shard_map/pallas_call | solution.py:411
  102.8 1.6 %shard_map.108.stay = bf16[16,128,256]{2,1,0:T(8,128)(2,1)S(1)} custom-call(bf16[384,256]{1,0:T(8,128)(2,1)S(1)} %get-tuple-element.28.grad, f32[1,256]{1,0:T(1,128)S(1)} %get-tuple-element.26.inverse, bf16[4096,384]{1,0:T(8,128)(2,1)S(1)} %copy-done, bf16[16,288,256]{2,1,0:T(8,128)(2,1)S(1)} %copy-done.2), custom_call_target="tpu_custom_call" | custom-call | flops 402653184 | bytes 4194304 | tf_op jit(solution)/shard_map/pallas_call | solution.py:424
  104.4 1.0 collective-permute-done.1.arrived
  105.7 19.4 %all_to_all.32.pieces = bf16[16,128,256]{2,1,0:T(8,128)(2,1)S(1)} all-to-all(bf16[16,128,256]{2,1,0:T(8,128)(2,1)S(1)} %shard_map.109), channel_id=1, replica_groups=mesh['grp'=16,'voc'=16] {'voc'}, dimensions={0} | all-to-all | bytes 2097152 | tf_op jit(solution)/shard_map/all_to_all | solution.py:344
  125.1 1.2 shard_map.110
  126.3 4.9 %all-to-all-start.5 = ((bf16[16,32,128]{2,1,0:T(8,128)(2,1)}), bf16[16,32,128]{2,1,0:T(8,128)(2,1)S(1)}, u32[]{:S(2)}, u32[]{:S(2)}) async-start(bf16[16,32,128]{2,1,0:T(8,128)(2,1)} %shard_map.110), calls=%async_computation.5 | async-start | bytes 262144 | tf_op jit(solution)/shard_map/all_to_all | solution.py:344
  131.2 1.7 %copy-done.6 = bf16[16,288,256]{2,1,0:T(8,128)(2,1)S(1)} copy-done((bf16[16,288,256]{2,1,0:T(8,128)(2,1)S(1)}, bf16[16,288,256]{2,1,0:T(8,128)(2,1)}, u32[]{:S(2)}) %copy-start.6) | copy-done | bytes 2359320
  132.9 3.1 %shard_map.112 = bf16[4096,384]{1,0:T(8,128)(2,1)} custom-call(bf16[16,288,256]{2,1,0:T(8,128)(2,1)S(1)} %copy-done.3, bf16[16,288,256]{2,1,0:T(8,128)(2,1)S(1)} %copy-done.6, bf16[384,256]{1,0:T(8,128)(2,1)S(1)} %get-tuple-element.33.scaled), custom_call_target="tpu_custom_call" | custom-call | flops 805306368 | bytes 4194304 | tf_op jit(solution)/shard_map/pallas_call | solution.py:434
  136.0 4.4 %all-to-all-done.5.pieces = bf16[16,32,128]{2,1,0:T(8,128)(2,1)S(1)} async-done(((bf16[16,32,128]{2,1,0:T(8,128)(2,1)}), bf16[16,32,128]{2,1,0:T(8,128)(2,1)S(1)}, u32[]{:S(2)}, u32[]{:S(2)}) %all-to-all-start.5) | async-done | bytes 131104 | tf_op jit(solution)/shard_map/all_to_all | solution.py:344
  (45 shorter events, 6.9 us)
Async XLA Ops:
  0.6 0.7 copy-start.12
  1.3 0.7 copy-start.14
  2.9 22.4 %all-to-all-start = ((bf16[16,24,288]{2,1,0:T(8,128)(2,1)}), bf16[16,24,288]{2,1,0:T(8,128)(2,1)S(1)}, u32[]{:S(2)}, u32[]{:S(2)}) async-start(bf16[16,24,288]{2,1,0:T(8,128)(2,1)} %shard_map.102), calls=%async_computation | async-start | bytes 589824 | tf_op jit(solution)/shard_map/all_to_all | solution.py:344
  15.6 49.7 %copy-start = (bf16[4096,384]{1,0:T(8,128)(2,1)S(1)}, bf16[4096,384]{1,0:T(8,128)(2,1)}, u32[]{:S(2)}) copy-start(bf16[4096,384]{1,0:T(8,128)(2,1)} %student_head.7) | copy-start | bytes 9437188
  25.3 40.0 %copy-start.7 = (bf16[5120,384]{1,0:T(8,128)(2,1)S(1)}, bf16[5120,384]{1,0:T(8,128)(2,1)}, u32[]{:S(2)}) copy-start(bf16[5120,384]{1,0:T(8,128)(2,1)} %teacher_head.3) | copy-start | bytes 11796484
  64.3 2.2 %copy-start.1 = (bf16[16,288,256]{2,1,0:T(8,128)(2,1)}, bf16[16,288,256]{2,1,0:T(8,128)(2,1)S(1)}, u32[]{:S(2)}) copy-start(bf16[16,288,256]{2,1,0:T(8,128)(2,1)S(1)} %all_to_all.30.mine) | copy-start | bytes 7077892
  64.3 5.1 %collective-permute-start = (bf16[16,288,256]{2,1,0:T(8,128)(2,1)S(1)}, bf16[16,288,256]{2,1,0:T(8,128)(2,1)S(1)}, u32[]{:S(2)}, u32[]{:S(2)}) collective-permute-start(bf16[16,288,256]{2,1,0:T(8,128)(2,1)S(1)} %all_to_all.30.mine), channel_id=1, source_target_pairs={{0,16},{16,0},{32,48},{48,32},{64,80},{80,64},{96,112},{112,96},{1... | collective-permute-start | bytes 7077896 | tf_op jit(solution)/shard_map/ppermute | solution.py:384
  69.4 1.7 %copy-start.4 = (bf16[16,288,256]{2,1,0:T(8,128)(2,1)}, bf16[16,288,256]{2,1,0:T(8,128)(2,1)S(1)}, u32[]{:S(2)}) copy-start(bf16[16,288,256]{2,1,0:T(8,128)(2,1)S(1)} %collective-permute-done.other) | copy-start | bytes 7077892
  71.1 0.8 copy-start.8
  71.9 0.8 copy-start.10
  82.8 14.2 %all-to-all-start.3 = ((f32[16,8,256]{2,1,0:T(8,128)}), f32[16,8,256]{2,1,0:T(8,128)S(1)}, u32[]{:S(2)}, u32[]{:S(2)}) async-start(f32[16,8,256]{2,1,0:T(8,128)} %shard_map.106), calls=%async_computation.3 | async-start | bytes 262144 | tf_op jit(solution)/shard_map/all_to_all | solution.py:344
  97.0 1.7 %copy-start.5 = (bf16[16,288,256]{2,1,0:T(8,128)(2,1)S(1)}, bf16[16,288,256]{2,1,0:T(8,128)(2,1)}, u32[]{:S(2)}) copy-start(bf16[16,288,256]{2,1,0:T(8,128)(2,1)} %copy-done.4) | copy-start | bytes 7077892
  98.7 1.0 copy-start.9
  99.6 1.0 copy-start.11
  100.6 2.2 %copy-start.2 = (bf16[16,288,256]{2,1,0:T(8,128)(2,1)S(1)}, bf16[16,288,256]{2,1,0:T(8,128)(2,1)}, u32[]{:S(2)}) copy-start(bf16[16,288,256]{2,1,0:T(8,128)(2,1)} %copy-done.1) | copy-start | bytes 7077892
  102.8 2.7 %collective-permute-start.1 = (bf16[16,128,256]{2,1,0:T(8,128)(2,1)S(1)}, bf16[16,128,256]{2,1,0:T(8,128)(2,1)S(1)}, u32[]{:S(2)}, u32[]{:S(2)}) collective-permute-start(bf16[16,128,256]{2,1,0:T(8,128)(2,1)S(1)} %get-tuple-element.29), channel_id=1, source_target_pairs={{0,16},{16,0},{32,48},{48,32},{64,80},{80,64},{96,112},{112,96},{1... | collective-permute-start | bytes 3145736 | tf_op jit(solution)/shard_map/ppermute | solution.py:423
  104.4 26.8 %copy-start.3 = (bf16[16,288,256]{2,1,0:T(8,128)(2,1)S(1)}, bf16[16,288,256]{2,1,0:T(8,128)(2,1)}, u32[]{:S(2)}) copy-start(bf16[16,288,256]{2,1,0:T(8,128)(2,1)} %copy-done.1) | copy-start | bytes 7077892
  126.3 14.1 %all-to-all-start.5 = ((bf16[16,32,128]{2,1,0:T(8,128)(2,1)}), bf16[16,32,128]{2,1,0:T(8,128)(2,1)S(1)}, u32[]{:S(2)}, u32[]{:S(2)}) async-start(bf16[16,32,128]{2,1,0:T(8,128)(2,1)} %shard_map.110), calls=%async_computation.5 | async-start | bytes 262144 | tf_op jit(solution)/shard_map/all_to_all | solution.py:344
  131.2 1.7 %copy-start.6 = (bf16[16,288,256]{2,1,0:T(8,128)(2,1)S(1)}, bf16[16,288,256]{2,1,0:T(8,128)(2,1)}, u32[]{:S(2)}) copy-start(bf16[16,288,256]{2,1,0:T(8,128)(2,1)} %copy-done.4) | copy-start | bytes 7077892
  132.9 7.5 %copy-start.13 = (bf16[24,256]{1,0:T(8,128)(2,1)S(1)}, bf16[24,256]{1,0:T(8,128)(2,1)}, u32[]{:S(2)}) copy-start(bf16[24,256]{1,0:T(8,128)(2,1)} %hidden.1) | copy-start | bytes 36868
  132.9 7.5 %copy-start.15 = (f32[256]{0:T(256)S(1)}, f32[256]{0:T(256)}, u32[]{:S(2)}) copy-start(f32[256]{0:T(256)} %param.8) | copy-start | bytes 3076

commit v4 on v3

v4 whole, which is shorter than its diff:
```python
import jax
import jax.numpy as jnp
from jax import lax
from jax.experimental import pallas as pl
from jax.experimental.pallas import tpu as pltpu
from jax.sharding import PartitionSpec as P

DS = 4096
SEQ = 2
VALID = 240
LANES = 256
EPSILON = 1e-06
GROUPS = 16
VOC = 16
ROWS = 24
HALF_S = 128
HALF_T = 160
HALF = HALF_S + HALF_T
VOC_DEV = 384
STATS = 8
SEND = 32
PACK = 56
TAIL = 32
PER = 4
SPARE = 16
SIDE = 4
BF = jnp.bfloat16
F32 = jnp.float32
CORE_SWAP = [(i, i ^ 1) for i in range(GROUPS)]
BOTH = ("grp", "voc")


def ring(phase, step):
    pairs = []
    for g in range(GROUPS):
        for v in range(VOC):
            y, x = divmod(v, SIDE)
            if (g % 2 == 0) == (phase == 1):
                x = (x + step) % SIDE
            else:
                y = (y + step) % SIDE
            pairs.append((g * VOC + v, g * VOC + y * SIDE + x))
    return pairs


TN = (((0,), (0,)), ((), ()))
NT = (((1,), (1,)), ((), ()))
NN = (((1,), (0,)), ((), ()))


def rounded(x):
    return lax.reduce_precision(x, 8, 7)


def dot(a, b, dims):
    return lax.dot_general(a, b, dims, preferred_element_type=F32)


def lane_tables(episode_source, lengths):
    episodes = lengths.shape[0]
    two = (lengths == 2).astype(jnp.int32)
    before = jnp.arange(episodes)[None, :] < jnp.arange(episodes)[:, None]
    rank = jnp.sum(jnp.where(before, two[None, :], 0), axis=1)
    lane = jnp.arange(LANES, dtype=jnp.int32)
    number = jnp.arange(episodes, dtype=jnp.int32)
    first = lane[None, :] == number[:, None]
    second = (two[:, None] == 1) & (lane[None, :] == episodes + rank[:, None])
    pick = first | second
    position = (lane >= episodes).astype(jnp.int32)
    inside = lane < VALID
    episode = jnp.sum(jnp.where(pick, number[:, None], 0), axis=0)
    source = jnp.sum(jnp.where(pick, episode_source[:, None], 0), axis=0)
    length = jnp.sum(jnp.where(pick, lengths[:, None], 0), axis=0)
    student_row = jnp.where(inside, episode * SEQ + position, -1)
    teacher_row = jnp.where(inside, source * SEQ + position, -1)
    weight = jnp.where(inside, 1.0 / jnp.maximum(length, 1).astype(F32), 0.0)
    return student_row[None], teacher_row[None], weight[None]


def own_core():
    return lax.rem(lax.axis_index("grp"), 2)


def lane_iota(shape):
    return lax.broadcasted_iota(jnp.int32, shape, len(shape) - 1)


def pack_kernel(student_in, teacher_in, out, student, teacher, in_sems):
    copies = [
        pltpu.make_async_copy(student_in, student, in_sems.at[0]),
        pltpu.make_async_copy(teacher_in, teacher, in_sems.at[1]),
    ]
    for copy in copies:
        copy.start()
    for copy in copies:
        copy.wait()
    for c in range(2):
        rows = teacher[:, c * HALF_T : (c + 1) * HALF_T].astype(F32)
        tail = rows[:, HALF_S:]
        tail = jnp.concatenate(
            [tail[:8], tail[8:16], tail[16:24], jnp.zeros((8, TAIL), F32)], axis=1
        )
        whole = jnp.concatenate(
            [student[:, c * HALF_S : (c + 1) * HALF_S].astype(F32), rows[:, :HALF_S], tail], axis=0
        )
        whole = whole.astype(BF)
        for z in range(GROUPS // 2):
            out[2 * z + c] = whole


def spare_lanes():
    source = lax.broadcasted_iota(jnp.int32, (LANES, LANES), 0)
    lane = lane_iota((LANES, LANES))
    return jnp.where(lane == VALID + lax.rem(source, SPARE), 1.0, 0.0).astype(BF)


def spare_rows():
    row = lax.broadcasted_iota(jnp.int32, (SPARE, LANES), 0)
    return lax.div(lane_iota((SPARE, LANES)), SPARE) == row


def split(x, parts):
    out = []
    for _ in range(parts):
        out.append(x.astype(BF))
        x = x - out[-1].astype(F32)
    return out


def compact_kernel(held, student_row, teacher_row, weight, gain, out, row_out, weight_out):
    row_out[...] = student_row[...]
    weight_out[...] = weight[...]
    blocks = [held[g].astype(F32) for g in range(GROUPS)]
    rows_s = jnp.concatenate([block[:ROWS] for block in blocks], axis=0).astype(BF)
    rows_t = jnp.concatenate([block[ROWS : 2 * ROWS] for block in blocks], axis=0).astype(BF)
    tails = jnp.concatenate([block[2 * ROWS :] for block in blocks], axis=0).astype(BF)
    ids = lax.broadcasted_iota(jnp.int32, (GROUPS * ROWS, LANES), 0)
    pick_s = jnp.where(ids == student_row[...], 1.0, 0.0).astype(BF)
    pick_t = jnp.where(ids == teacher_row[...], 1.0, 0.0).astype(BF)
    block_s = dot(rows_s, pick_s, TN)
    block_t = dot(rows_t, pick_t, TN).astype(BF)
    short = lax.broadcasted_iota(jnp.int32, (GROUPS * 8, LANES), 0)
    short = lax.div(short, 8) * ROWS + lax.rem(short, 8)
    tail = jnp.zeros((TAIL, LANES), F32)
    for k in range(3):
        pick = jnp.where(short + 8 * k == teacher_row[...], 1.0, 0.0).astype(BF)
        tail = tail + dot(tails, pick, TN)[k * TAIL : (k + 1) * TAIL]
    spread_gain = dot(gain[...].astype(BF), jnp.ones((16, LANES), BF), TN)
    squares = jnp.sum(block_s * block_s, axis=0, keepdims=True)
    parts = split(jnp.where(spare_rows(), squares, 0.0), 2)
    lanes = spare_lanes()
    spare = jnp.concatenate([dot(part, lanes, NN) for part in parts], axis=0)
    block_s = block_s * spread_gain
    block_s = jnp.concatenate([block_s[: 2 * SPARE] + spare, block_s[2 * SPARE :]], axis=0)
    out[:HALF_S, :] = block_s.astype(BF)
    out[HALF_S : 2 * HALF_S, :] = block_t
    out[2 * HALF_S :, :] = tail.astype(BF)


def stack_rows(values):
    row = lax.broadcasted_iota(jnp.int32, (STATS, LANES), 0)
    out = jnp.zeros((STATS, LANES), F32)
    for k, value in enumerate(values):
        out = jnp.where(row == k, value, out)
    return out


def total(x):
    return jnp.sum(x, axis=0, keepdims=True)


def combined(stats):
    top_s, sum_s, top_t, sum_t, mean_d, mean_u, mean_du = [stats[:, k, :] for k in range(7)]
    all_s = jnp.max(top_s, axis=0, keepdims=True)
    all_t = jnp.max(top_t, axis=0, keepdims=True)
    shift_s = top_s - all_s
    shift_t = top_t - all_t
    scale_s = jnp.exp(shift_s)
    scale_t = jnp.exp(shift_t)
    shift_d = shift_s - shift_t
    return (
        all_s,
        total(scale_s * sum_s),
        all_t,
        total(scale_t * sum_t),
        total(scale_s * (mean_d + shift_d * sum_s)),
        total(scale_s * (mean_u + shift_s * sum_s)),
        total(
            scale_s
            * (mean_du + shift_s * mean_d + shift_d * mean_u + shift_s * shift_d * sum_s)
        ),
    )


def span_of(v, core, half):
    return pl.ds(pl.multiple_of(v * 2 * half + core * half, 32), half)


def places(core):
    index = lax.axis_index("voc")
    x, y = lax.rem(index, SIDE), lax.div(index, SIDE)
    a = lax.select(core == 0, x, y)
    b = lax.select(core == 0, y, x)

    def place(j, k):
        u = lax.rem(a + SIDE - j, SIDE)
        w = lax.rem(b + SIDE - k, SIDE)
        return lax.select(core == 0, SIDE * w + u, SIDE * u + w)

    return place


def batches(refs, core):
    place = places(core)
    return [
        [(ref, j, place(j, k)) for j in range(SIDE)] for ref, k in zip(refs, (0, 1, 3, 2))
    ]


def logits_of(groups, student_head, teacher_head, core):
    student = jnp.zeros((VOC_DEV, LANES), F32)
    teacher = jnp.zeros((VOC_DEV, LANES), F32)
    squares = jnp.zeros((SPARE, LANES), F32)
    for group in groups:
        head_s = jnp.concatenate(
            [student_head[span_of(v, core, HALF_S), :] for _, _, v in group], axis=0
        )
        head_t = jnp.concatenate(
            [teacher_head[span_of(v, core, HALF_T), :] for _, _, v in group], axis=0
        )
        rows_s = jnp.concatenate([ref[j, :HALF_S, :] for ref, j, _ in group], axis=0)
        rows_t = jnp.concatenate([ref[j, HALF_S:, :] for ref, j, _ in group], axis=0)
        student = student + dot(head_s, rows_s, TN)
        teacher = teacher + dot(head_t, rows_t, TN)
        for ref, j, _ in group:
            squares = squares + ref[j, :SPARE, :].astype(F32)
            squares = squares + ref[j, SPARE : 2 * SPARE, :].astype(F32)
    return student, teacher, squares


def forward_near(
    a, u, d, student_head, teacher_head, student_out, teacher_out, squares_out, zero_out
):
    core = own_core()
    groups = batches((a, u, d), core)
    student, teacher, squares = logits_of(groups, student_head, teacher_head, core)
    student_out[...] = student
    teacher_out[...] = teacher
    squares_out[...] = squares
    zero_out[...] = jnp.zeros((1, LANES), F32)


def forward_mid(
    far, other_a, other_u, other_d, student_head, teacher_head,
    student_in, teacher_in, squares_in, student_out, teacher_out, squares_out,
):
    core = own_core()
    one = logits_of(batches((None, None, None, far), core)[3:], student_head, teacher_head, core)
    groups = batches((other_a, other_u, other_d), 1 - core)
    two = logits_of(groups, student_head, teacher_head, 1 - core)
    student_out[...] = one[0] + two[0] + student_in[...]
    teacher_out[...] = one[1] + two[1] + teacher_in[...]
    squares_out[...] = one[2] + two[2] + squares_in[...]


def forward_last(
    other_far, student_head, teacher_head, student_in, teacher_in, squares_in,
    exp_out, ratio_out, stats_out, tops_out, inverse_out,
):
    core = 1 - own_core()
    student, teacher, squares = logits_of(
        batches((None, None, None, other_far), core)[3:], student_head, teacher_head, core
    )
    squares = squares + squares_in[...]
    squares = jnp.where(lane_iota((SPARE, LANES)) >= VALID, squares, 0.0)
    lanes = spare_lanes()
    by_row = sum(dot(part, lanes, NT) for part in split(squares, 3))
    squares = total(jnp.where(spare_rows(), by_row, 0.0))
    inverse = lax.rsqrt(squares / DS + EPSILON)
    inverse_out[...] = inverse
    student = (student + student_in[...]) * inverse
    teacher = teacher + teacher_in[...]

    top_s = jnp.max(student, axis=0, keepdims=True)
    top_t = jnp.max(teacher, axis=0, keepdims=True)
    below = student - top_s
    exp_s = jnp.exp(below)
    below_t = teacher - top_t
    ratio = below - below_t
    exp_out[...] = exp_s
    ratio_out[...] = ratio
    weighted = exp_s * ratio
    stats = stack_rows(
        [
            top_s,
            total(exp_s),
            top_t,
            total(jnp.exp(below_t)),
            total(weighted),
            total(exp_s * below),
            total(weighted * below),
        ]
    )
    tops_out[...] = stats
    for v in range(VOC):
        stats_out[v] = stats


def combine_kernel(stats, out):
    tile = stack_rows(combined(stats))
    for g in range(GROUPS):
        out[g] = tile


def terms_of(groups, student_head, grad, core, out):
    for group in groups:
        head = jnp.concatenate(
            [student_head[span_of(v, core, HALF_S), :] for _, _, v in group], axis=0
        )
        term = dot(head, grad, NN).astype(BF)
        for i, (_, _, v) in enumerate(group):
            out[v] = term[i * HALF_S : (i + 1) * HALF_S]


def backward_one(
    stats, tops, exp_in, ratio_in, weight, inverse, student_head,
    grad_out, scaled_out, away, pull_out, loss_out,
):
    core = 1 - own_core()
    all_s, total_s, all_t, total_t, sum_d, sum_u, sum_du = combined(stats)
    inside = lane_iota((1, LANES)) < VALID
    mean_d = sum_d / total_s
    mean_u = sum_u / total_s
    covariance = sum_du / total_s - mean_d * mean_u
    divergence = mean_d - jnp.log(total_s) + jnp.log(total_t)
    loss_out[...] = jnp.sum(
        jnp.where(inside, weight[...] * divergence, 0.0), axis=1, keepdims=True
    )
    pull_out[...] = weight[...] * covariance * inverse[...] * inverse[...] / DS
    shift_s = tops[0:1, :] - all_s
    shift_t = tops[2:3, :] - all_t
    factor = weight[...] * jnp.exp(shift_s) / total_s
    offset = shift_s - shift_t - mean_d
    grad = jnp.where(inside, factor * exp_in[...] * (ratio_in[...] + offset), 0.0)
    kept = jnp.where(inside, inverse[...], 0.0)
    scaled_out[...] = (grad * kept).astype(BF)
    grad = grad.astype(BF)
    grad_out[...] = grad
    terms_of(batches((None,) * 4, core), student_head, grad, core, away)


def backward_two(*refs):
    mine, other = refs[:4], refs[4:8]
    grad, student_head, hidden, gain, student_row, inverse, pull = refs[8:15]
    stay, base_out, rows_out, sems = refs[15:]
    core = own_core()
    groups = batches(mine, core)
    copies = []
    for k, part in enumerate((groups, batches(other, 1 - core))):
        for group in part:
            for ref, j, v in group:
                n = len(copies)
                copies.append(
                    pltpu.make_async_copy(
                        ref.at[j, pl.ds(0, HALF_S)], rows_out.at[k, v], sems.at[n]
                    )
                )
                copies[n].start()
    first = lax.axis_index("grp") * ROWS
    own = lax.broadcasted_iota(jnp.int32, (ROWS, LANES), 0) + first == student_row[...]
    own_rms = jnp.sum(jnp.where(own, inverse[...], 0.0), axis=1, keepdims=True)
    own_pull = jnp.sum(jnp.where(own, pull[...], 0.0), axis=1, keepdims=True)
    base_out[:ROWS] = own_rms * gain[...]
    base_out[ROWS : 2 * ROWS] = hidden[...].astype(F32) * own_pull
    base_out[2 * ROWS :] = jnp.broadcast_to(1.0 / gain[...], (8, LANES))
    terms_of(groups, student_head, grad[...], core, stay)
    for copy in copies:
        copy.wait()


def head_kernel(source, scaled_in, out, rows, scaled, blocks, in_sems, scaled_sem, sems):
    waiting = []
    for k in range(2):
        for j in range(VOC // PER):
            waiting.append(
                pltpu.make_async_copy(
                    source.at[k, pl.ds(j * PER, PER)], rows.at[k, pl.ds(j * PER, PER)], in_sems.at[k, j]
                )
            )
    first = pltpu.make_async_copy(scaled_in, scaled, scaled_sem)
    first.start()
    for copy in waiting:
        copy.start()
    first.wait()
    copies = []
    for k, core in enumerate((own_core(), 1 - own_core())):
        for j in range(VOC // PER):
            waiting[k * (VOC // PER) + j].wait()
            block = rows[k, pl.ds(j * PER, PER)].reshape(PER * HALF_S, LANES)
            result = dot(block, scaled[...], NT).astype(BF)
            for i in range(PER):
                n = len(copies)
                blocks[n] = result[i * HALF_S : (i + 1) * HALF_S]
                copies.append(
                    pltpu.make_async_copy(
                        blocks.at[n], out.at[span_of(j * PER + i, core, HALF_S)], sems.at[n]
                    )
                )
                copies[n].start()
    for copy in copies:
        copy.wait()


def pair_kernel(stay, arrived, out):
    for v in range(VOC):
        out[v] = (stay[v].astype(F32) + arrived[v].astype(F32)).astype(BF)


def send_kernel(pieces, student_row, block, inverse, out):
    summed = pieces[0].astype(F32)
    for v in range(1, VOC):
        summed = summed + pieces[v].astype(F32)
    lane = lane_iota((HALF_S, LANES))
    inside = lane < VALID
    scaled = jnp.where(inside, block[:HALF_S, :].astype(F32) * inverse[...], 0.0)
    gain = jnp.sum(summed * scaled, axis=1, keepdims=True)
    summed = jnp.where(lane == VALID, gain, summed).astype(BF)
    slot = lax.broadcasted_iota(jnp.int32, (SEND, LANES), 0)
    extra = (slot == ROWS) & (lane_iota((SEND, LANES)) == VALID)
    picks = []
    for g in range(GROUPS):
        pick = ((slot < ROWS) & (student_row[...] == slot + g * ROWS)) | extra
        picks.append(jnp.where(pick, 1.0, 0.0).astype(BF))
    result = dot(jnp.concatenate(picks, axis=0), summed, NT).astype(BF)
    for g in range(GROUPS):
        out[g] = result[g * SEND : (g + 1) * SEND]


def finish_kernel(pieces_in, base_in, grad_hidden, grad_gain, pieces, base, sems):
    copies = [
        pltpu.make_async_copy(pieces_in, pieces, sems.at[0]),
        pltpu.make_async_copy(base_in, base, sems.at[1]),
    ]
    for copy in copies:
        copy.start()
    for copy in copies:
        copy.wait()
    halves = []
    for c in range(2):
        summed = pieces[c].astype(F32)
        for z in range(1, GROUPS // 2):
            summed = summed + pieces[2 * z + c].astype(F32)
        halves.append(summed)
    summed = jnp.concatenate(halves, axis=1)
    grad_gain[...] = summed[ROWS : ROWS + 1] * base[2 * ROWS : 2 * ROWS + 1]
    grad_hidden[...] = (summed[:ROWS] * base[:ROWS] - base[ROWS : 2 * ROWS]).astype(BF)


def shape(dims, dtype):
    return jax.ShapeDtypeStruct(dims, dtype)


def params(mib):
    return pltpu.CompilerParams(vmem_limit_bytes=mib * 1024 * 1024)


def in_hbm(x):
    return pltpu.with_memory_space_constraint(x, pltpu.HBM)


def cost(flops):
    return pl.CostEstimate(flops=flops, bytes_accessed=4 * 1024 * 1024, transcendentals=0)


def exchange(x, axis):
    return lax.all_to_all(x, axis, 0, 0, tiled=True)


HBM = pl.BlockSpec(memory_space=pltpu.HBM)
ANY = pl.BlockSpec(memory_space=pl.ANY)
VMEM = pl.BlockSpec(memory_space=pltpu.VMEM)


def local(
    student_hidden, norm_gain, teacher_hidden, student_head, teacher_head, episode_source, lengths
):
    core = own_core()
    row = shape((1, LANES), F32)
    logits = shape((VOC_DEV, LANES), F32)
    half_rows = shape((VOC, HALF_S, LANES), BF)
    student_row, teacher_row, weight = lane_tables(episode_source, lengths)

    packed = pl.pallas_call(
        pack_kernel,
        out_shape=pltpu.HBM((GROUPS, PACK, HALF_S), BF),
        in_specs=[HBM] * 2,
        out_specs=VMEM,
        scratch_shapes=[
            pltpu.VMEM((ROWS, 2 * HALF_S), BF),
            pltpu.VMEM((ROWS, 2 * HALF_T), BF),
            pltpu.SemaphoreType.DMA((2,)),
        ],
        compiler_params=params(4),
    )(in_hbm(student_hidden), in_hbm(teacher_hidden))
    held = exchange(packed, "grp")

    gain_half = lax.dynamic_slice_in_dim(norm_gain, core * HALF_S, HALF_S)
    gain_high = rounded(gain_half)
    gain_mid = rounded(gain_half - gain_high)
    gain_low = gain_half - gain_high - gain_mid
    gain_parts = jnp.concatenate(
        [jnp.stack([gain_high, gain_mid, gain_low]), jnp.zeros((13, HALF_S), F32)], axis=0
    )
    block, student_row, weight = pl.pallas_call(
        compact_kernel,
        out_shape=(shape((HALF, LANES), BF), shape((1, LANES), jnp.int32), row),
        compiler_params=params(8),
    )(held, student_row, teacher_row, weight, gain_parts)

    one = lax.ppermute(block, BOTH, ring(1, 1))
    three = lax.ppermute(block, BOTH, ring(1, 3))
    two = lax.ppermute(block, BOTH, ring(1, 2))
    a = jnp.stack([block, one, two, three])
    u = lax.ppermute(a, BOTH, ring(2, 1))
    d = lax.ppermute(a, BOTH, ring(2, 3))
    v = lax.ppermute(u[:2], BOTH, ring(2, 1))
    w = lax.ppermute(d[2:], BOTH, ring(2, 3))
    other = tuple(lax.ppermute(part, "grp", CORE_SWAP) for part in (a, u, d))

    partial = (logits, logits, shape((SPARE, LANES), F32))
    *sums, zero = pl.pallas_call(
        forward_near,
        out_shape=partial + (row,),
        compiler_params=params(12),
        cost_estimate=cost(12 * HALF * VOC_DEV * LANES * 2),
    )(a, u, d, student_head, teacher_head)
    far = jnp.concatenate([v, w], axis=0) + zero.astype(BF)
    mine = (a, u, d, far)
    other = other + (lax.ppermute(far, "grp", CORE_SWAP),)
    sums = pl.pallas_call(
        forward_mid,
        out_shape=partial,
        compiler_params=params(12),
        cost_estimate=cost(VOC * HALF * VOC_DEV * LANES * 2),
    )(far, *other[:3], student_head, teacher_head, *sums)
    exp_s, ratio, stats, tops, inverse = pl.pallas_call(
        forward_last,
        out_shape=(
            logits,
            logits,
            shape((VOC, STATS, LANES), F32),
            shape((STATS, LANES), F32),
            row,
        ),
        compiler_params=params(12),
        cost_estimate=cost(4 * HALF * VOC_DEV * LANES * 2),
    )(other[3], student_head, teacher_head, *sums)

    from_voc = exchange(stats, "voc")
    spread = pl.pallas_call(
        combine_kernel, out_shape=shape((GROUPS, STATS, LANES), F32), compiler_params=params(4)
    )(from_voc)
    from_grp = exchange(spread, "grp")

    grad, scaled, away, pull, loss = pl.pallas_call(
        backward_one,
        out_shape=(
            shape((VOC_DEV, LANES), BF),
            pltpu.HBM((VOC_DEV, LANES), BF),
            half_rows,
            row,
            shape((1, 1), F32),
        ),
        out_specs=(VMEM,) * 5,
        compiler_params=params(8),
        cost_estimate=cost(DS * VOC_DEV * LANES),
    )(from_grp, tops, exp_s, ratio, weight, inverse, student_head)
    arrived = lax.ppermute(away, "grp", CORE_SWAP)
    stay, base, rows = pl.pallas_call(
        backward_two,
        out_shape=(
            half_rows,
            pltpu.HBM((2 * ROWS + 8, LANES), F32),
            pltpu.HBM((2, VOC, HALF_S, LANES), BF),
        ),
        out_specs=(VMEM, VMEM, HBM),
        scratch_shapes=[pltpu.SemaphoreType.DMA((2 * VOC,))],
        compiler_params=params(8),
        cost_estimate=cost(DS * VOC_DEV * LANES),
    )(
        *mine, *other, grad, student_head,
        student_hidden, norm_gain[None], student_row, inverse, pull,
    )
    pair = pl.pallas_call(pair_kernel, out_shape=half_rows, compiler_params=params(8))(
        stay, arrived
    )
    pieces = exchange(pair, "voc")
    grad_head = pl.pallas_call(
        head_kernel,
        out_shape=shape((DS, VOC_DEV), BF),
        in_specs=[HBM] * 2,
        out_specs=HBM,
        scratch_shapes=[
            pltpu.VMEM((2, VOC, HALF_S, LANES), BF),
            pltpu.VMEM((VOC_DEV, LANES), BF),
            pltpu.VMEM((2 * VOC, HALF_S, VOC_DEV), BF),
            pltpu.SemaphoreType.DMA((2, VOC // PER)),
            pltpu.SemaphoreType.DMA,
            pltpu.SemaphoreType.DMA((2 * VOC,)),
        ],
        compiler_params=params(12),
        cost_estimate=cost(DS * VOC_DEV * LANES * 2),
    )(in_hbm(rows), in_hbm(scaled))
    outgoing = pl.pallas_call(
        send_kernel,
        out_shape=pltpu.HBM((GROUPS, SEND, HALF_S), BF),
        out_specs=VMEM,
        compiler_params=params(8),
    )(pieces, student_row, block, inverse)
    pieces = exchange(outgoing, "grp")
    grad_hidden, grad_gain = pl.pallas_call(
        finish_kernel,
        out_shape=(shape((ROWS, 2 * HALF_S), BF), row),
        in_specs=[ANY, HBM],
        scratch_shapes=[
            pltpu.VMEM((GROUPS, SEND, HALF_S), BF),
            pltpu.VMEM((2 * ROWS + 8, LANES), F32),
            pltpu.SemaphoreType.DMA((2,)),
        ],
        compiler_params=params(4),
    )(pieces, in_hbm(base))
    return (loss.reshape(()), grad_hidden, grad_gain.reshape(-1), grad_head)


def solution(mesh):
    placed = (
        P("grp", "voc"),
        P("voc"),
        P("grp", "voc"),
        P(None, ("grp", "voc")),
        P(None, ("grp", "voc")),
        P(),
        P(),
    )
    return jax.shard_map(
        local,
        mesh=mesh,
        in_specs=placed,
        out_specs=(P(), P("grp", "voc"), P("voc"), P(None, ("grp", "voc"))),
        check_vma=False,
    )
```

time: 142 us -> 124 us (0.87)
  blocking collectives: 67.3 us -> 42.2 us
  starting transfers between devices: 20.7 us -> 30.7 us
  local copies, waits for them, and re-layouts: 8.36 us -> 2.25 us
  Pallas kernels: 14.1 us -> 17.6 us
    all_to_all x3, blocking collectives: 67.3 us -> 42.2 us  [exchange(): return lax.all_to_all(x, axis, 0, 0, tiled=True)]
    ppermute x1 -> x11, starting transfers between devices: 0.95 us -> 15.6 us  [the longest x1 3.47 us: local(): w = lax.ppermute(d[2:], BOTH, ring(2, 3))]
    ppermute x1 -> x11, waiting for transfers between devices: 2.89 us -> 14.6 us  [the longest x1 6.84 us: local(): d = lax.ppermute(a, BOTH, ring(2, 3))]
    all_to_all x3 -> x2, waiting for transfers between devices: 23.3 us -> 12.5 us  [exchange(): return lax.all_to_all(x, axis, 0, 0, tiled=True)]
    unnamed x32 -> x8, local copies, waits for them, and re-layouts: 8.28 us -> 2.13 us
    all_to_all x3 -> x2, starting transfers between devices: 19.8 us -> 15.2 us  [exchange(): return lax.all_to_all(x, axis, 0, 0, tiled=True)]
    pallas_call x8 -> x9, Pallas kernels: 12.4 us -> 15.6 us  [the longest x1 5.12 us: local(): pl.pallas_call(head_kernel, out_shape=shape((DS, VOC_DEV), BF), in_specs=...]
  transfers between devices with their start and end apart: 5 -> 14, of which waited for: 5 -> 8; matrix products, arithmetic and copies ran while one was open for 2% -> 2% of each run, Pallas kernels for 4% -> 8%
where the time goes in v4:
time: 124 us; the launch traced here: 123 us
  blocking collectives  42.2 us (34%)
  starting transfers between devices  30.7 us (25%)
  waiting for transfers between devices  27.1 us (22%)
  Pallas kernels  17.6 us (14%)
  other arithmetic  2.69 us (2%)
  local copies, waits for them, and re-layouts  2.25 us (2%)
    all_to_all x3, blocking collectives, exchange(): return lax.all_to_all(x, axis, 0, 0, tiled=True)  42.2 us
    all_to_all x2, starting transfers between devices, exchange(): return lax.all_to_all(x, axis, 0, 0, tiled=True)  15.2 us
    all_to_all x2, waiting for transfers between devices, exchange(): return lax.all_to_all(x, axis, 0, 0, tiled=True)  12.5 us
    ppermute x1, waiting for transfers between devices, local(): d = lax.ppermute(a, BOTH, ring(2, 3))  6.84 us
    pallas_call x1, Pallas kernels, local(): pl.pallas_call(head_kernel, out_shape=shape((DS, VOC_DEV), BF), in_specs=...  5.12 us
    ppermute x1, starting transfers between devices, local(): w = lax.ppermute(d[2:], BOTH, ring(2, 3))  3.47 us
    ppermute x1, starting transfers between devices, local(): other = other + (lax.ppermute(far, 'grp', CORE_SWAP),)  3.12 us
    pallas_call x1, Pallas kernels, local(): pl.pallas_call(backward_two, out_shape=(half_rows, pltpu.HBM((2 * ROWS +...  2.89 us
  transfers between devices with their start and end apart: 14, of which 8 were waited for; matrix products, arithmetic and copies ran while one was open for 2% of the time, Pallas kernels for 8%

profile of v4, /device:TPU:1, one launch (start us, length us, event | category | flops | bytes accessed | tf_op | source)
XLA Modules:
  0.0 123.5 jit_solution(18197346915953061730)
XLA Ops:
  0.6 1.7 %shard_map.102 = bf16[16,56,128]{2,1,0:T(8,128)(2,1)} custom-call(bf16[24,256]{1,0:T(8,128)(2,1)} %refs_10_.1, bf16[24,320]{1,0:T(8,128)(2,1)} %teacher_in.1), custom_call_target="tpu_custom_call" | custom-call | tf_op jit(solution)/shard_map/pallas_call | solution.py:493
  2.3 10.0 %all-to-all-start = ((bf16[16,56,128]{2,1,0:T(8,128)(2,1)}), bf16[16,56,128]{2,1,0:T(8,128)(2,1)S(1)}, u32[]{:S(2)}, u32[]{:S(2)}) async-start(bf16[16,56,128]{2,1,0:T(8,128)(2,1)} %shard_map.102), calls=%async_computation | async-start | bytes 458752 | tf_op jit(solution)/shard_map/all_to_all | solution.py:476
  15.0 8.4 %all-to-all-done.held = bf16[16,56,128]{2,1,0:T(8,128)(2,1)S(1)} async-done(((bf16[16,56,128]{2,1,0:T(8,128)(2,1)}), bf16[16,56,128]{2,1,0:T(8,128)(2,1)S(1)}, u32[]{:S(2)}, u32[]{:S(2)}) %all-to-all-start) | async-done | bytes 229408 | tf_op jit(solution)/shard_map/all_to_all | solution.py:476
  23.7 2.8 %collective-permute-start.2 = (bf16[288,256]{1,0:T(8,128)(2,1)S(1)}, bf16[288,256]{1,0:T(8,128)(2,1)S(1)}, u32[]{:S(2)}, u32[]{:S(2)}) collective-permute-start(bf16[288,256]{1,0:T(8,128)(2,1)S(1)} %get-tuple-element.29.block), channel_id=1, source_target_pairs={{0,3},{1,0},{2,1},{3,2},{4,7},{5,4},{6,5},{7,6},{8,11},{9,8},{10,9... | collective-permute-start | bytes 442376 | tf_op jit(solution)/shard_map/ppermute | solution.py:521
  27.6 2.6 %collective-permute-done.2 = bf16[288,256]{1,0:T(8,128)(2,1)S(1)} collective-permute-done((bf16[288,256]{1,0:T(8,128)(2,1)S(1)}, bf16[288,256]{1,0:T(8,128)(2,1)S(1)}, u32[]{:S(2)}, u32[]{:S(2)}) %collective-permute-start.2) | collective-permute-done | bytes 147488 | tf_op jit(solution)/shard_map/ppermute | solution.py:521
  30.2 2.1 %collective-permute-done.1 = bf16[288,256]{1,0:T(8,128)(2,1)S(1)} collective-permute-done((bf16[288,256]{1,0:T(8,128)(2,1)S(1)}, bf16[288,256]{1,0:T(8,128)(2,1)S(1)}, u32[]{:S(2)}, u32[]{:S(2)}) %collective-permute-start.1) | collective-permute-done | bytes 147488 | tf_op jit(solution)/shard_map/ppermute | solution.py:522
  32.4 1.6 %collective-permute-done = bf16[288,256]{1,0:T(8,128)(2,1)S(1)} collective-permute-done((bf16[288,256]{1,0:T(8,128)(2,1)S(1)}, bf16[288,256]{1,0:T(8,128)(2,1)S(1)}, u32[]{:S(2)}, u32[]{:S(2)}) %collective-permute-start) | collective-permute-done | bytes 147488 | tf_op jit(solution)/shard_map/ppermute | solution.py:520
  34.0 2.3 %collective-permute-start.5 = (bf16[4,288,256]{2,1,0:T(8,128)(2,1)S(1)}, bf16[4,288,256]{2,1,0:T(8,128)(2,1)S(1)}, u32[]{:S(2)}, u32[]{:S(2)}) collective-permute-start(bf16[4,288,256]{2,1,0:T(8,128)(2,1)S(1)} %pad_maximum_fusion.a.refs_0_), channel_id=1, source_target_pairs={{0,12},{1,13},{2,14},{3,15},{4,0},{5,1},{6,2},{7,3},{8,4},{9,5},{1... | collective-permute-start | bytes 1769480 | tf_op jit(solution)/shard_map/ppermute | solution.py:525
  36.3 6.8 %collective-permute-done.5.d.refs_2_ = bf16[4,288,256]{2,1,0:T(8,128)(2,1)S(1)} collective-permute-done((bf16[4,288,256]{2,1,0:T(8,128)(2,1)S(1)}, bf16[4,288,256]{2,1,0:T(8,128)(2,1)S(1)}, u32[]{:S(2)}, u32[]{:S(2)}) %collective-permute-start.5) | collective-permute-done | bytes 589856 | tf_op jit(solution)/shard_map/ppermute | solution.py:525
  43.1 3.5 %collective-permute-start.6 = (bf16[2,288,256]{2,1,0:T(8,128)(2,1)S(1)}, bf16[2,288,256]{2,1,0:T(8,128)(2,1)S(1)}, u32[]{:S(2)}, u32[]{:S(2)}) collective-permute-start(bf16[2,288,256]{2,1,0:T(8,128)(2,1)S(1)} %slice.9), channel_id=1, source_target_pairs={{0,12},{1,13},{2,14},{3,15},{4,0},{5,1},{6,2},{7,3},{8,4},{9,5},{1... | collective-permute-start | bytes 884744 | tf_op jit(solution)/shard_map/ppermute | solution.py:527
  46.7 2.3 %collective-permute-start.8 = (bf16[4,288,256]{2,1,0:T(8,128)(2,1)S(1)}, bf16[4,288,256]{2,1,0:T(8,128)(2,1)S(1)}, u32[]{:S(2)}, u32[]{:S(2)}) collective-permute-start(bf16[4,288,256]{2,1,0:T(8,128)(2,1)S(1)} %pad_maximum_fusion.a.refs_0_), channel_id=1, source_target_pairs={{0,16},{16,0},{32,48},{48,32},{64,80},{80,64},{96,112},{112,96},{1... | collective-permute-start | bytes 1769480 | tf_op jit(solution)/shard_map/ppermute | solution.py:528
  49.5 2.1 %copy-done.1 = bf16[5120,384]{1,0:T(8,128)(2,1)S(1)} copy-done((bf16[5120,384]{1,0:T(8,128)(2,1)S(1)}, bf16[5120,384]{1,0:T(8,128)(2,1)}, u32[]{:S(2)}) %copy-start.1) | copy-done | bytes 3932184
  52.7 1.1 collective-permute-done.4
  53.9 3.1 %collective-permute-start.7 = (bf16[4,288,256]{2,1,0:T(8,128)(2,1)S(1)}, bf16[4,288,256]{2,1,0:T(8,128)(2,1)S(1)}, u32[]{:S(2)}, u32[]{:S(2)}) collective-permute-start(bf16[4,288,256]{2,1,0:T(8,128)(2,1)S(1)} %maximum_add_fusion.far.refs_3_), channel_id=1, source_target_pairs={{0,16},{16,0},{32,48},{48,32},{64,80},{80,64},{96,112},{112,96},{1... | collective-permute-start | bytes 1769480 | tf_op jit(solution)/shard_map/ppermute | solution.py:539
  57.0 1.3 %shard_map.105 = (f32[384,256]{1,0:T(8,128)S(1)}, f32[384,256]{1,0:T(8,128)S(1)}, f32[16,256]{1,0:T(8,128)S(1)}) custom-call(bf16[4,288,256]{2,1,0:T(8,128)(2,1)S(1)} %maximum_add_fusion.far.refs_3_, bf16[4,288,256]{2,1,0:T(8,128)(2,1)S(1)} %collective-permute-done.8.other_a.refs_4_, bf16[4,288,256]{2,1,0:T(8,128)(2,1)S(1)} %collective-permute-done.9.other_u.refs_5_, ...), custom_call_target="tpu_custom_call" | custom-call | flops 905969664 | bytes 4194304 | tf_op jit(solution)/shard_map/pallas_call | solution.py:540
  59.4 9.4 %all_to_all.25.stats = f32[16,8,256]{2,1,0:T(8,128)S(1)} all-to-all(f32[16,8,256]{2,1,0:T(8,128)S(1)} %get-tuple-element.37), channel_id=1, replica_groups=mesh['grp'=16,'voc'=16] {'voc'}, dimensions={0} | all-to-all | bytes 262144 | tf_op jit(solution)/shard_map/all_to_all | solution.py:476
  69.0 13.7 %all_to_all.26.stats = f32[16,8,256]{2,1,0:T(8,128)S(1)} all-to-all(f32[16,8,256]{2,1,0:T(8,128)S(1)} %shard_map.107), channel_id=1, replica_groups=mesh['grp'=16,'voc'=16] {'grp'}, dimensions={0} | all-to-all | bytes 262144 | tf_op jit(solution)/shard_map/all_to_all | solution.py:476
  82.7 1.3 %shard_map.108 = (bf16[384,256]{1,0:T(8,128)(2,1)S(1)}, bf16[384,256]{1,0:T(8,128)(2,1)}, bf16[16,128,256]{2,1,0:T(8,128)(2,1)S(1)}, f32[1,256]{1,0:T(1,128)S(1)}, f32[1,1]{1,0:T(1,128)}) custom-call(f32[16,8,256]{2,1,0:T(8,128)S(1)} %all_to_all.26.stats, f32[8,256]{1,0:T(8,128)S(1)} %get-tuple-element.38.tops, f32[384,256]{1,0:T(8,128)S(1)} %get-tuple-element.39.exp_in, ...), custom_call_target="tpu_custom_call" | custom-call | flops 402653184 | bytes 4194304 | tf_op jit(solution)/shard_map/pallas_call | solution.py:565
  84.0 2.9 %shard_map.109 = (bf16[16,128,256]{2,1,0:T(8,128)(2,1)S(1)}, f32[56,256]{1,0:T(8,128)}, bf16[2,16,128,256]{3,2,1,0:T(8,128)(2,1)}) custom-call(bf16[4,288,256]{2,1,0:T(8,128)(2,1)S(1)} %pad_maximum_fusion.a.refs_0_, bf16[4,288,256]{2,1,0:T(8,128)(2,1)S(1)} %collective-permute-done.3.u.refs_1_, bf16[4,288,256]{2,1,0:T(8,128)(2,1)S(1)} %collective-permute-done.5.d.refs_2_, ...), custom_call_target="tpu_custom_call" | custom-call | flops 402653184 | bytes 4194304 | tf_op jit(solution)/shard_map/pallas_call | solution.py:579
  87.2 19.0 %all_to_all.27.pieces = bf16[16,128,256]{2,1,0:T(8,128)(2,1)S(1)} all-to-all(bf16[16,128,256]{2,1,0:T(8,128)(2,1)S(1)} %shard_map.110), channel_id=1, replica_groups=mesh['grp'=16,'voc'=16] {'voc'}, dimensions={0} | all-to-all | bytes 2097152 | tf_op jit(solution)/shard_map/all_to_all | solution.py:476
  107.3 5.2 %all-to-all-start.4 = ((bf16[16,32,128]{2,1,0:T(8,128)(2,1)}), bf16[16,32,128]{2,1,0:T(8,128)(2,1)S(1)}, u32[]{:S(2)}, u32[]{:S(2)}) async-start(bf16[16,32,128]{2,1,0:T(8,128)(2,1)} %shard_map.111), calls=%async_computation.4 | async-start | bytes 262144 | tf_op jit(solution)/shard_map/all_to_all | solution.py:476
  112.5 5.1 %shard_map.113 = bf16[4096,384]{1,0:T(8,128)(2,1)} custom-call(bf16[2,16,128,256]{3,2,1,0:T(8,128)(2,1)} %get-tuple-element.52.source, bf16[384,256]{1,0:T(8,128)(2,1)} %get-tuple-element.53.scaled_in), custom_call_target="tpu_custom_call" | custom-call | flops 805306368 | bytes 4194304 | tf_op jit(solution)/shard_map/pallas_call | solution.py:598
  117.6 4.1 %all-to-all-done.4.pieces_in = bf16[16,32,128]{2,1,0:T(8,128)(2,1)S(1)} async-done(((bf16[16,32,128]{2,1,0:T(8,128)(2,1)}), bf16[16,32,128]{2,1,0:T(8,128)(2,1)S(1)}, u32[]{:S(2)}, u32[]{:S(2)}) %all-to-all-start.4) | async-done | bytes 131104 | tf_op jit(solution)/shard_map/all_to_all | solution.py:476
  121.7 1.6 %shard_map.112 = (bf16[24,256]{1,0:T(8,128)(2,1)}, f32[1,256]{1,0:T(1,128)}) custom-call(bf16[16,32,128]{2,1,0:T(8,128)(2,1)S(1)} %all-to-all-done.4.pieces_in, f32[56,256]{1,0:T(8,128)} %get-tuple-element.49.base_in), custom_call_target="tpu_custom_call" | custom-call | tf_op jit(solution)/shard_map/pallas_call | solution.py:621
  (45 shorter events, 8.5 us)
Async XLA Ops:
  0.6 48.9 %copy-start = (bf16[4096,384]{1,0:T(8,128)(2,1)S(1)}, bf16[4096,384]{1,0:T(8,128)(2,1)}, u32[]{:S(2)}) copy-start(bf16[4096,384]{1,0:T(8,128)(2,1)} %refs_9_.1) | copy-start | bytes 9437188
  2.3 21.0 %all-to-all-start = ((bf16[16,56,128]{2,1,0:T(8,128)(2,1)}), bf16[16,56,128]{2,1,0:T(8,128)(2,1)S(1)}, u32[]{:S(2)}, u32[]{:S(2)}) async-start(bf16[16,56,128]{2,1,0:T(8,128)(2,1)} %shard_map.102), calls=%async_computation | async-start | bytes 458752 | tf_op jit(solution)/shard_map/all_to_all | solution.py:476
  23.7 6.5 %collective-permute-start.2 = (bf16[288,256]{1,0:T(8,128)(2,1)S(1)}, bf16[288,256]{1,0:T(8,128)(2,1)S(1)}, u32[]{:S(2)}, u32[]{:S(2)}) collective-permute-start(bf16[288,256]{1,0:T(8,128)(2,1)S(1)} %get-tuple-element.29.block), channel_id=1, source_target_pairs={{0,3},{1,0},{2,1},{3,2},{4,7},{5,4},{6,5},{7,6},{8,11},{9,8},{10,9... | collective-permute-start | bytes 442376 | tf_op jit(solution)/shard_map/ppermute | solution.py:521
  26.6 5.8 %collective-permute-start.1 = (bf16[288,256]{1,0:T(8,128)(2,1)S(1)}, bf16[288,256]{1,0:T(8,128)(2,1)S(1)}, u32[]{:S(2)}, u32[]{:S(2)}) collective-permute-start(bf16[288,256]{1,0:T(8,128)(2,1)S(1)} %get-tuple-element.29.block), channel_id=1, source_target_pairs={{0,2},{1,3},{2,0},{3,1},{4,6},{5,7},{6,4},{7,5},{8,10},{9,11},{10,... | collective-permute-start | bytes 442376 | tf_op jit(solution)/shard_map/ppermute | solution.py:522
  26.9 7.0 %collective-permute-start = (bf16[288,256]{1,0:T(8,128)(2,1)S(1)}, bf16[288,256]{1,0:T(8,128)(2,1)S(1)}, u32[]{:S(2)}, u32[]{:S(2)}) collective-permute-start(bf16[288,256]{1,0:T(8,128)(2,1)S(1)} %get-tuple-element.29.block), channel_id=1, source_target_pairs={{0,1},{1,2},{2,3},{3,0},{4,5},{5,6},{6,7},{7,4},{8,9},{9,10},{10,1... | collective-permute-start | bytes 442376 | tf_op jit(solution)/shard_map/ppermute | solution.py:520
  34.0 9.1 %collective-permute-start.5 = (bf16[4,288,256]{2,1,0:T(8,128)(2,1)S(1)}, bf16[4,288,256]{2,1,0:T(8,128)(2,1)S(1)}, u32[]{:S(2)}, u32[]{:S(2)}) collective-permute-start(bf16[4,288,256]{2,1,0:T(8,128)(2,1)S(1)} %pad_maximum_fusion.a.refs_0_), channel_id=1, source_target_pairs={{0,12},{1,13},{2,14},{3,15},{4,0},{5,1},{6,2},{7,3},{8,4},{9,5},{1... | collective-permute-start | bytes 1769480 | tf_op jit(solution)/shard_map/ppermute | solution.py:525
  36.3 10.3 %collective-permute-start.3 = (bf16[4,288,256]{2,1,0:T(8,128)(2,1)S(1)}, bf16[4,288,256]{2,1,0:T(8,128)(2,1)S(1)}, u32[]{:S(2)}, u32[]{:S(2)}) collective-permute-start(bf16[4,288,256]{2,1,0:T(8,128)(2,1)S(1)} %pad_maximum_fusion.a.refs_0_), channel_id=1, source_target_pairs={{0,4},{1,5},{2,6},{3,7},{4,8},{5,9},{6,10},{7,11},{8,12},{9,13},{1... | collective-permute-start | bytes 1769480 | tf_op jit(solution)/shard_map/ppermute | solution.py:524
  43.1 9.6 %collective-permute-start.6 = (bf16[2,288,256]{2,1,0:T(8,128)(2,1)S(1)}, bf16[2,288,256]{2,1,0:T(8,128)(2,1)S(1)}, u32[]{:S(2)}, u32[]{:S(2)}) collective-permute-start(bf16[2,288,256]{2,1,0:T(8,128)(2,1)S(1)} %slice.9), channel_id=1, source_target_pairs={{0,12},{1,13},{2,14},{3,15},{4,0},{5,1},{6,2},{7,3},{8,4},{9,5},{1... | collective-permute-start | bytes 884744 | tf_op jit(solution)/shard_map/ppermute | solution.py:527
  46.6 7.2 %collective-permute-start.4 = (bf16[2,288,256]{2,1,0:T(8,128)(2,1)S(1)}, bf16[2,288,256]{2,1,0:T(8,128)(2,1)S(1)}, u32[]{:S(2)}, u32[]{:S(2)}) collective-permute-start(bf16[2,288,256]{2,1,0:T(8,128)(2,1)S(1)} %slice.8), channel_id=1, source_target_pairs={{0,4},{1,5},{2,6},{3,7},{4,8},{5,9},{6,10},{7,11},{8,12},{9,13},{1... | collective-permute-start | bytes 884744 | tf_op jit(solution)/shard_map/ppermute | solution.py:526
  46.7 10.2 %collective-permute-start.8 = (bf16[4,288,256]{2,1,0:T(8,128)(2,1)S(1)}, bf16[4,288,256]{2,1,0:T(8,128)(2,1)S(1)}, u32[]{:S(2)}, u32[]{:S(2)}) collective-permute-start(bf16[4,288,256]{2,1,0:T(8,128)(2,1)S(1)} %pad_maximum_fusion.a.refs_0_), channel_id=1, source_target_pairs={{0,16},{16,0},{32,48},{48,32},{64,80},{80,64},{96,112},{112,96},{1... | collective-permute-start | bytes 1769480 | tf_op jit(solution)/shard_map/ppermute | solution.py:528
  49.0 8.0 %collective-permute-start.10 = (bf16[4,288,256]{2,1,0:T(8,128)(2,1)S(1)}, bf16[4,288,256]{2,1,0:T(8,128)(2,1)S(1)}, u32[]{:S(2)}, u32[]{:S(2)}) collective-permute-start(bf16[4,288,256]{2,1,0:T(8,128)(2,1)S(1)} %collective-permute-done.5.d.refs_2_), channel_id=1, source_target_pairs={{0,16},{16,0},{32,48},{48,32},{64,80},{80,64},{96,112},{112,96},{1... | collective-permute-start | bytes 1769480 | tf_op jit(solution)/shard_map/ppermute | solution.py:528
  49.1 7.9 %collective-permute-start.9 = (bf16[4,288,256]{2,1,0:T(8,128)(2,1)S(1)}, bf16[4,288,256]{2,1,0:T(8,128)(2,1)S(1)}, u32[]{:S(2)}, u32[]{:S(2)}) collective-permute-start(bf16[4,288,256]{2,1,0:T(8,128)(2,1)S(1)} %collective-permute-done.3.u.refs_1_), channel_id=1, source_target_pairs={{0,16},{16,0},{32,48},{48,32},{64,80},{80,64},{96,112},{112,96},{1... | collective-permute-start | bytes 1769480 | tf_op jit(solution)/shard_map/ppermute | solution.py:528
  49.5 2.1 %copy-start.1 = (bf16[5120,384]{1,0:T(8,128)(2,1)S(1)}, bf16[5120,384]{1,0:T(8,128)(2,1)}, u32[]{:S(2)}) copy-start(bf16[5120,384]{1,0:T(8,128)(2,1)} %teacher_head.5) | copy-start | bytes 11796484
  53.9 4.8 %collective-permute-start.7 = (bf16[4,288,256]{2,1,0:T(8,128)(2,1)S(1)}, bf16[4,288,256]{2,1,0:T(8,128)(2,1)S(1)}, u32[]{:S(2)}, u32[]{:S(2)}) collective-permute-start(bf16[4,288,256]{2,1,0:T(8,128)(2,1)S(1)} %maximum_add_fusion.far.refs_3_), channel_id=1, source_target_pairs={{0,16},{16,0},{32,48},{48,32},{64,80},{80,64},{96,112},{112,96},{1... | collective-permute-start | bytes 1769480 | tf_op jit(solution)/shard_map/ppermute | solution.py:539
  59.4 24.6 %copy-start.2 = (bf16[24,256]{1,0:T(8,128)(2,1)S(1)}, bf16[24,256]{1,0:T(8,128)(2,1)}, u32[]{:S(2)}) copy-start(bf16[24,256]{1,0:T(8,128)(2,1)} %refs_10_.1) | copy-start | bytes 36868
  59.4 24.6 %copy-start.3 = (f32[256]{0:T(256)S(1)}, f32[256]{0:T(256)}, u32[]{:S(2)}) copy-start(f32[256]{0:T(256)} %param.8) | copy-start | bytes 3076
  84.0 2.9 %collective-permute-start.11 = (bf16[16,128,256]{2,1,0:T(8,128)(2,1)S(1)}, bf16[16,128,256]{2,1,0:T(8,128)(2,1)S(1)}, u32[]{:S(2)}, u32[]{:S(2)}) collective-permute-start(bf16[16,128,256]{2,1,0:T(8,128)(2,1)S(1)} %get-tuple-element.48), channel_id=1, source_target_pairs={{0,16},{16,0},{32,48},{48,32},{64,80},{80,64},{96,112},{112,96},{1... | collective-permute-start | bytes 3145736 | tf_op jit(solution)/shard_map/ppermute | solution.py:578
  107.3 14.4 %all-to-all-start.4 = ((bf16[16,32,128]{2,1,0:T(8,128)(2,1)}), bf16[16,32,128]{2,1,0:T(8,128)(2,1)S(1)}, u32[]{:S(2)}, u32[]{:S(2)}) async-start(bf16[16,32,128]{2,1,0:T(8,128)(2,1)} %shard_map.111), calls=%async_computation.4 | async-start | bytes 262144 | tf_op jit(solution)/shard_map/all_to_all | solution.py:476

commit v5 on v4

--- a/solution.py
+++ b/solution.py
@@ -356,16 +356,16 @@
     core = own_core()
     groups = batches(mine, core)
     copies = []
-    for k, part in enumerate((groups, batches(other, 1 - core))):
-        for group in part:
-            for ref, j, v in group:
-                n = len(copies)
-                copies.append(
-                    pltpu.make_async_copy(
-                        ref.at[j, pl.ds(0, HALF_S)], rows_out.at[k, v], sems.at[n]
-                    )
+    for k, refs in enumerate((mine, other)):
+        for j, ref in enumerate(refs):
+            copies.append(
+                pltpu.make_async_copy(
+                    ref.at[:, pl.ds(0, HALF_S)],
+                    rows_out.at[k, pl.ds(j * SIDE, SIDE)],
+                    sems.at[k, j],
                 )
-                copies[n].start()
+            )
+            copies[-1].start()
     first = lax.axis_index("grp") * ROWS
     own = lax.broadcasted_iota(jnp.int32, (ROWS, LANES), 0) + first == student_row[...]
     own_rms = jnp.sum(jnp.where(own, inverse[...], 0.0), axis=1, keepdims=True)
@@ -394,16 +394,17 @@
     first.wait()
     copies = []
     for k, core in enumerate((own_core(), 1 - own_core())):
+        groups = batches((None,) * 4, core)
         for j in range(VOC // PER):
             waiting[k * (VOC // PER) + j].wait()
             block = rows[k, pl.ds(j * PER, PER)].reshape(PER * HALF_S, LANES)
             result = dot(block, scaled[...], NT).astype(BF)
-            for i in range(PER):
+            for i, (_, _, v) in enumerate(groups[j]):
                 n = len(copies)
                 blocks[n] = result[i * HALF_S : (i + 1) * HALF_S]
                 copies.append(
                     pltpu.make_async_copy(
-                        blocks.at[n], out.at[span_of(j * PER + i, core, HALF_S)], sems.at[n]
+                        blocks.at[n], out.at[span_of(v, core, HALF_S)], sems.at[n]
                     )
                 )
                 copies[n].start()
@@ -520,11 +521,17 @@
     one = lax.ppermute(block, BOTH, ring(1, 1))
     three = lax.ppermute(block, BOTH, ring(1, 3))
     two = lax.ppermute(block, BOTH, ring(1, 2))
-    a = jnp.stack([block, one, two, three])
-    u = lax.ppermute(a, BOTH, ring(2, 1))
-    d = lax.ppermute(a, BOTH, ring(2, 3))
-    v = lax.ppermute(u[:2], BOTH, ring(2, 1))
-    w = lax.ppermute(d[2:], BOTH, ring(2, 3))
+    first = jnp.stack([block, one])
+    second = jnp.stack([two, three])
+    u_first = lax.ppermute(first, BOTH, ring(2, 1))
+    d_second = lax.ppermute(second, BOTH, ring(2, 3))
+    u_second = lax.ppermute(second, BOTH, ring(2, 1))
+    d_first = lax.ppermute(first, BOTH, ring(2, 3))
+    v = lax.ppermute(u_first, BOTH, ring(2, 1))
+    w = lax.ppermute(d_second, BOTH, ring(2, 3))
+    a = jnp.concatenate([first, second], axis=0)
+    u = jnp.concatenate([u_first, u_second], axis=0)
+    d = jnp.concatenate([d_first, d_second], axis=0)
     other = tuple(lax.ppermute(part, "grp", CORE_SWAP) for part in (a, u, d))
 
     partial = (logits, logits, shape((SPARE, LANES), F32))
@@ -584,7 +591,7 @@
             pltpu.HBM((2, VOC, HALF_S, LANES), BF),
         ),
         out_specs=(VMEM, VMEM, HBM),
-        scratch_shapes=[pltpu.SemaphoreType.DMA((2 * VOC,))],
+        scratch_shapes=[pltpu.SemaphoreType.DMA((2, SIDE))],
         compiler_params=params(8),
         cost_estimate=cost(DS * VOC_DEV * LANES),
     )(

time: 124 us -> 121 us (0.976)
  waiting for transfers between devices: 27.1 us -> 17.3 us
  blocking collectives: 42.2 us -> 46.7 us
  starting transfers between devices: 30.7 us -> 33.3 us
    ppermute x4 -> x6, waiting for transfers between devices: 7.94 us -> 1.25 us  [the longest x1 0.99 us: local(): u_second = lax.ppermute(second, BOTH, ring(2, 1))]
    all_to_all x3, blocking collectives: 42.2 us -> 46.7 us  [exchange(): return lax.all_to_all(x, axis, 0, 0, tiled=True)]
    ppermute x1, waiting for transfers between devices: 2.63 us -> 0.01 us  [local(): three = lax.ppermute(block, BOTH, ring(1, 3))]
    ppermute x3, starting transfers between devices: 2.78 us -> 5.06 us  [local(): other = tuple((lax.ppermute(part, 'grp', CORE_SWAP) for part in (a, u, d)))]
    ppermute x1, starting transfers between devices: 3.12 us -> 1.21 us  [local(): other = other + (lax.ppermute(far, 'grp', CORE_SWAP),)]
    ppermute x4 -> x6, starting transfers between devices: 5.82 us -> 7.39 us  [the longest x1 2.5 us: local(): w = lax.ppermute(d_second, BOTH, ring(2, 3))]
    ppermute x1, starting transfers between devices: 2.81 us -> 1.53 us  [local(): three = lax.ppermute(block, BOTH, ring(1, 3))]
  transfers between devices with their start and end apart: 14 -> 16, of which waited for: 8 -> 7; matrix products, arithmetic and copies ran while one was open for 2% -> 2% of each run, Pallas kernels for 8% -> 8%
where the time goes in v5:
time: 121 us
  blocking collectives  46.7 us (39%)
  starting transfers between devices  33.3 us (28%)
  Pallas kernels  17.3 us (14%)
  waiting for transfers between devices  17.3 us (14%)
  other arithmetic  2.75 us (2%)
  local copies, waits for them, and re-layouts  2.29 us (2%)
    all_to_all x3, blocking collectives, exchange(): return lax.all_to_all(x, axis, 0, 0, tiled=True)  46.7 us
    all_to_all x2, starting transfers between devices, exchange(): return lax.all_to_all(x, axis, 0, 0, tiled=True)  15.2 us
    all_to_all x2, waiting for transfers between devices, exchange(): return lax.all_to_all(x, axis, 0, 0, tiled=True)  12.5 us
    pallas_call x1, Pallas kernels, local(): pl.pallas_call(head_kernel, out_shape=shape((DS, VOC_DEV), BF), in_specs=...  5.12 us
    ppermute x3, starting transfers between devices, local(): other = tuple((lax.ppermute(part, 'grp', CORE_SWAP) for part in (a, u, d)))  5.06 us
    pallas_call x1, Pallas kernels, local(): pl.pallas_call(backward_two, out_shape=(half_rows, pltpu.HBM((2 * ROWS +...  2.63 us
    ppermute x1, starting transfers between devices, local(): w = lax.ppermute(d_second, BOTH, ring(2, 3))  2.5 us
  transfers between devices with their start and end apart: 16, of which 7 were waited for; matrix products, arithmetic and copies ran while one was open for 2% of the time, Pallas kernels for 8%

profile of v5, /device:TPU:1, one launch (start us, length us, event | category | flops | bytes accessed | tf_op | source)
XLA Modules:
  0.0 120.6 jit_solution(1663279389063358434)
XLA Ops:
  0.6 1.7 %shard_map.102 = bf16[16,56,128]{2,1,0:T(8,128)(2,1)} custom-call(bf16[24,256]{1,0:T(8,128)(2,1)} %refs_10_.1, bf16[24,320]{1,0:T(8,128)(2,1)} %teacher_in.1), custom_call_target="tpu_custom_call" | custom-call | tf_op jit(solution)/shard_map/pallas_call | solution.py:494
  2.3 10.0 %all-to-all-start = ((bf16[16,56,128]{2,1,0:T(8,128)(2,1)}), bf16[16,56,128]{2,1,0:T(8,128)(2,1)S(1)}, u32[]{:S(2)}, u32[]{:S(2)}) async-start(bf16[16,56,128]{2,1,0:T(8,128)(2,1)} %shard_map.102), calls=%async_computation | async-start | bytes 458752 | tf_op jit(solution)/shard_map/all_to_all | solution.py:477
  15.0 8.4 %all-to-all-done.held = bf16[16,56,128]{2,1,0:T(8,128)(2,1)S(1)} async-done(((bf16[16,56,128]{2,1,0:T(8,128)(2,1)}), bf16[16,56,128]{2,1,0:T(8,128)(2,1)S(1)}, u32[]{:S(2)}, u32[]{:S(2)}) %all-to-all-start) | async-done | bytes 229408 | tf_op jit(solution)/shard_map/all_to_all | solution.py:477
  23.7 1.4 %collective-permute-start = (bf16[288,256]{1,0:T(8,128)(2,1)S(1)}, bf16[288,256]{1,0:T(8,128)(2,1)S(1)}, u32[]{:S(2)}, u32[]{:S(2)}) collective-permute-start(bf16[288,256]{1,0:T(8,128)(2,1)S(1)} %get-tuple-element.29.block), channel_id=1, source_target_pairs={{0,1},{1,2},{2,3},{3,0},{4,5},{5,6},{6,7},{7,4},{8,9},{9,10},{10,1... | collective-permute-start | bytes 442376 | tf_op jit(solution)/shard_map/ppermute | solution.py:521
  25.1 1.5 %collective-permute-start.4 = (bf16[288,256]{1,0:T(8,128)(2,1)S(1)}, bf16[288,256]{1,0:T(8,128)(2,1)S(1)}, u32[]{:S(2)}, u32[]{:S(2)}) collective-permute-start(bf16[288,256]{1,0:T(8,128)(2,1)S(1)} %get-tuple-element.29.block), channel_id=1, source_target_pairs={{0,3},{1,0},{2,1},{3,2},{4,7},{5,4},{6,5},{7,6},{8,11},{9,8},{10,9... | collective-permute-start | bytes 442376 | tf_op jit(solution)/shard_map/ppermute | solution.py:522
  26.6 1.6 %collective-permute-start.3 = (bf16[288,256]{1,0:T(8,128)(2,1)S(1)}, bf16[288,256]{1,0:T(8,128)(2,1)S(1)}, u32[]{:S(2)}, u32[]{:S(2)}) collective-permute-start(bf16[288,256]{1,0:T(8,128)(2,1)S(1)} %get-tuple-element.29.block), channel_id=1, source_target_pairs={{0,2},{1,3},{2,0},{3,1},{4,6},{5,7},{6,4},{7,5},{8,10},{9,11},{10,... | collective-permute-start | bytes 442376 | tf_op jit(solution)/shard_map/ppermute | solution.py:523
  28.2 1.2 collective-permute-done
  30.4 2.0 %collective-permute-done.3 = bf16[288,256]{1,0:T(8,128)(2,1)S(1)} collective-permute-done((bf16[288,256]{1,0:T(8,128)(2,1)S(1)}, bf16[288,256]{1,0:T(8,128)(2,1)S(1)}, u32[]{:S(2)}, u32[]{:S(2)}) %collective-permute-start.3) | collective-permute-done | bytes 147488 | tf_op jit(solution)/shard_map/ppermute | solution.py:523
  33.5 1.8 %collective-permute-start.5 = (bf16[2,288,256]{2,1,0:T(8,128)(2,1)S(1)}, bf16[2,288,256]{2,1,0:T(8,128)(2,1)S(1)}, u32[]{:S(2)}, u32[]{:S(2)}) collective-permute-start(bf16[2,288,256]{2,1,0:T(8,128)(2,1)S(1)} %pad_maximum_fusion.2), channel_id=1, source_target_pairs={{0,12},{1,13},{2,14},{3,15},{4,0},{5,1},{6,2},{7,3},{8,4},{9,5},{1... | collective-permute-start | bytes 884744 | tf_op jit(solution)/shard_map/ppermute | solution.py:527
  36.3 2.4 %collective-permute-start.10 = (bf16[4,288,256]{2,1,0:T(8,128)(2,1)S(1)}, bf16[4,288,256]{2,1,0:T(8,128)(2,1)S(1)}, u32[]{:S(2)}, u32[]{:S(2)}) collective-permute-start(bf16[4,288,256]{2,1,0:T(8,128)(2,1)S(1)} %pad_maximum_fusion.a.refs_0_), channel_id=1, source_target_pairs={{0,16},{16,0},{32,48},{48,32},{64,80},{80,64},{96,112},{112,96},{1... | collective-permute-start | bytes 1769480 | tf_op jit(solution)/shard_map/ppermute | solution.py:535
  39.8 1.7 %collective-permute-start.11 = (bf16[4,288,256]{2,1,0:T(8,128)(2,1)S(1)}, bf16[4,288,256]{2,1,0:T(8,128)(2,1)S(1)}, u32[]{:S(2)}, u32[]{:S(2)}) collective-permute-start(bf16[4,288,256]{2,1,0:T(8,128)(2,1)S(1)} %constant_dynamic-update-slice_fusion.u.refs_1_), channel_id=1, source_target_pairs={{0,16},{16,0},{32,48},{48,32},{64,80},{80,64},{96,112},{112,96},{1... | collective-permute-start | bytes 1769480 | tf_op jit(solution)/shard_map/ppermute | solution.py:535
  41.7 2.5 %collective-permute-start.6 = (bf16[2,288,256]{2,1,0:T(8,128)(2,1)S(1)}, bf16[2,288,256]{2,1,0:T(8,128)(2,1)S(1)}, u32[]{:S(2)}, u32[]{:S(2)}) collective-permute-start(bf16[2,288,256]{2,1,0:T(8,128)(2,1)S(1)} %collective-permute-done.5), channel_id=1, source_target_pairs={{0,12},{1,13},{2,14},{3,15},{4,0},{5,1},{6,2},{7,3},{8,4},{9,5},{1... | collective-permute-start | bytes 884744 | tf_op jit(solution)/shard_map/ppermute | solution.py:531
  45.1 2.1 %copy-done.1 = bf16[5120,384]{1,0:T(8,128)(2,1)S(1)} copy-done((bf16[5120,384]{1,0:T(8,128)(2,1)S(1)}, bf16[5120,384]{1,0:T(8,128)(2,1)}, u32[]{:S(2)}) %copy-start.1) | copy-done | bytes 3932184
  48.6 1.2 %collective-permute-start.9 = (bf16[4,288,256]{2,1,0:T(8,128)(2,1)S(1)}, bf16[4,288,256]{2,1,0:T(8,128)(2,1)S(1)}, u32[]{:S(2)}, u32[]{:S(2)}) collective-permute-start(bf16[4,288,256]{2,1,0:T(8,128)(2,1)S(1)} %maximum_add_fusion.far.refs_3_), channel_id=1, source_target_pairs={{0,16},{16,0},{32,48},{48,32},{64,80},{80,64},{96,112},{112,96},{1... | collective-permute-start | bytes 1769480 | tf_op jit(solution)/shard_map/ppermute | solution.py:546
  49.8 1.3 %shard_map.105 = (f32[384,256]{1,0:T(8,128)S(1)}, f32[384,256]{1,0:T(8,128)S(1)}, f32[16,256]{1,0:T(8,128)S(1)}) custom-call(bf16[4,288,256]{2,1,0:T(8,128)(2,1)S(1)} %maximum_add_fusion.far.refs_3_, bf16[4,288,256]{2,1,0:T(8,128)(2,1)S(1)} %collective-permute-done.10.other_a.refs_4_, bf16[4,288,256]{2,1,0:T(8,128)(2,1)S(1)} %collective-permute-done.11.other_u.refs_5_, ...), custom_call_target="tpu_custom_call" | custom-call | flops 905969664 | bytes 4194304 | tf_op jit(solution)/shard_map/pallas_call | solution.py:547
  52.3 12.9 %all_to_all.25.stats = f32[16,8,256]{2,1,0:T(8,128)S(1)} all-to-all(f32[16,8,256]{2,1,0:T(8,128)S(1)} %get-tuple-element.37), channel_id=1, replica_groups=mesh['grp'=16,'voc'=16] {'voc'}, dimensions={0} | all-to-all | bytes 262144 | tf_op jit(solution)/shard_map/all_to_all | solution.py:477
  65.3 14.8 %all_to_all.26.stats = f32[16,8,256]{2,1,0:T(8,128)S(1)} all-to-all(f32[16,8,256]{2,1,0:T(8,128)S(1)} %shard_map.107), channel_id=1, replica_groups=mesh['grp'=16,'voc'=16] {'grp'}, dimensions={0} | all-to-all | bytes 262144 | tf_op jit(solution)/shard_map/all_to_all | solution.py:477
  80.1 1.3 %shard_map.108 = (bf16[384,256]{1,0:T(8,128)(2,1)S(1)}, bf16[384,256]{1,0:T(8,128)(2,1)}, bf16[16,128,256]{2,1,0:T(8,128)(2,1)S(1)}, f32[1,256]{1,0:T(1,128)S(1)}, f32[1,1]{1,0:T(1,128)}) custom-call(f32[16,8,256]{2,1,0:T(8,128)S(1)} %all_to_all.26.stats, f32[8,256]{1,0:T(8,128)S(1)} %get-tuple-element.38.tops, f32[384,256]{1,0:T(8,128)S(1)} %get-tuple-element.39.exp_in, ...), custom_call_target="tpu_custom_call" | custom-call | flops 402653184 | bytes 4194304 | tf_op jit(solution)/shard_map/pallas_call | solution.py:572
  81.4 2.6 %shard_map.109 = (bf16[16,128,256]{2,1,0:T(8,128)(2,1)S(1)}, f32[56,256]{1,0:T(8,128)}, bf16[2,16,128,256]{3,2,1,0:T(8,128)(2,1)}) custom-call(bf16[4,288,256]{2,1,0:T(8,128)(2,1)S(1)} %pad_maximum_fusion.a.refs_0_, bf16[4,288,256]{2,1,0:T(8,128)(2,1)S(1)} %constant_dynamic-update-slice_fusion.u.refs_1_, ...), custom_call_target="tpu_custom_call" | custom-call | flops 402653184 | bytes 4194304 | tf_op jit(solution)/shard_map/pallas_call | solution.py:586
  84.3 19.0 %all_to_all.27.pieces = bf16[16,128,256]{2,1,0:T(8,128)(2,1)S(1)} all-to-all(bf16[16,128,256]{2,1,0:T(8,128)(2,1)S(1)} %shard_map.110), channel_id=1, replica_groups=mesh['grp'=16,'voc'=16] {'voc'}, dimensions={0} | all-to-all | bytes 2097152 | tf_op jit(solution)/shard_map/all_to_all | solution.py:477
  104.4 5.2 %all-to-all-start.4 = ((bf16[16,32,128]{2,1,0:T(8,128)(2,1)}), bf16[16,32,128]{2,1,0:T(8,128)(2,1)S(1)}, u32[]{:S(2)}, u32[]{:S(2)}) async-start(bf16[16,32,128]{2,1,0:T(8,128)(2,1)} %shard_map.111), calls=%async_computation.4 | async-start | bytes 262144 | tf_op jit(solution)/shard_map/all_to_all | solution.py:477
  109.6 5.1 %shard_map.113 = bf16[4096,384]{1,0:T(8,128)(2,1)} custom-call(bf16[2,16,128,256]{3,2,1,0:T(8,128)(2,1)} %get-tuple-element.52.source, bf16[384,256]{1,0:T(8,128)(2,1)} %get-tuple-element.53.scaled_in), custom_call_target="tpu_custom_call" | custom-call | flops 805306368 | bytes 4194304 | tf_op jit(solution)/shard_map/pallas_call | solution.py:605
  114.7 4.1 %all-to-all-done.4.pieces_in = bf16[16,32,128]{2,1,0:T(8,128)(2,1)S(1)} async-done(((bf16[16,32,128]{2,1,0:T(8,128)(2,1)}), bf16[16,32,128]{2,1,0:T(8,128)(2,1)S(1)}, u32[]{:S(2)}, u32[]{:S(2)}) %all-to-all-start.4) | async-done | bytes 131104 | tf_op jit(solution)/shard_map/all_to_all | solution.py:477
  118.8 1.6 %shard_map.112 = (bf16[24,256]{1,0:T(8,128)(2,1)}, f32[1,256]{1,0:T(1,128)}) custom-call(bf16[16,32,128]{2,1,0:T(8,128)(2,1)S(1)} %all-to-all-done.4.pieces_in, f32[56,256]{1,0:T(8,128)} %get-tuple-element.49.base_in), custom_call_target="tpu_custom_call" | custom-call | tf_op jit(solution)/shard_map/pallas_call | solution.py:628
  (53 shorter events, 12.3 us)
Async XLA Ops:
  0.6 44.5 %copy-start = (bf16[4096,384]{1,0:T(8,128)(2,1)S(1)}, bf16[4096,384]{1,0:T(8,128)(2,1)}, u32[]{:S(2)}) copy-start(bf16[4096,384]{1,0:T(8,128)(2,1)} %refs_9_.1) | copy-start | bytes 9437188
  2.3 21.0 %all-to-all-start = ((bf16[16,56,128]{2,1,0:T(8,128)(2,1)}), bf16[16,56,128]{2,1,0:T(8,128)(2,1)S(1)}, u32[]{:S(2)}, u32[]{:S(2)}) async-start(bf16[16,56,128]{2,1,0:T(8,128)(2,1)} %shard_map.102), calls=%async_computation | async-start | bytes 458752 | tf_op jit(solution)/shard_map/all_to_all | solution.py:477
  23.7 5.6 %collective-permute-start = (bf16[288,256]{1,0:T(8,128)(2,1)S(1)}, bf16[288,256]{1,0:T(8,128)(2,1)S(1)}, u32[]{:S(2)}, u32[]{:S(2)}) collective-permute-start(bf16[288,256]{1,0:T(8,128)(2,1)S(1)} %get-tuple-element.29.block), channel_id=1, source_target_pairs={{0,1},{1,2},{2,3},{3,0},{4,5},{5,6},{6,7},{7,4},{8,9},{9,10},{10,1... | collective-permute-start | bytes 442376 | tf_op jit(solution)/shard_map/ppermute | solution.py:521
  25.1 5.3 %collective-permute-start.4 = (bf16[288,256]{1,0:T(8,128)(2,1)S(1)}, bf16[288,256]{1,0:T(8,128)(2,1)S(1)}, u32[]{:S(2)}, u32[]{:S(2)}) collective-permute-start(bf16[288,256]{1,0:T(8,128)(2,1)S(1)} %get-tuple-element.29.block), channel_id=1, source_target_pairs={{0,3},{1,0},{2,1},{3,2},{4,7},{5,4},{6,5},{7,6},{8,11},{9,8},{10,9... | collective-permute-start | bytes 442376 | tf_op jit(solution)/shard_map/ppermute | solution.py:522
  26.6 5.8 %collective-permute-start.3 = (bf16[288,256]{1,0:T(8,128)(2,1)S(1)}, bf16[288,256]{1,0:T(8,128)(2,1)S(1)}, u32[]{:S(2)}, u32[]{:S(2)}) collective-permute-start(bf16[288,256]{1,0:T(8,128)(2,1)S(1)} %get-tuple-element.29.block), channel_id=1, source_target_pairs={{0,2},{1,3},{2,0},{3,1},{4,6},{5,7},{6,4},{7,5},{8,10},{9,11},{10,... | collective-permute-start | bytes 442376 | tf_op jit(solution)/shard_map/ppermute | solution.py:523
  29.4 9.3 %collective-permute-start.1 = (bf16[2,288,256]{2,1,0:T(8,128)(2,1)S(1)}, bf16[2,288,256]{2,1,0:T(8,128)(2,1)S(1)}, u32[]{:S(2)}, u32[]{:S(2)}) collective-permute-start(bf16[2,288,256]{2,1,0:T(8,128)(2,1)S(1)} %pad_maximum_fusion.1), channel_id=1, source_target_pairs={{0,4},{1,5},{2,6},{3,7},{4,8},{5,9},{6,10},{7,11},{8,12},{9,13},{1... | collective-permute-start | bytes 884744 | tf_op jit(solution)/shard_map/ppermute | solution.py:526
  32.5 7.3 %collective-permute-start.7 = (bf16[2,288,256]{2,1,0:T(8,128)(2,1)S(1)}, bf16[2,288,256]{2,1,0:T(8,128)(2,1)S(1)}, u32[]{:S(2)}, u32[]{:S(2)}) collective-permute-start(bf16[2,288,256]{2,1,0:T(8,128)(2,1)S(1)} %pad_maximum_fusion.2), channel_id=1, source_target_pairs={{0,4},{1,5},{2,6},{3,7},{4,8},{5,9},{6,10},{7,11},{8,12},{9,13},{1... | collective-permute-start | bytes 884744 | tf_op jit(solution)/shard_map/ppermute | solution.py:528
  33.5 8.2 %collective-permute-start.5 = (bf16[2,288,256]{2,1,0:T(8,128)(2,1)S(1)}, bf16[2,288,256]{2,1,0:T(8,128)(2,1)S(1)}, u32[]{:S(2)}, u32[]{:S(2)}) collective-permute-start(bf16[2,288,256]{2,1,0:T(8,128)(2,1)S(1)} %pad_maximum_fusion.2), channel_id=1, source_target_pairs={{0,12},{1,13},{2,14},{3,15},{4,0},{5,1},{6,2},{7,3},{8,4},{9,5},{1... | collective-permute-start | bytes 884744 | tf_op jit(solution)/shard_map/ppermute | solution.py:527
  35.2 8.9 %collective-permute-start.8 = (bf16[2,288,256]{2,1,0:T(8,128)(2,1)S(1)}, bf16[2,288,256]{2,1,0:T(8,128)(2,1)S(1)}, u32[]{:S(2)}, u32[]{:S(2)}) collective-permute-start(bf16[2,288,256]{2,1,0:T(8,128)(2,1)S(1)} %pad_maximum_fusion.1), channel_id=1, source_target_pairs={{0,12},{1,13},{2,14},{3,15},{4,0},{5,1},{6,2},{7,3},{8,4},{9,5},{1... | collective-permute-start | bytes 884744 | tf_op jit(solution)/shard_map/ppermute | solution.py:529
  36.3 13.6 %collective-permute-start.10 = (bf16[4,288,256]{2,1,0:T(8,128)(2,1)S(1)}, bf16[4,288,256]{2,1,0:T(8,128)(2,1)S(1)}, u32[]{:S(2)}, u32[]{:S(2)}) collective-permute-start(bf16[4,288,256]{2,1,0:T(8,128)(2,1)S(1)} %pad_maximum_fusion.a.refs_0_), channel_id=1, source_target_pairs={{0,16},{16,0},{32,48},{48,32},{64,80},{80,64},{96,112},{112,96},{1... | collective-permute-start | bytes 1769480 | tf_op jit(solution)/shard_map/ppermute | solution.py:535
  39.8 10.1 %collective-permute-start.11 = (bf16[4,288,256]{2,1,0:T(8,128)(2,1)S(1)}, bf16[4,288,256]{2,1,0:T(8,128)(2,1)S(1)}, u32[]{:S(2)}, u32[]{:S(2)}) collective-permute-start(bf16[4,288,256]{2,1,0:T(8,128)(2,1)S(1)} %constant_dynamic-update-slice_fusion.u.refs_1_), channel_id=1, source_target_pairs={{0,16},{16,0},{32,48},{48,32},{64,80},{80,64},{96,112},{112,96},{1... | collective-permute-start | bytes 1769480 | tf_op jit(solution)/shard_map/ppermute | solution.py:535
  41.5 7.1 %collective-permute-start.2 = (bf16[2,288,256]{2,1,0:T(8,128)(2,1)S(1)}, bf16[2,288,256]{2,1,0:T(8,128)(2,1)S(1)}, u32[]{:S(2)}, u32[]{:S(2)}) collective-permute-start(bf16[2,288,256]{2,1,0:T(8,128)(2,1)S(1)} %collective-permute-done.1), channel_id=1, source_target_pairs={{0,4},{1,5},{2,6},{3,7},{4,8},{5,9},{6,10},{7,11},{8,12},{9,13},{1... | collective-permute-start | bytes 884744 | tf_op jit(solution)/shard_map/ppermute | solution.py:530
  41.7 6.6 %collective-permute-start.6 = (bf16[2,288,256]{2,1,0:T(8,128)(2,1)S(1)}, bf16[2,288,256]{2,1,0:T(8,128)(2,1)S(1)}, u32[]{:S(2)}, u32[]{:S(2)}) collective-permute-start(bf16[2,288,256]{2,1,0:T(8,128)(2,1)S(1)} %collective-permute-done.5), channel_id=1, source_target_pairs={{0,12},{1,13},{2,14},{3,15},{4,0},{5,1},{6,2},{7,3},{8,4},{9,5},{1... | collective-permute-start | bytes 884744 | tf_op jit(solution)/shard_map/ppermute | solution.py:531
  44.2 5.6 %collective-permute-start.12 = (bf16[4,288,256]{2,1,0:T(8,128)(2,1)S(1)}, bf16[4,288,256]{2,1,0:T(8,128)(2,1)S(1)}, u32[]{:S(2)}, u32[]{:S(2)}) collective-permute-start(bf16[4,288,256]{2,1,0:T(8,128)(2,1)S(1)} %constant_dynamic-update-slice_fusion.2.d.refs_2_), channel_id=1, source_target_pairs={{0,16},{16,0},{32,48},{48,32},{64,80},{80,64},{96,112},{112,96},{1... | collective-permute-start | bytes 1769480 | tf_op jit(solution)/shard_map/ppermute | solution.py:535
  45.1 2.1 %copy-start.1 = (bf16[5120,384]{1,0:T(8,128)(2,1)S(1)}, bf16[5120,384]{1,0:T(8,128)(2,1)}, u32[]{:S(2)}) copy-start(bf16[5120,384]{1,0:T(8,128)(2,1)} %teacher_head.5) | copy-start | bytes 11796484
  48.6 2.8 %collective-permute-start.9 = (bf16[4,288,256]{2,1,0:T(8,128)(2,1)S(1)}, bf16[4,288,256]{2,1,0:T(8,128)(2,1)S(1)}, u32[]{:S(2)}, u32[]{:S(2)}) collective-permute-start(bf16[4,288,256]{2,1,0:T(8,128)(2,1)S(1)} %maximum_add_fusion.far.refs_3_), channel_id=1, source_target_pairs={{0,16},{16,0},{32,48},{48,32},{64,80},{80,64},{96,112},{112,96},{1... | collective-permute-start | bytes 1769480 | tf_op jit(solution)/shard_map/ppermute | solution.py:546
  52.3 29.1 %copy-start.2 = (bf16[24,256]{1,0:T(8,128)(2,1)S(1)}, bf16[24,256]{1,0:T(8,128)(2,1)}, u32[]{:S(2)}) copy-start(bf16[24,256]{1,0:T(8,128)(2,1)} %refs_10_.1) | copy-start | bytes 36868
  52.3 29.1 %copy-start.3 = (f32[256]{0:T(256)S(1)}, f32[256]{0:T(256)}, u32[]{:S(2)}) copy-start(f32[256]{0:T(256)} %param.8) | copy-start | bytes 3076
  81.4 2.7 %collective-permute-start.13 = (bf16[16,128,256]{2,1,0:T(8,128)(2,1)S(1)}, bf16[16,128,256]{2,1,0:T(8,128)(2,1)S(1)}, u32[]{:S(2)}, u32[]{:S(2)}) collective-permute-start(bf16[16,128,256]{2,1,0:T(8,128)(2,1)S(1)} %get-tuple-element.48), channel_id=1, source_target_pairs={{0,16},{16,0},{32,48},{48,32},{64,80},{80,64},{96,112},{112,96},{1... | collective-permute-start | bytes 3145736 | tf_op jit(solution)/shard_map/ppermute | solution.py:585
  104.4 14.4 %all-to-all-start.4 = ((bf16[16,32,128]{2,1,0:T(8,128)(2,1)}), bf16[16,32,128]{2,1,0:T(8,128)(2,1)S(1)}, u32[]{:S(2)}, u32[]{:S(2)}) async-start(bf16[16,32,128]{2,1,0:T(8,128)(2,1)} %shard_map.111), calls=%async_computation.4 | async-start | bytes 262144 | tf_op jit(solution)/shard_map/all_to_all | solution.py:477

commit v6 on v5

--- a/solution.py
+++ b/solution.py
@@ -238,29 +238,61 @@
     return student, teacher, squares
 
 
-def forward_near(
-    a, u, d, student_head, teacher_head, student_out, teacher_out, squares_out, zero_out
+def forward_own(
+    a, u_first, d_second, student_head, teacher_in,
+    student_out, teacher_out, squares_out, teacher_head, zero_out, sem,
 ):
+    copy = pltpu.make_async_copy(teacher_in, teacher_head, sem)
+    copy.start()
+    zero_out[...] = jnp.zeros((1, LANES), F32)
+    copy.wait()
     core = own_core()
-    groups = batches((a, u, d), core)
-    student, teacher, squares = logits_of(groups, student_head, teacher_head, core)
+    student, teacher, squares = logits_of(batches((a,), core), student_head, teacher_head, core)
     student_out[...] = student
     teacher_out[...] = teacher
     squares_out[...] = squares
+
+
+def save_rows(refs, out, sems):
+    copies = []
+    for k, ref in enumerate(refs):
+        copies.append(
+            pltpu.make_async_copy(
+                ref.at[:, pl.ds(0, HALF_S)], out.at[pl.ds(k * SIDE, SIDE)], sems.at[k]
+            )
+        )
+        copies[k].start()
+    return copies
+
+
+def forward_near(
+    a, u, d, student_head, teacher_head, student_sum, teacher_sum, squares_sum,
+    student_out, teacher_out, squares_out, zero_out, rows_out, row_sems,
+):
+    core = own_core()
+    saved = save_rows((a, u, d), rows_out, row_sems)
+    groups = batches((None, u, d), core)[1:]
+    student, teacher, squares = logits_of(groups, student_head, teacher_head, core)
+    student_out[...] = student + student_sum[...]
+    teacher_out[...] = teacher + teacher_sum[...]
+    squares_out[...] = squares + squares_sum[...]
     zero_out[...] = jnp.zeros((1, LANES), F32)
+    for copy in saved:
+        copy.wait()
 
 
 def forward_mid(
     far, other_a, other_u, other_d, student_head, teacher_head,
-    student_in, teacher_in, squares_in, student_out, teacher_out, squares_out,
+    student_sum, teacher_sum, squares_sum, student_out, teacher_out, squares_out,
 ):
     core = own_core()
-    one = logits_of(batches((None, None, None, far), core)[3:], student_head, teacher_head, core)
+    groups = batches((None, None, None, far), core)[3:]
+    one = logits_of(groups, student_head, teacher_head, core)
     groups = batches((other_a, other_u, other_d), 1 - core)
     two = logits_of(groups, student_head, teacher_head, 1 - core)
-    student_out[...] = one[0] + two[0] + student_in[...]
-    teacher_out[...] = one[1] + two[1] + teacher_in[...]
-    squares_out[...] = one[2] + two[2] + squares_in[...]
+    student_out[...] = one[0] + two[0] + student_sum[...]
+    teacher_out[...] = one[1] + two[1] + teacher_sum[...]
+    squares_out[...] = one[2] + two[2] + squares_sum[...]
 
 
 def forward_last(
@@ -350,22 +382,10 @@
 
 
 def backward_two(*refs):
-    mine, other = refs[:4], refs[4:8]
-    grad, student_head, hidden, gain, student_row, inverse, pull = refs[8:15]
-    stay, base_out, rows_out, sems = refs[15:]
+    grad, student_head, hidden, gain, student_row, inverse, pull = refs[5:12]
+    stay, base_out, rows_out, sems = refs[12:]
+    saved = save_rows(refs[:5], rows_out, sems)
     core = own_core()
-    groups = batches(mine, core)
-    copies = []
-    for k, refs in enumerate((mine, other)):
-        for j, ref in enumerate(refs):
-            copies.append(
-                pltpu.make_async_copy(
-                    ref.at[:, pl.ds(0, HALF_S)],
-                    rows_out.at[k, pl.ds(j * SIDE, SIDE)],
-                    sems.at[k, j],
-                )
-            )
-            copies[-1].start()
     first = lax.axis_index("grp") * ROWS
     own = lax.broadcasted_iota(jnp.int32, (ROWS, LANES), 0) + first == student_row[...]
     own_rms = jnp.sum(jnp.where(own, inverse[...], 0.0), axis=1, keepdims=True)
@@ -373,31 +393,33 @@
     base_out[:ROWS] = own_rms * gain[...]
     base_out[ROWS : 2 * ROWS] = hidden[...].astype(F32) * own_pull
     base_out[2 * ROWS :] = jnp.broadcast_to(1.0 / gain[...], (8, LANES))
-    terms_of(groups, student_head, grad[...], core, stay)
-    for copy in copies:
+    terms_of(batches((None,) * 4, core), student_head, grad[...], core, stay)
+    for copy in saved:
         copy.wait()
 
 
-def head_kernel(source, scaled_in, out, rows, scaled, blocks, in_sems, scaled_sem, sems):
-    waiting = []
-    for k in range(2):
-        for j in range(VOC // PER):
-            waiting.append(
-                pltpu.make_async_copy(
-                    source.at[k, pl.ds(j * PER, PER)], rows.at[k, pl.ds(j * PER, PER)], in_sems.at[k, j]
-                )
-            )
+def head_kernel(
+    near, rest, scaled_in, out, rows, scaled, blocks, in_sems, scaled_sem, sems
+):
     first = pltpu.make_async_copy(scaled_in, scaled, scaled_sem)
     first.start()
-    for copy in waiting:
-        copy.start()
+    waiting = []
+    for n in range(2 * SIDE):
+        source, start = (near, n) if n < 3 else (rest, n - 3)
+        waiting.append(
+            pltpu.make_async_copy(
+                source.at[pl.ds(start * SIDE, SIDE)], rows.at[pl.ds(n * SIDE, SIDE)], in_sems.at[n]
+            )
+        )
+        waiting[n].start()
     first.wait()
     copies = []
     for k, core in enumerate((own_core(), 1 - own_core())):
         groups = batches((None,) * 4, core)
-        for j in range(VOC // PER):
-            waiting[k * (VOC // PER) + j].wait()
-            block = rows[k, pl.ds(j * PER, PER)].reshape(PER * HALF_S, LANES)
+        for j in range(SIDE):
+            m = k * SIDE + j
+            waiting[m].wait()
+            block = rows[pl.ds(m * SIDE, SIDE)].reshape(SIDE * HALF_S, LANES)
             result = dot(block, scaled[...], NT).astype(BF)
             for i, (_, _, v) in enumerate(groups[j]):
                 n = len(copies)
@@ -532,24 +554,39 @@
     a = jnp.concatenate([first, second], axis=0)
     u = jnp.concatenate([u_first, u_second], axis=0)
     d = jnp.concatenate([d_first, d_second], axis=0)
-    other = tuple(lax.ppermute(part, "grp", CORE_SWAP) for part in (a, u, d))
-
     partial = (logits, logits, shape((SPARE, LANES), F32))
-    *sums, zero = pl.pallas_call(
+
+    def sems(count):
+        return pltpu.SemaphoreType.DMA((count,))
+
+    *sums, head_t, zero = pl.pallas_call(
+        forward_own,
+        out_shape=partial + (pltpu.VMEM(teacher_head.shape, BF), row),
+        in_specs=[VMEM, ANY, ANY, VMEM, HBM],
+        out_specs=(VMEM,) * 5,
+        scratch_shapes=[pltpu.SemaphoreType.DMA],
+        compiler_params=params(12),
+        cost_estimate=cost(SIDE * HALF * VOC_DEV * LANES * 2),
+    )(a, u_first, d_second, student_head, in_hbm(teacher_head))
+    other = (lax.ppermute(a, "grp", CORE_SWAP),) + tuple(
+        lax.ppermute(part + zero.astype(BF), "grp", CORE_SWAP) for part in (u, d)
+    )
+    *sums, zero, saved_near = pl.pallas_call(
         forward_near,
-        out_shape=partial + (row,),
+        out_shape=partial + (row, pltpu.HBM((3 * SIDE, HALF_S, LANES), BF)),
+        out_specs=(VMEM,) * 4 + (HBM,),
+        scratch_shapes=[sems(3)],
         compiler_params=params(12),
-        cost_estimate=cost(12 * HALF * VOC_DEV * LANES * 2),
-    )(a, u, d, student_head, teacher_head)
+        cost_estimate=cost(2 * SIDE * HALF * VOC_DEV * LANES * 2),
+    )(a, u, d, student_head, head_t, *sums)
     far = jnp.concatenate([v, w], axis=0) + zero.astype(BF)
-    mine = (a, u, d, far)
-    other = other + (lax.ppermute(far, "grp", CORE_SWAP),)
+    other_far = lax.ppermute(far, "grp", CORE_SWAP)
     sums = pl.pallas_call(
         forward_mid,
         out_shape=partial,
         compiler_params=params(12),
         cost_estimate=cost(VOC * HALF * VOC_DEV * LANES * 2),
-    )(far, *other[:3], student_head, teacher_head, *sums)
+    )(far, *other, student_head, head_t, *sums)
     exp_s, ratio, stats, tops, inverse = pl.pallas_call(
         forward_last,
         out_shape=(
@@ -560,8 +597,8 @@
             row,
         ),
         compiler_params=params(12),
-        cost_estimate=cost(4 * HALF * VOC_DEV * LANES * 2),
-    )(other[3], student_head, teacher_head, *sums)
+        cost_estimate=cost(SIDE * HALF * VOC_DEV * LANES * 2),
+    )(other_far, student_head, head_t, *sums)
 
     from_voc = exchange(stats, "voc")
     spread = pl.pallas_call(
@@ -583,19 +620,19 @@
         cost_estimate=cost(DS * VOC_DEV * LANES),
     )(from_grp, tops, exp_s, ratio, weight, inverse, student_head)
     arrived = lax.ppermute(away, "grp", CORE_SWAP)
-    stay, base, rows = pl.pallas_call(
+    stay, base, saved_rest = pl.pallas_call(
         backward_two,
         out_shape=(
             half_rows,
             pltpu.HBM((2 * ROWS + 8, LANES), F32),
-            pltpu.HBM((2, VOC, HALF_S, LANES), BF),
+            pltpu.HBM((5 * SIDE, HALF_S, LANES), BF),
         ),
         out_specs=(VMEM, VMEM, HBM),
-        scratch_shapes=[pltpu.SemaphoreType.DMA((2, SIDE))],
+        scratch_shapes=[sems(5)],
         compiler_params=params(8),
         cost_estimate=cost(DS * VOC_DEV * LANES),
     )(
-        *mine, *other, grad, student_head,
+        far, *other, other_far, grad, student_head,
         student_hidden, norm_gain[None], student_row, inverse, pull,
     )
     pair = pl.pallas_call(pair_kernel, out_shape=half_rows, compiler_params=params(8))(
@@ -605,19 +642,19 @@
     grad_head = pl.pallas_call(
         head_kernel,
         out_shape=shape((DS, VOC_DEV), BF),
-        in_specs=[HBM] * 2,
+        in_specs=[HBM] * 3,
         out_specs=HBM,
         scratch_shapes=[
-            pltpu.VMEM((2, VOC, HALF_S, LANES), BF),
+            pltpu.VMEM((2 * VOC, HALF_S, LANES), BF),
             pltpu.VMEM((VOC_DEV, LANES), BF),
             pltpu.VMEM((2 * VOC, HALF_S, VOC_DEV), BF),
-            pltpu.SemaphoreType.DMA((2, VOC // PER)),
+            pltpu.SemaphoreType.DMA((2 * SIDE,)),
             pltpu.SemaphoreType.DMA,
             pltpu.SemaphoreType.DMA((2 * VOC,)),
         ],
         compiler_params=params(12),
         cost_estimate=cost(DS * VOC_DEV * LANES * 2),
-    )(in_hbm(rows), in_hbm(scaled))
+    )(in_hbm(saved_near), in_hbm(saved_rest), in_hbm(scaled))
     outgoing = pl.pallas_call(
         send_kernel,
         out_shape=pltpu.HBM((GROUPS, SEND, HALF_S), BF),

time: 121 us -> 119 us (0.983)
  blocking collectives: 46.7 us -> 42.4 us
  Pallas kernels: 17.3 us -> 20.2 us
  local copies, waits for them, and re-layouts: 2.29 us -> 0.18 us
    all_to_all x3, blocking collectives: 46.7 us -> 42.4 us  [exchange(): return lax.all_to_all(x, axis, 0, 0, tiled=True)]
    pallas_call x1 -> x2, Pallas kernels: 1.04 us -> 4.2 us  [the longest x1 2.62 us: local(): pl.pallas_call(forward_own, out_shape=partial + (pltpu.VMEM(teacher_head....]
    ppermute x1, waiting for transfers between devices: 0.01 us -> 2.63 us  [local(): three = lax.ppermute(block, BOTH, ring(1, 3))]
    unnamed x10 -> x8, local copies, waits for them, and re-layouts: 2.17 us -> 0.06 us
    ppermute x1, starting transfers between devices: 0.97 us -> 2.58 us  [local(): d_first = lax.ppermute(first, BOTH, ring(2, 3))]
    ppermute x1, starting transfers between devices: 1.53 us -> 2.81 us  [local(): three = lax.ppermute(block, BOTH, ring(1, 3))]
  transfers between devices with their start and end apart: 16 -> 16, of which waited for: 7 -> 8; matrix products, arithmetic and copies ran while one was open for 2% -> 3% of each run, Pallas kernels for 8% -> 11%
where the time goes in v6:
time: 119 us
  blocking collectives  42.4 us (36%)
  starting transfers between devices  33.6 us (28%)
  Pallas kernels  20.2 us (17%)
  waiting for transfers between devices  18.3 us (15%)
  other arithmetic  2.86 us (2%)
    all_to_all x3, blocking collectives, exchange(): return lax.all_to_all(x, axis, 0, 0, tiled=True)  42.4 us
    all_to_all x2, starting transfers between devices, exchange(): return lax.all_to_all(x, axis, 0, 0, tiled=True)  14.9 us
    all_to_all x2, waiting for transfers between devices, exchange(): return lax.all_to_all(x, axis, 0, 0, tiled=True)  12.5 us
    pallas_call x1, Pallas kernels, local(): pl.pallas_call(head_kernel, out_shape=shape((DS, VOC_DEV), BF), in_specs=...  5.12 us
    ppermute x1, starting transfers between devices, local(): other_far = lax.ppermute(far, 'grp', CORE_SWAP)  2.87 us
    ppermute x1, starting transfers between devices, local(): three = lax.ppermute(block, BOTH, ring(1, 3))  2.81 us
    ppermute x1, waiting for transfers between devices, local(): three = lax.ppermute(block, BOTH, ring(1, 3))  2.63 us
    pallas_call x1, Pallas kernels, local(): pl.pallas_call(forward_own, out_shape=partial + (pltpu.VMEM(teacher_head....  2.62 us
  transfers between devices with their start and end apart: 16, of which 8 were waited for; matrix products, arithmetic and copies ran while one was open for 3% of the time, Pallas kernels for 11%

profile of v6, /device:TPU:1, one launch (start us, length us, event | category | flops | bytes accessed | tf_op | source)
XLA Modules:
  0.0 118.6 jit_solution(8359845553363358608)
XLA Ops:
  0.6 1.7 %shard_map.102 = bf16[16,56,128]{2,1,0:T(8,128)(2,1)} custom-call(bf16[24,256]{1,0:T(8,128)(2,1)} %refs_7_.1, bf16[24,320]{1,0:T(8,128)(2,1)} %teacher_in.2), custom_call_target="tpu_custom_call" | custom-call | tf_op jit(solution)/shard_map/pallas_call | solution.py:516
  2.3 10.0 %all-to-all-start = ((bf16[16,56,128]{2,1,0:T(8,128)(2,1)}), bf16[16,56,128]{2,1,0:T(8,128)(2,1)S(1)}, u32[]{:S(2)}, u32[]{:S(2)}) async-start(bf16[16,56,128]{2,1,0:T(8,128)(2,1)} %shard_map.102), calls=%async_computation | async-start | bytes 458752 | tf_op jit(solution)/shard_map/all_to_all | solution.py:499
  15.0 8.4 %all-to-all-done.held = bf16[16,56,128]{2,1,0:T(8,128)(2,1)S(1)} async-done(((bf16[16,56,128]{2,1,0:T(8,128)(2,1)}), bf16[16,56,128]{2,1,0:T(8,128)(2,1)S(1)}, u32[]{:S(2)}, u32[]{:S(2)}) %all-to-all-start) | async-done | bytes 229408 | tf_op jit(solution)/shard_map/all_to_all | solution.py:499
  23.7 2.8 %collective-permute-start.4 = (bf16[288,256]{1,0:T(8,128)(2,1)S(1)}, bf16[288,256]{1,0:T(8,128)(2,1)S(1)}, u32[]{:S(2)}, u32[]{:S(2)}) collective-permute-start(bf16[288,256]{1,0:T(8,128)(2,1)S(1)} %get-tuple-element.35.block), channel_id=1, source_target_pairs={{0,3},{1,0},{2,1},{3,2},{4,7},{5,4},{6,5},{7,6},{8,11},{9,8},{10,9... | collective-permute-start | bytes 442376 | tf_op jit(solution)/shard_map/ppermute | solution.py:544
  27.6 2.6 %collective-permute-done.4 = bf16[288,256]{1,0:T(8,128)(2,1)S(1)} collective-permute-done((bf16[288,256]{1,0:T(8,128)(2,1)S(1)}, bf16[288,256]{1,0:T(8,128)(2,1)S(1)}, u32[]{:S(2)}, u32[]{:S(2)}) %collective-permute-start.4) | collective-permute-done | bytes 147488 | tf_op jit(solution)/shard_map/ppermute | solution.py:544
  30.2 2.1 %collective-permute-done.3 = bf16[288,256]{1,0:T(8,128)(2,1)S(1)} collective-permute-done((bf16[288,256]{1,0:T(8,128)(2,1)S(1)}, bf16[288,256]{1,0:T(8,128)(2,1)S(1)}, u32[]{:S(2)}, u32[]{:S(2)}) %collective-permute-start.3) | collective-permute-done | bytes 147488 | tf_op jit(solution)/shard_map/ppermute | solution.py:545
  32.4 2.4 %collective-permute-start.5 = (bf16[2,288,256]{2,1,0:T(8,128)(2,1)S(1)}, bf16[2,288,256]{2,1,0:T(8,128)(2,1)S(1)}, u32[]{:S(2)}, u32[]{:S(2)}) collective-permute-start(bf16[2,288,256]{2,1,0:T(8,128)(2,1)S(1)} %pad_maximum_fusion.2), channel_id=1, source_target_pairs={{0,12},{1,13},{2,14},{3,15},{4,0},{5,1},{6,2},{7,3},{8,4},{9,5},{1... | collective-permute-start | bytes 884744 | tf_op jit(solution)/shard_map/ppermute | solution.py:549
  35.0 2.6 %collective-permute-start.8 = (bf16[2,288,256]{2,1,0:T(8,128)(2,1)S(1)}, bf16[2,288,256]{2,1,0:T(8,128)(2,1)S(1)}, u32[]{:S(2)}, u32[]{:S(2)}) collective-permute-start(bf16[2,288,256]{2,1,0:T(8,128)(2,1)S(1)} %pad_maximum_fusion.1), channel_id=1, source_target_pairs={{0,12},{1,13},{2,14},{3,15},{4,0},{5,1},{6,2},{7,3},{8,4},{9,5},{1... | collective-permute-start | bytes 884744 | tf_op jit(solution)/shard_map/ppermute | solution.py:551
  37.7 2.0 %collective-permute-start.10 = (bf16[4,288,256]{2,1,0:T(8,128)(2,1)S(1)}, bf16[4,288,256]{2,1,0:T(8,128)(2,1)S(1)}, u32[]{:S(2)}, u32[]{:S(2)}) collective-permute-start(bf16[4,288,256]{2,1,0:T(8,128)(2,1)S(1)} %pad_maximum_fusion.a), channel_id=1, source_target_pairs={{0,16},{16,0},{32,48},{48,32},{64,80},{80,64},{96,112},{112,96},{1... | collective-permute-start | bytes 1769480 | tf_op jit(solution)/shard_map/ppermute | solution.py:571
  39.7 2.1 %collective-permute-start.6 = (bf16[2,288,256]{2,1,0:T(8,128)(2,1)S(1)}, bf16[2,288,256]{2,1,0:T(8,128)(2,1)S(1)}, u32[]{:S(2)}, u32[]{:S(2)}) collective-permute-start(bf16[2,288,256]{2,1,0:T(8,128)(2,1)S(1)} %collective-permute-done.5.d_second), channel_id=1, source_target_pairs={{0,12},{1,13},{2,14},{3,15},{4,0},{5,1},{6,2},{7,3},{8,4},{9,5},{1... | collective-permute-start | bytes 884744 | tf_op jit(solution)/shard_map/ppermute | solution.py:553
  41.9 2.6 %shard_map.104 = (f32[384,256]{1,0:T(8,128)S(1)}, f32[384,256]{1,0:T(8,128)S(1)}, f32[16,256]{1,0:T(8,128)S(1)}, bf16[5120,384]{1,0:T(8,128)(2,1)S(1)}, f32[1,256]{1,0:T(1,128)S(1)}) custom-call(bf16[4,288,256]{2,1,0:T(8,128)(2,1)S(1)} %pad_maximum_fusion.a, bf16[2,288,256]{2,1,0:T(8,128)(2,1)S(1)} %collective-permute-done.1.u_first, ...), custom_call_target="tpu_custom_call" | custom-call | flops 226492416 | bytes 4194304 | tf_op jit(solution)/shard_map/pallas_call | solution.py:562
  45.2 2.5 %collective-permute-start.12 = (bf16[4,288,256]{2,1,0:T(8,128)(2,1)S(1)}, bf16[4,288,256]{2,1,0:T(8,128)(2,1)S(1)}, u32[]{:S(2)}, u32[]{:S(2)}) collective-permute-start(bf16[4,288,256]{2,1,0:T(8,128)(2,1)S(1)} %get-tuple-element.74), channel_id=1, source_target_pairs={{0,16},{16,0},{32,48},{48,32},{64,80},{80,64},{96,112},{112,96},{1... | collective-permute-start | bytes 1769480 | tf_op jit(solution)/shard_map/ppermute | solution.py:572
  47.8 1.6 %shard_map.105 = (f32[384,256]{1,0:T(8,128)S(1)}, f32[384,256]{1,0:T(8,128)S(1)}, f32[16,256]{1,0:T(8,128)S(1)}, f32[1,256]{1,0:T(1,128)S(1)}, bf16[12,128,256]{2,1,0:T(8,128)(2,1)}) custom-call(bf16[4,288,256]{2,1,0:T(8,128)(2,1)S(1)} %pad_maximum_fusion.a, bf16[4,288,256]{2,1,0:T(8,128)(2,1)S(1)} %constant_dynamic-update-slice_fusion.u, ...), custom_call_target="tpu_custom_call" | custom-call | flops 452984832 | bytes 4194304 | tf_op jit(solution)/shard_map/pallas_call | solution.py:574
  49.5 2.9 %collective-permute-start.9 = (bf16[4,288,256]{2,1,0:T(8,128)(2,1)S(1)}, bf16[4,288,256]{2,1,0:T(8,128)(2,1)S(1)}, u32[]{:S(2)}, u32[]{:S(2)}) collective-permute-start(bf16[4,288,256]{2,1,0:T(8,128)(2,1)S(1)} %maximum_add_fusion.far.refs_0_), channel_id=1, source_target_pairs={{0,16},{16,0},{32,48},{48,32},{64,80},{80,64},{96,112},{112,96},{1... | collective-permute-start | bytes 1769480 | tf_op jit(solution)/shard_map/ppermute | solution.py:583
  52.4 1.3 %shard_map.106 = (f32[384,256]{1,0:T(8,128)S(1)}, f32[384,256]{1,0:T(8,128)S(1)}, f32[16,256]{1,0:T(8,128)S(1)}) custom-call(bf16[4,288,256]{2,1,0:T(8,128)(2,1)S(1)} %maximum_add_fusion.far.refs_0_, bf16[4,288,256]{2,1,0:T(8,128)(2,1)S(1)} %collective-permute-done.10.other_a.refs_1_, bf16[4,288,256]{2,1,0:T(8,128)(2,1)S(1)} %collective-permute-done.11.other_u.refs_2_, ...), custom_call_target="tpu_custom_call" | custom-call | flops 905969664 | bytes 4194304 | tf_op jit(solution)/shard_map/pallas_call | solution.py:584
  54.9 9.4 %all_to_all.25.stats = f32[16,8,256]{2,1,0:T(8,128)S(1)} all-to-all(f32[16,8,256]{2,1,0:T(8,128)S(1)} %get-tuple-element.48), channel_id=1, replica_groups=mesh['grp'=16,'voc'=16] {'voc'}, dimensions={0} | all-to-all | bytes 262144 | tf_op jit(solution)/shard_map/all_to_all | solution.py:499
  64.4 13.7 %all_to_all.26.stats = f32[16,8,256]{2,1,0:T(8,128)S(1)} all-to-all(f32[16,8,256]{2,1,0:T(8,128)S(1)} %shard_map.108), channel_id=1, replica_groups=mesh['grp'=16,'voc'=16] {'grp'}, dimensions={0} | all-to-all | bytes 262144 | tf_op jit(solution)/shard_map/all_to_all | solution.py:499
  78.1 1.3 %shard_map.109 = (bf16[384,256]{1,0:T(8,128)(2,1)S(1)}, bf16[384,256]{1,0:T(8,128)(2,1)}, bf16[16,128,256]{2,1,0:T(8,128)(2,1)S(1)}, f32[1,256]{1,0:T(1,128)S(1)}, f32[1,1]{1,0:T(1,128)}) custom-call(f32[16,8,256]{2,1,0:T(8,128)S(1)} %all_to_all.26.stats, f32[8,256]{1,0:T(8,128)S(1)} %get-tuple-element.49.tops, f32[384,256]{1,0:T(8,128)S(1)} %get-tuple-element.50.exp_in, ...), custom_call_target="tpu_custom_call" | custom-call | flops 402653184 | bytes 4194304 | tf_op jit(solution)/shard_map/pallas_call | solution.py:609
  79.5 2.4 %shard_map.110 = (bf16[16,128,256]{2,1,0:T(8,128)(2,1)S(1)}, f32[56,256]{1,0:T(8,128)}, bf16[20,128,256]{2,1,0:T(8,128)(2,1)}) custom-call(bf16[4,288,256]{2,1,0:T(8,128)(2,1)S(1)} %maximum_add_fusion.far.refs_0_, bf16[4,288,256]{2,1,0:T(8,128)(2,1)S(1)} %collective-permute-done.10.other_a.refs_1_, ...), custom_call_target="tpu_custom_call" | custom-call | flops 402653184 | bytes 4194304 | tf_op jit(solution)/shard_map/pallas_call | solution.py:623
  82.3 19.3 %all_to_all.27.pieces = bf16[16,128,256]{2,1,0:T(8,128)(2,1)S(1)} all-to-all(bf16[16,128,256]{2,1,0:T(8,128)(2,1)S(1)} %shard_map.111), channel_id=1, replica_groups=mesh['grp'=16,'voc'=16] {'voc'}, dimensions={0} | all-to-all | bytes 2097152 | tf_op jit(solution)/shard_map/all_to_all | solution.py:499
  102.7 4.9 %all-to-all-start.4 = ((bf16[16,32,128]{2,1,0:T(8,128)(2,1)}), bf16[16,32,128]{2,1,0:T(8,128)(2,1)S(1)}, u32[]{:S(2)}, u32[]{:S(2)}) async-start(bf16[16,32,128]{2,1,0:T(8,128)(2,1)} %shard_map.112), calls=%async_computation.4 | async-start | bytes 262144 | tf_op jit(solution)/shard_map/all_to_all | solution.py:499
  107.6 5.1 %shard_map.114 = bf16[4096,384]{1,0:T(8,128)(2,1)} custom-call(bf16[12,128,256]{2,1,0:T(8,128)(2,1)} %get-tuple-element.63.near, bf16[20,128,256]{2,1,0:T(8,128)(2,1)} %get-tuple-element.64.rest, bf16[384,256]{1,0:T(8,128)(2,1)} %get-tuple-element.65.scaled_in), custom_call_target="tpu_custom_call" | custom-call | flops 805306368 | bytes 4194304 | tf_op jit(solution)/shard_map/pallas_call | solution.py:642
  112.8 4.1 %all-to-all-done.4.pieces_in = bf16[16,32,128]{2,1,0:T(8,128)(2,1)S(1)} async-done(((bf16[16,32,128]{2,1,0:T(8,128)(2,1)}), bf16[16,32,128]{2,1,0:T(8,128)(2,1)S(1)}, u32[]{:S(2)}, u32[]{:S(2)}) %all-to-all-start.4) | async-done | bytes 131104 | tf_op jit(solution)/shard_map/all_to_all | solution.py:499
  116.8 1.6 %shard_map.113 = (bf16[24,256]{1,0:T(8,128)(2,1)}, f32[1,256]{1,0:T(1,128)}) custom-call(bf16[16,32,128]{2,1,0:T(8,128)(2,1)S(1)} %all-to-all-done.4.pieces_in, f32[56,256]{1,0:T(8,128)} %get-tuple-element.60.base_in), custom_call_target="tpu_custom_call" | custom-call | tf_op jit(solution)/shard_map/pallas_call | solution.py:665
  (54 shorter events, 8.2 us)
Async XLA Ops:
  0.6 41.3 %copy-start = (bf16[4096,384]{1,0:T(8,128)(2,1)S(1)}, bf16[4096,384]{1,0:T(8,128)(2,1)}, u32[]{:S(2)}) copy-start(bf16[4096,384]{1,0:T(8,128)(2,1)} %refs_6_.1) | copy-start | bytes 9437188
  2.3 21.0 %all-to-all-start = ((bf16[16,56,128]{2,1,0:T(8,128)(2,1)}), bf16[16,56,128]{2,1,0:T(8,128)(2,1)S(1)}, u32[]{:S(2)}, u32[]{:S(2)}) async-start(bf16[16,56,128]{2,1,0:T(8,128)(2,1)} %shard_map.102), calls=%async_computation | async-start | bytes 458752 | tf_op jit(solution)/shard_map/all_to_all | solution.py:499
  23.7 6.5 %collective-permute-start.4 = (bf16[288,256]{1,0:T(8,128)(2,1)S(1)}, bf16[288,256]{1,0:T(8,128)(2,1)S(1)}, u32[]{:S(2)}, u32[]{:S(2)}) collective-permute-start(bf16[288,256]{1,0:T(8,128)(2,1)S(1)} %get-tuple-element.35.block), channel_id=1, source_target_pairs={{0,3},{1,0},{2,1},{3,2},{4,7},{5,4},{6,5},{7,6},{8,11},{9,8},{10,9... | collective-permute-start | bytes 442376 | tf_op jit(solution)/shard_map/ppermute | solution.py:544
  26.6 5.8 %collective-permute-start.3 = (bf16[288,256]{1,0:T(8,128)(2,1)S(1)}, bf16[288,256]{1,0:T(8,128)(2,1)S(1)}, u32[]{:S(2)}, u32[]{:S(2)}) collective-permute-start(bf16[288,256]{1,0:T(8,128)(2,1)S(1)} %get-tuple-element.35.block), channel_id=1, source_target_pairs={{0,2},{1,3},{2,0},{3,1},{4,6},{5,7},{6,4},{7,5},{8,10},{9,11},{10,... | collective-permute-start | bytes 442376 | tf_op jit(solution)/shard_map/ppermute | solution.py:545
  26.9 7.8 %collective-permute-start = (bf16[288,256]{1,0:T(8,128)(2,1)S(1)}, bf16[288,256]{1,0:T(8,128)(2,1)S(1)}, u32[]{:S(2)}, u32[]{:S(2)}) collective-permute-start(bf16[288,256]{1,0:T(8,128)(2,1)S(1)} %get-tuple-element.35.block), channel_id=1, source_target_pairs={{0,1},{1,2},{2,3},{3,0},{4,5},{5,6},{6,7},{7,4},{8,9},{9,10},{10,1... | collective-permute-start | bytes 442376 | tf_op jit(solution)/shard_map/ppermute | solution.py:543
  32.4 7.3 %collective-permute-start.5 = (bf16[2,288,256]{2,1,0:T(8,128)(2,1)S(1)}, bf16[2,288,256]{2,1,0:T(8,128)(2,1)S(1)}, u32[]{:S(2)}, u32[]{:S(2)}) collective-permute-start(bf16[2,288,256]{2,1,0:T(8,128)(2,1)S(1)} %pad_maximum_fusion.2), channel_id=1, source_target_pairs={{0,12},{1,13},{2,14},{3,15},{4,0},{5,1},{6,2},{7,3},{8,4},{9,5},{1... | collective-permute-start | bytes 884744 | tf_op jit(solution)/shard_map/ppermute | solution.py:549
  34.8 7.2 %collective-permute-start.1 = (bf16[2,288,256]{2,1,0:T(8,128)(2,1)S(1)}, bf16[2,288,256]{2,1,0:T(8,128)(2,1)S(1)}, u32[]{:S(2)}, u32[]{:S(2)}) collective-permute-start(bf16[2,288,256]{2,1,0:T(8,128)(2,1)S(1)} %pad_maximum_fusion.1), channel_id=1, source_target_pairs={{0,4},{1,5},{2,6},{3,7},{4,8},{5,9},{6,10},{7,11},{8,12},{9,13},{1... | collective-permute-start | bytes 884744 | tf_op jit(solution)/shard_map/ppermute | solution.py:548
  35.0 9.7 %collective-permute-start.8 = (bf16[2,288,256]{2,1,0:T(8,128)(2,1)S(1)}, bf16[2,288,256]{2,1,0:T(8,128)(2,1)S(1)}, u32[]{:S(2)}, u32[]{:S(2)}) collective-permute-start(bf16[2,288,256]{2,1,0:T(8,128)(2,1)S(1)} %pad_maximum_fusion.1), channel_id=1, source_target_pairs={{0,12},{1,13},{2,14},{3,15},{4,0},{5,1},{6,2},{7,3},{8,4},{9,5},{1... | collective-permute-start | bytes 884744 | tf_op jit(solution)/shard_map/ppermute | solution.py:551
  37.6 7.5 %collective-permute-start.7 = (bf16[2,288,256]{2,1,0:T(8,128)(2,1)S(1)}, bf16[2,288,256]{2,1,0:T(8,128)(2,1)S(1)}, u32[]{:S(2)}, u32[]{:S(2)}) collective-permute-start(bf16[2,288,256]{2,1,0:T(8,128)(2,1)S(1)} %pad_maximum_fusion.2), channel_id=1, source_target_pairs={{0,4},{1,5},{2,6},{3,7},{4,8},{5,9},{6,10},{7,11},{8,12},{9,13},{1... | collective-permute-start | bytes 884744 | tf_op jit(solution)/shard_map/ppermute | solution.py:550
  37.7 14.7 %collective-permute-start.10 = (bf16[4,288,256]{2,1,0:T(8,128)(2,1)S(1)}, bf16[4,288,256]{2,1,0:T(8,128)(2,1)S(1)}, u32[]{:S(2)}, u32[]{:S(2)}) collective-permute-start(bf16[4,288,256]{2,1,0:T(8,128)(2,1)S(1)} %pad_maximum_fusion.a), channel_id=1, source_target_pairs={{0,16},{16,0},{32,48},{48,32},{64,80},{80,64},{96,112},{112,96},{1... | collective-permute-start | bytes 1769480 | tf_op jit(solution)/shard_map/ppermute | solution.py:571
  39.7 9.7 %collective-permute-start.6 = (bf16[2,288,256]{2,1,0:T(8,128)(2,1)S(1)}, bf16[2,288,256]{2,1,0:T(8,128)(2,1)S(1)}, u32[]{:S(2)}, u32[]{:S(2)}) collective-permute-start(bf16[2,288,256]{2,1,0:T(8,128)(2,1)S(1)} %collective-permute-done.5.d_second), channel_id=1, source_target_pairs={{0,12},{1,13},{2,14},{3,15},{4,0},{5,1},{6,2},{7,3},{8,4},{9,5},{1... | collective-permute-start | bytes 884744 | tf_op jit(solution)/shard_map/ppermute | solution.py:553
  41.9 7.5 %collective-permute-start.2 = (bf16[2,288,256]{2,1,0:T(8,128)(2,1)S(1)}, bf16[2,288,256]{2,1,0:T(8,128)(2,1)S(1)}, u32[]{:S(2)}, u32[]{:S(2)}) collective-permute-start(bf16[2,288,256]{2,1,0:T(8,128)(2,1)S(1)} %collective-permute-done.1.u_first), channel_id=1, source_target_pairs={{0,4},{1,5},{2,6},{3,7},{4,8},{5,9},{6,10},{7,11},{8,12},{9,13},{1... | collective-permute-start | bytes 884744 | tf_op jit(solution)/shard_map/ppermute | solution.py:552
  45.2 7.2 %collective-permute-start.12 = (bf16[4,288,256]{2,1,0:T(8,128)(2,1)S(1)}, bf16[4,288,256]{2,1,0:T(8,128)(2,1)S(1)}, u32[]{:S(2)}, u32[]{:S(2)}) collective-permute-start(bf16[4,288,256]{2,1,0:T(8,128)(2,1)S(1)} %get-tuple-element.74), channel_id=1, source_target_pairs={{0,16},{16,0},{32,48},{48,32},{64,80},{80,64},{96,112},{112,96},{1... | collective-permute-start | bytes 1769480 | tf_op jit(solution)/shard_map/ppermute | solution.py:572
  47.7 4.7 %collective-permute-start.11 = (bf16[4,288,256]{2,1,0:T(8,128)(2,1)S(1)}, bf16[4,288,256]{2,1,0:T(8,128)(2,1)S(1)}, u32[]{:S(2)}, u32[]{:S(2)}) collective-permute-start(bf16[4,288,256]{2,1,0:T(8,128)(2,1)S(1)} %get-tuple-element.75), channel_id=1, source_target_pairs={{0,16},{16,0},{32,48},{48,32},{64,80},{80,64},{96,112},{112,96},{1... | collective-permute-start | bytes 1769480 | tf_op jit(solution)/shard_map/ppermute | solution.py:572
  49.5 4.5 %collective-permute-start.9 = (bf16[4,288,256]{2,1,0:T(8,128)(2,1)S(1)}, bf16[4,288,256]{2,1,0:T(8,128)(2,1)S(1)}, u32[]{:S(2)}, u32[]{:S(2)}) collective-permute-start(bf16[4,288,256]{2,1,0:T(8,128)(2,1)S(1)} %maximum_add_fusion.far.refs_0_), channel_id=1, source_target_pairs={{0,16},{16,0},{32,48},{48,32},{64,80},{80,64},{96,112},{112,96},{1... | collective-permute-start | bytes 1769480 | tf_op jit(solution)/shard_map/ppermute | solution.py:583
  54.8 24.6 %copy-start.1 = (bf16[24,256]{1,0:T(8,128)(2,1)S(1)}, bf16[24,256]{1,0:T(8,128)(2,1)}, u32[]{:S(2)}) copy-start(bf16[24,256]{1,0:T(8,128)(2,1)} %refs_7_.1) | copy-start | bytes 36868
  54.8 24.6 %copy-start.2 = (f32[256]{0:T(256)S(1)}, f32[256]{0:T(256)}, u32[]{:S(2)}) copy-start(f32[256]{0:T(256)} %param.8) | copy-start | bytes 3076
  79.4 2.7 %collective-permute-start.13 = (bf16[16,128,256]{2,1,0:T(8,128)(2,1)S(1)}, bf16[16,128,256]{2,1,0:T(8,128)(2,1)S(1)}, u32[]{:S(2)}, u32[]{:S(2)}) collective-permute-start(bf16[16,128,256]{2,1,0:T(8,128)(2,1)S(1)} %get-tuple-element.59), channel_id=1, source_target_pairs={{0,16},{16,0},{32,48},{48,32},{64,80},{80,64},{96,112},{112,96},{1... | collective-permute-start | bytes 3145736 | tf_op jit(solution)/shard_map/ppermute | solution.py:622
  102.7 14.2 %all-to-all-start.4 = ((bf16[16,32,128]{2,1,0:T(8,128)(2,1)}), bf16[16,32,128]{2,1,0:T(8,128)(2,1)S(1)}, u32[]{:S(2)}, u32[]{:S(2)}) async-start(bf16[16,32,128]{2,1,0:T(8,128)(2,1)} %shard_map.112), calls=%async_computation.4 | async-start | bytes 262144 | tf_op jit(solution)/shard_map/all_to_all | solution.py:499

commit v7 on v6

--- a/solution.py
+++ b/solution.py
@@ -459,15 +459,7 @@
         out[g] = result[g * SEND : (g + 1) * SEND]
 
 
-def finish_kernel(pieces_in, base_in, grad_hidden, grad_gain, pieces, base, sems):
-    copies = [
-        pltpu.make_async_copy(pieces_in, pieces, sems.at[0]),
-        pltpu.make_async_copy(base_in, base, sems.at[1]),
-    ]
-    for copy in copies:
-        copy.start()
-    for copy in copies:
-        copy.wait()
+def finish_kernel(pieces, base, grad_hidden, grad_gain):
     halves = []
     for c in range(2):
         summed = pieces[c].astype(F32)
@@ -624,7 +616,7 @@
         backward_two,
         out_shape=(
             half_rows,
-            pltpu.HBM((2 * ROWS + 8, LANES), F32),
+            shape((2 * ROWS + 8, LANES), F32),
             pltpu.HBM((5 * SIDE, HALF_S, LANES), BF),
         ),
         out_specs=(VMEM, VMEM, HBM),
@@ -665,14 +657,8 @@
     grad_hidden, grad_gain = pl.pallas_call(
         finish_kernel,
         out_shape=(shape((ROWS, 2 * HALF_S), BF), row),
-        in_specs=[ANY, HBM],
-        scratch_shapes=[
-            pltpu.VMEM((GROUPS, SEND, HALF_S), BF),
-            pltpu.VMEM((2 * ROWS + 8, LANES), F32),
-            pltpu.SemaphoreType.DMA((2,)),
-        ],
         compiler_params=params(4),
-    )(pieces, in_hbm(base))
+    )(pieces, base)
     return (loss.reshape(()), grad_hidden, grad_gain.reshape(-1), grad_head)
 
 

time: 119 us -> 118 us (level)
  Pallas kernels: 20.2 us -> 18.7 us
where the time goes in v7:
time: 118 us
  blocking collectives  42.5 us (36%)
  starting transfers between devices  33.5 us (28%)
  waiting for transfers between devices  18.9 us (16%)
  Pallas kernels  18.7 us (16%)
  other arithmetic  2.86 us (2%)
    all_to_all x3, blocking collectives, exchange(): return lax.all_to_all(x, axis, 0, 0, tiled=True)  42.5 us
    all_to_all x2, starting transfers between devices, exchange(): return lax.all_to_all(x, axis, 0, 0, tiled=True)  14.9 us
    all_to_all x2, waiting for transfers between devices, exchange(): return lax.all_to_all(x, axis, 0, 0, tiled=True)  12.5 us
    pallas_call x1, Pallas kernels, local(): pl.pallas_call(head_kernel, out_shape=shape((DS, VOC_DEV), BF), in_specs=...  5.12 us
    ppermute x1, starting transfers between devices, local(): other_far = lax.ppermute(far, 'grp', CORE_SWAP)  2.87 us
    ppermute x1, starting transfers between devices, local(): three = lax.ppermute(block, BOTH, ring(1, 3))  2.81 us
    ppermute x1, waiting for transfers between devices, local(): three = lax.ppermute(block, BOTH, ring(1, 3))  2.63 us
    pallas_call x1, Pallas kernels, local(): pl.pallas_call(forward_own, out_shape=partial + (pltpu.VMEM(teacher_head....  2.62 us
  transfers between devices with their start and end apart: 16, of which 8 were waited for; matrix products, arithmetic and copies ran while one was open for 3% of the time, Pallas kernels for 11%

profile of v7, /device:TPU:1, one launch (start us, length us, event | category | flops | bytes accessed | tf_op | source)
XLA Modules:
  0.0 117.5 jit_solution(15928154105639247190)
XLA Ops:
  0.6 1.7 %shard_map.102 = bf16[16,56,128]{2,1,0:T(8,128)(2,1)} custom-call(bf16[24,256]{1,0:T(8,128)(2,1)} %refs_7_.1, bf16[24,320]{1,0:T(8,128)(2,1)} %teacher_in.2), custom_call_target="tpu_custom_call" | custom-call | tf_op jit(solution)/shard_map/pallas_call | solution.py:508
  2.3 10.0 %all-to-all-start = ((bf16[16,56,128]{2,1,0:T(8,128)(2,1)}), bf16[16,56,128]{2,1,0:T(8,128)(2,1)S(1)}, u32[]{:S(2)}, u32[]{:S(2)}) async-start(bf16[16,56,128]{2,1,0:T(8,128)(2,1)} %shard_map.102), calls=%async_computation | async-start | bytes 458752 | tf_op jit(solution)/shard_map/all_to_all | solution.py:491
  15.0 8.4 %all-to-all-done.held = bf16[16,56,128]{2,1,0:T(8,128)(2,1)S(1)} async-done(((bf16[16,56,128]{2,1,0:T(8,128)(2,1)}), bf16[16,56,128]{2,1,0:T(8,128)(2,1)S(1)}, u32[]{:S(2)}, u32[]{:S(2)}) %all-to-all-start) | async-done | bytes 229408 | tf_op jit(solution)/shard_map/all_to_all | solution.py:491
  23.7 2.8 %collective-permute-start.4 = (bf16[288,256]{1,0:T(8,128)(2,1)S(1)}, bf16[288,256]{1,0:T(8,128)(2,1)S(1)}, u32[]{:S(2)}, u32[]{:S(2)}) collective-permute-start(bf16[288,256]{1,0:T(8,128)(2,1)S(1)} %get-tuple-element.35.block), channel_id=1, source_target_pairs={{0,3},{1,0},{2,1},{3,2},{4,7},{5,4},{6,5},{7,6},{8,11},{9,8},{10,9... | collective-permute-start | bytes 442376 | tf_op jit(solution)/shard_map/ppermute | solution.py:536
  27.6 2.6 %collective-permute-done.4 = bf16[288,256]{1,0:T(8,128)(2,1)S(1)} collective-permute-done((bf16[288,256]{1,0:T(8,128)(2,1)S(1)}, bf16[288,256]{1,0:T(8,128)(2,1)S(1)}, u32[]{:S(2)}, u32[]{:S(2)}) %collective-permute-start.4) | collective-permute-done | bytes 147488 | tf_op jit(solution)/shard_map/ppermute | solution.py:536
  30.2 2.1 %collective-permute-done.3 = bf16[288,256]{1,0:T(8,128)(2,1)S(1)} collective-permute-done((bf16[288,256]{1,0:T(8,128)(2,1)S(1)}, bf16[288,256]{1,0:T(8,128)(2,1)S(1)}, u32[]{:S(2)}, u32[]{:S(2)}) %collective-permute-start.3) | collective-permute-done | bytes 147488 | tf_op jit(solution)/shard_map/ppermute | solution.py:537
  32.4 2.4 %collective-permute-start.5 = (bf16[2,288,256]{2,1,0:T(8,128)(2,1)S(1)}, bf16[2,288,256]{2,1,0:T(8,128)(2,1)S(1)}, u32[]{:S(2)}, u32[]{:S(2)}) collective-permute-start(bf16[2,288,256]{2,1,0:T(8,128)(2,1)S(1)} %pad_maximum_fusion.2), channel_id=1, source_target_pairs={{0,12},{1,13},{2,14},{3,15},{4,0},{5,1},{6,2},{7,3},{8,4},{9,5},{1... | collective-permute-start | bytes 884744 | tf_op jit(solution)/shard_map/ppermute | solution.py:541
  35.0 2.6 %collective-permute-start.8 = (bf16[2,288,256]{2,1,0:T(8,128)(2,1)S(1)}, bf16[2,288,256]{2,1,0:T(8,128)(2,1)S(1)}, u32[]{:S(2)}, u32[]{:S(2)}) collective-permute-start(bf16[2,288,256]{2,1,0:T(8,128)(2,1)S(1)} %pad_maximum_fusion.1), channel_id=1, source_target_pairs={{0,12},{1,13},{2,14},{3,15},{4,0},{5,1},{6,2},{7,3},{8,4},{9,5},{1... | collective-permute-start | bytes 884744 | tf_op jit(solution)/shard_map/ppermute | solution.py:543
  37.7 2.0 %collective-permute-start.10 = (bf16[4,288,256]{2,1,0:T(8,128)(2,1)S(1)}, bf16[4,288,256]{2,1,0:T(8,128)(2,1)S(1)}, u32[]{:S(2)}, u32[]{:S(2)}) collective-permute-start(bf16[4,288,256]{2,1,0:T(8,128)(2,1)S(1)} %pad_maximum_fusion.a), channel_id=1, source_target_pairs={{0,16},{16,0},{32,48},{48,32},{64,80},{80,64},{96,112},{112,96},{1... | collective-permute-start | bytes 1769480 | tf_op jit(solution)/shard_map/ppermute | solution.py:563
  39.7 2.1 %collective-permute-start.6 = (bf16[2,288,256]{2,1,0:T(8,128)(2,1)S(1)}, bf16[2,288,256]{2,1,0:T(8,128)(2,1)S(1)}, u32[]{:S(2)}, u32[]{:S(2)}) collective-permute-start(bf16[2,288,256]{2,1,0:T(8,128)(2,1)S(1)} %collective-permute-done.5.d_second), channel_id=1, source_target_pairs={{0,12},{1,13},{2,14},{3,15},{4,0},{5,1},{6,2},{7,3},{8,4},{9,5},{1... | collective-permute-start | bytes 884744 | tf_op jit(solution)/shard_map/ppermute | solution.py:545
  41.9 2.6 %shard_map.104 = (f32[384,256]{1,0:T(8,128)S(1)}, f32[384,256]{1,0:T(8,128)S(1)}, f32[16,256]{1,0:T(8,128)S(1)}, bf16[5120,384]{1,0:T(8,128)(2,1)S(1)}, f32[1,256]{1,0:T(1,128)S(1)}) custom-call(bf16[4,288,256]{2,1,0:T(8,128)(2,1)S(1)} %pad_maximum_fusion.a, bf16[2,288,256]{2,1,0:T(8,128)(2,1)S(1)} %collective-permute-done.1.u_first, ...), custom_call_target="tpu_custom_call" | custom-call | flops 226492416 | bytes 4194304 | tf_op jit(solution)/shard_map/pallas_call | solution.py:554
  45.2 2.5 %collective-permute-start.12 = (bf16[4,288,256]{2,1,0:T(8,128)(2,1)S(1)}, bf16[4,288,256]{2,1,0:T(8,128)(2,1)S(1)}, u32[]{:S(2)}, u32[]{:S(2)}) collective-permute-start(bf16[4,288,256]{2,1,0:T(8,128)(2,1)S(1)} %get-tuple-element.74), channel_id=1, source_target_pairs={{0,16},{16,0},{32,48},{48,32},{64,80},{80,64},{96,112},{112,96},{1... | collective-permute-start | bytes 1769480 | tf_op jit(solution)/shard_map/ppermute | solution.py:564
  47.8 1.6 %shard_map.105 = (f32[384,256]{1,0:T(8,128)S(1)}, f32[384,256]{1,0:T(8,128)S(1)}, f32[16,256]{1,0:T(8,128)S(1)}, f32[1,256]{1,0:T(1,128)S(1)}, bf16[12,128,256]{2,1,0:T(8,128)(2,1)}) custom-call(bf16[4,288,256]{2,1,0:T(8,128)(2,1)S(1)} %pad_maximum_fusion.a, bf16[4,288,256]{2,1,0:T(8,128)(2,1)S(1)} %constant_dynamic-update-slice_fusion.u, ...), custom_call_target="tpu_custom_call" | custom-call | flops 452984832 | bytes 4194304 | tf_op jit(solution)/shard_map/pallas_call | solution.py:566
  49.5 2.9 %collective-permute-start.9 = (bf16[4,288,256]{2,1,0:T(8,128)(2,1)S(1)}, bf16[4,288,256]{2,1,0:T(8,128)(2,1)S(1)}, u32[]{:S(2)}, u32[]{:S(2)}) collective-permute-start(bf16[4,288,256]{2,1,0:T(8,128)(2,1)S(1)} %maximum_add_fusion.far.refs_0_), channel_id=1, source_target_pairs={{0,16},{16,0},{32,48},{48,32},{64,80},{80,64},{96,112},{112,96},{1... | collective-permute-start | bytes 1769480 | tf_op jit(solution)/shard_map/ppermute | solution.py:575
  52.4 1.3 %shard_map.106 = (f32[384,256]{1,0:T(8,128)S(1)}, f32[384,256]{1,0:T(8,128)S(1)}, f32[16,256]{1,0:T(8,128)S(1)}) custom-call(bf16[4,288,256]{2,1,0:T(8,128)(2,1)S(1)} %maximum_add_fusion.far.refs_0_, bf16[4,288,256]{2,1,0:T(8,128)(2,1)S(1)} %collective-permute-done.10.other_a.refs_1_, bf16[4,288,256]{2,1,0:T(8,128)(2,1)S(1)} %collective-permute-done.11.other_u.refs_2_, ...), custom_call_target="tpu_custom_call" | custom-call | flops 905969664 | bytes 4194304 | tf_op jit(solution)/shard_map/pallas_call | solution.py:576
  54.9 9.4 %all_to_all.25.stats = f32[16,8,256]{2,1,0:T(8,128)S(1)} all-to-all(f32[16,8,256]{2,1,0:T(8,128)S(1)} %get-tuple-element.48), channel_id=1, replica_groups=mesh['grp'=16,'voc'=16] {'voc'}, dimensions={0} | all-to-all | bytes 262144 | tf_op jit(solution)/shard_map/all_to_all | solution.py:491
  64.4 13.7 %all_to_all.26.stats = f32[16,8,256]{2,1,0:T(8,128)S(1)} all-to-all(f32[16,8,256]{2,1,0:T(8,128)S(1)} %shard_map.108), channel_id=1, replica_groups=mesh['grp'=16,'voc'=16] {'grp'}, dimensions={0} | all-to-all | bytes 262144 | tf_op jit(solution)/shard_map/all_to_all | solution.py:491
  78.1 1.3 %shard_map.109 = (bf16[384,256]{1,0:T(8,128)(2,1)S(1)}, bf16[384,256]{1,0:T(8,128)(2,1)}, bf16[16,128,256]{2,1,0:T(8,128)(2,1)S(1)}, f32[1,256]{1,0:T(1,128)S(1)}, f32[1,1]{1,0:T(1,128)}) custom-call(f32[16,8,256]{2,1,0:T(8,128)S(1)} %all_to_all.26.stats, f32[8,256]{1,0:T(8,128)S(1)} %get-tuple-element.49.tops, f32[384,256]{1,0:T(8,128)S(1)} %get-tuple-element.50.exp_in, ...), custom_call_target="tpu_custom_call" | custom-call | flops 402653184 | bytes 4194304 | tf_op jit(solution)/shard_map/pallas_call | solution.py:601
  79.5 1.8 %shard_map.110 = (bf16[16,128,256]{2,1,0:T(8,128)(2,1)S(1)}, f32[56,256]{1,0:T(8,128)S(1)}, bf16[20,128,256]{2,1,0:T(8,128)(2,1)}) custom-call(bf16[4,288,256]{2,1,0:T(8,128)(2,1)S(1)} %maximum_add_fusion.far.refs_0_, bf16[4,288,256]{2,1,0:T(8,128)(2,1)S(1)} %collective-permute-done.10.other_a.refs_1_, ...), custom_call_target="tpu_custom_call" | custom-call | flops 402653184 | bytes 4194304 | tf_op jit(solution)/shard_map/pallas_call | solution.py:615
  82.3 19.4 %all_to_all.27.pieces = bf16[16,128,256]{2,1,0:T(8,128)(2,1)S(1)} all-to-all(bf16[16,128,256]{2,1,0:T(8,128)(2,1)S(1)} %shard_map.111), channel_id=1, replica_groups=mesh['grp'=16,'voc'=16] {'voc'}, dimensions={0} | all-to-all | bytes 2097152 | tf_op jit(solution)/shard_map/all_to_all | solution.py:491
  101.7 1.1 shard_map.112
  102.8 4.9 %all-to-all-start.4 = ((bf16[16,32,128]{2,1,0:T(8,128)(2,1)}), bf16[16,32,128]{2,1,0:T(8,128)(2,1)S(1)}, u32[]{:S(2)}, u32[]{:S(2)}) async-start(bf16[16,32,128]{2,1,0:T(8,128)(2,1)} %shard_map.112), calls=%async_computation.4 | async-start | bytes 262144 | tf_op jit(solution)/shard_map/all_to_all | solution.py:491
  107.7 5.1 %shard_map.114 = bf16[4096,384]{1,0:T(8,128)(2,1)} custom-call(bf16[12,128,256]{2,1,0:T(8,128)(2,1)} %get-tuple-element.63.near, bf16[20,128,256]{2,1,0:T(8,128)(2,1)} %get-tuple-element.64.rest, bf16[384,256]{1,0:T(8,128)(2,1)} %get-tuple-element.65.scaled_in), custom_call_target="tpu_custom_call" | custom-call | flops 805306368 | bytes 4194304 | tf_op jit(solution)/shard_map/pallas_call | solution.py:634
  112.8 4.1 %all-to-all-done.4.pieces = bf16[16,32,128]{2,1,0:T(8,128)(2,1)S(1)} async-done(((bf16[16,32,128]{2,1,0:T(8,128)(2,1)}), bf16[16,32,128]{2,1,0:T(8,128)(2,1)S(1)}, u32[]{:S(2)}, u32[]{:S(2)}) %all-to-all-start.4) | async-done | bytes 131104 | tf_op jit(solution)/shard_map/all_to_all | solution.py:491
  (54 shorter events, 8.3 us)
Async XLA Ops:
  0.6 41.3 %copy-start = (bf16[4096,384]{1,0:T(8,128)(2,1)S(1)}, bf16[4096,384]{1,0:T(8,128)(2,1)}, u32[]{:S(2)}) copy-start(bf16[4096,384]{1,0:T(8,128)(2,1)} %refs_6_.1) | copy-start | bytes 9437188
  2.3 21.0 %all-to-all-start = ((bf16[16,56,128]{2,1,0:T(8,128)(2,1)}), bf16[16,56,128]{2,1,0:T(8,128)(2,1)S(1)}, u32[]{:S(2)}, u32[]{:S(2)}) async-start(bf16[16,56,128]{2,1,0:T(8,128)(2,1)} %shard_map.102), calls=%async_computation | async-start | bytes 458752 | tf_op jit(solution)/shard_map/all_to_all | solution.py:491
  23.7 6.5 %collective-permute-start.4 = (bf16[288,256]{1,0:T(8,128)(2,1)S(1)}, bf16[288,256]{1,0:T(8,128)(2,1)S(1)}, u32[]{:S(2)}, u32[]{:S(2)}) collective-permute-start(bf16[288,256]{1,0:T(8,128)(2,1)S(1)} %get-tuple-element.35.block), channel_id=1, source_target_pairs={{0,3},{1,0},{2,1},{3,2},{4,7},{5,4},{6,5},{7,6},{8,11},{9,8},{10,9... | collective-permute-start | bytes 442376 | tf_op jit(solution)/shard_map/ppermute | solution.py:536
  26.6 5.8 %collective-permute-start.3 = (bf16[288,256]{1,0:T(8,128)(2,1)S(1)}, bf16[288,256]{1,0:T(8,128)(2,1)S(1)}, u32[]{:S(2)}, u32[]{:S(2)}) collective-permute-start(bf16[288,256]{1,0:T(8,128)(2,1)S(1)} %get-tuple-element.35.block), channel_id=1, source_target_pairs={{0,2},{1,3},{2,0},{3,1},{4,6},{5,7},{6,4},{7,5},{8,10},{9,11},{10,... | collective-permute-start | bytes 442376 | tf_op jit(solution)/shard_map/ppermute | solution.py:537
  26.9 7.8 %collective-permute-start = (bf16[288,256]{1,0:T(8,128)(2,1)S(1)}, bf16[288,256]{1,0:T(8,128)(2,1)S(1)}, u32[]{:S(2)}, u32[]{:S(2)}) collective-permute-start(bf16[288,256]{1,0:T(8,128)(2,1)S(1)} %get-tuple-element.35.block), channel_id=1, source_target_pairs={{0,1},{1,2},{2,3},{3,0},{4,5},{5,6},{6,7},{7,4},{8,9},{9,10},{10,1... | collective-permute-start | bytes 442376 | tf_op jit(solution)/shard_map/ppermute | solution.py:535
  32.4 7.3 %collective-permute-start.5 = (bf16[2,288,256]{2,1,0:T(8,128)(2,1)S(1)}, bf16[2,288,256]{2,1,0:T(8,128)(2,1)S(1)}, u32[]{:S(2)}, u32[]{:S(2)}) collective-permute-start(bf16[2,288,256]{2,1,0:T(8,128)(2,1)S(1)} %pad_maximum_fusion.2), channel_id=1, source_target_pairs={{0,12},{1,13},{2,14},{3,15},{4,0},{5,1},{6,2},{7,3},{8,4},{9,5},{1... | collective-permute-start | bytes 884744 | tf_op jit(solution)/shard_map/ppermute | solution.py:541
  34.8 7.2 %collective-permute-start.1 = (bf16[2,288,256]{2,1,0:T(8,128)(2,1)S(1)}, bf16[2,288,256]{2,1,0:T(8,128)(2,1)S(1)}, u32[]{:S(2)}, u32[]{:S(2)}) collective-permute-start(bf16[2,288,256]{2,1,0:T(8,128)(2,1)S(1)} %pad_maximum_fusion.1), channel_id=1, source_target_pairs={{0,4},{1,5},{2,6},{3,7},{4,8},{5,9},{6,10},{7,11},{8,12},{9,13},{1... | collective-permute-start | bytes 884744 | tf_op jit(solution)/shard_map/ppermute | solution.py:540
  35.0 9.7 %collective-permute-start.8 = (bf16[2,288,256]{2,1,0:T(8,128)(2,1)S(1)}, bf16[2,288,256]{2,1,0:T(8,128)(2,1)S(1)}, u32[]{:S(2)}, u32[]{:S(2)}) collective-permute-start(bf16[2,288,256]{2,1,0:T(8,128)(2,1)S(1)} %pad_maximum_fusion.1), channel_id=1, source_target_pairs={{0,12},{1,13},{2,14},{3,15},{4,0},{5,1},{6,2},{7,3},{8,4},{9,5},{1... | collective-permute-start | bytes 884744 | tf_op jit(solution)/shard_map/ppermute | solution.py:543
  37.6 7.5 %collective-permute-start.7 = (bf16[2,288,256]{2,1,0:T(8,128)(2,1)S(1)}, bf16[2,288,256]{2,1,0:T(8,128)(2,1)S(1)}, u32[]{:S(2)}, u32[]{:S(2)}) collective-permute-start(bf16[2,288,256]{2,1,0:T(8,128)(2,1)S(1)} %pad_maximum_fusion.2), channel_id=1, source_target_pairs={{0,4},{1,5},{2,6},{3,7},{4,8},{5,9},{6,10},{7,11},{8,12},{9,13},{1... | collective-permute-start | bytes 884744 | tf_op jit(solution)/shard_map/ppermute | solution.py:542
  37.7 14.7 %collective-permute-start.10 = (bf16[4,288,256]{2,1,0:T(8,128)(2,1)S(1)}, bf16[4,288,256]{2,1,0:T(8,128)(2,1)S(1)}, u32[]{:S(2)}, u32[]{:S(2)}) collective-permute-start(bf16[4,288,256]{2,1,0:T(8,128)(2,1)S(1)} %pad_maximum_fusion.a), channel_id=1, source_target_pairs={{0,16},{16,0},{32,48},{48,32},{64,80},{80,64},{96,112},{112,96},{1... | collective-permute-start | bytes 1769480 | tf_op jit(solution)/shard_map/ppermute | solution.py:563
  39.7 9.7 %collective-permute-start.6 = (bf16[2,288,256]{2,1,0:T(8,128)(2,1)S(1)}, bf16[2,288,256]{2,1,0:T(8,128)(2,1)S(1)}, u32[]{:S(2)}, u32[]{:S(2)}) collective-permute-start(bf16[2,288,256]{2,1,0:T(8,128)(2,1)S(1)} %collective-permute-done.5.d_second), channel_id=1, source_target_pairs={{0,12},{1,13},{2,14},{3,15},{4,0},{5,1},{6,2},{7,3},{8,4},{9,5},{1... | collective-permute-start | bytes 884744 | tf_op jit(solution)/shard_map/ppermute | solution.py:545
  41.9 7.5 %collective-permute-start.2 = (bf16[2,288,256]{2,1,0:T(8,128)(2,1)S(1)}, bf16[2,288,256]{2,1,0:T(8,128)(2,1)S(1)}, u32[]{:S(2)}, u32[]{:S(2)}) collective-permute-start(bf16[2,288,256]{2,1,0:T(8,128)(2,1)S(1)} %collective-permute-done.1.u_first), channel_id=1, source_target_pairs={{0,4},{1,5},{2,6},{3,7},{4,8},{5,9},{6,10},{7,11},{8,12},{9,13},{1... | collective-permute-start | bytes 884744 | tf_op jit(solution)/shard_map/ppermute | solution.py:544
  45.2 7.2 %collective-permute-start.12 = (bf16[4,288,256]{2,1,0:T(8,128)(2,1)S(1)}, bf16[4,288,256]{2,1,0:T(8,128)(2,1)S(1)}, u32[]{:S(2)}, u32[]{:S(2)}) collective-permute-start(bf16[4,288,256]{2,1,0:T(8,128)(2,1)S(1)} %get-tuple-element.74), channel_id=1, source_target_pairs={{0,16},{16,0},{32,48},{48,32},{64,80},{80,64},{96,112},{112,96},{1... | collective-permute-start | bytes 1769480 | tf_op jit(solution)/shard_map/ppermute | solution.py:564
  47.7 4.7 %collective-permute-start.11 = (bf16[4,288,256]{2,1,0:T(8,128)(2,1)S(1)}, bf16[4,288,256]{2,1,0:T(8,128)(2,1)S(1)}, u32[]{:S(2)}, u32[]{:S(2)}) collective-permute-start(bf16[4,288,256]{2,1,0:T(8,128)(2,1)S(1)} %get-tuple-element.75), channel_id=1, source_target_pairs={{0,16},{16,0},{32,48},{48,32},{64,80},{80,64},{96,112},{112,96},{1... | collective-permute-start | bytes 1769480 | tf_op jit(solution)/shard_map/ppermute | solution.py:564
  49.5 4.5 %collective-permute-start.9 = (bf16[4,288,256]{2,1,0:T(8,128)(2,1)S(1)}, bf16[4,288,256]{2,1,0:T(8,128)(2,1)S(1)}, u32[]{:S(2)}, u32[]{:S(2)}) collective-permute-start(bf16[4,288,256]{2,1,0:T(8,128)(2,1)S(1)} %maximum_add_fusion.far.refs_0_), channel_id=1, source_target_pairs={{0,16},{16,0},{32,48},{48,32},{64,80},{80,64},{96,112},{112,96},{1... | collective-permute-start | bytes 1769480 | tf_op jit(solution)/shard_map/ppermute | solution.py:575
  54.8 24.6 %copy-start.1 = (bf16[24,256]{1,0:T(8,128)(2,1)S(1)}, bf16[24,256]{1,0:T(8,128)(2,1)}, u32[]{:S(2)}) copy-start(bf16[24,256]{1,0:T(8,128)(2,1)} %refs_7_.1) | copy-start | bytes 36868
  54.8 24.6 %copy-start.2 = (f32[256]{0:T(256)S(1)}, f32[256]{0:T(256)}, u32[]{:S(2)}) copy-start(f32[256]{0:T(256)} %param.8) | copy-start | bytes 3076
  79.4 2.7 %collective-permute-start.13 = (bf16[16,128,256]{2,1,0:T(8,128)(2,1)S(1)}, bf16[16,128,256]{2,1,0:T(8,128)(2,1)S(1)}, u32[]{:S(2)}, u32[]{:S(2)}) collective-permute-start(bf16[16,128,256]{2,1,0:T(8,128)(2,1)S(1)} %get-tuple-element.59), channel_id=1, source_target_pairs={{0,16},{16,0},{32,48},{48,32},{64,80},{80,64},{96,112},{112,96},{1... | collective-permute-start | bytes 3145736 | tf_op jit(solution)/shard_map/ppermute | solution.py:614
  102.8 14.1 %all-to-all-start.4 = ((bf16[16,32,128]{2,1,0:T(8,128)(2,1)}), bf16[16,32,128]{2,1,0:T(8,128)(2,1)S(1)}, u32[]{:S(2)}, u32[]{:S(2)}) async-start(bf16[16,32,128]{2,1,0:T(8,128)(2,1)} %shard_map.112), calls=%async_computation.4 | async-start | bytes 262144 | tf_op jit(solution)/shard_map/all_to_all | solution.py:491

commit v8 on v7

--- a/solution.py
+++ b/solution.py
@@ -48,33 +48,38 @@
 NN = (((1,), (0,)), ((), ()))
 
 
-def rounded(x):
-    return lax.reduce_precision(x, 8, 7)
-
-
 def dot(a, b, dims):
     return lax.dot_general(a, b, dims, preferred_element_type=F32)
 
 
-def lane_tables(episode_source, lengths):
-    episodes = lengths.shape[0]
-    two = (lengths == 2).astype(jnp.int32)
-    before = jnp.arange(episodes)[None, :] < jnp.arange(episodes)[:, None]
-    rank = jnp.sum(jnp.where(before, two[None, :], 0), axis=1)
-    lane = jnp.arange(LANES, dtype=jnp.int32)
-    number = jnp.arange(episodes, dtype=jnp.int32)
-    first = lane[None, :] == number[:, None]
-    second = (two[:, None] == 1) & (lane[None, :] == episodes + rank[:, None])
-    pick = first | second
-    position = (lane >= episodes).astype(jnp.int32)
+def lane_tables(source, lengths):
+    episodes = lengths.shape[1]
+    here = lax.broadcasted_iota(jnp.int32, (episodes, episodes), 0)
+    there = lane_iota((episodes, episodes))
+
+    def column(mask, values):
+        return jnp.sum(jnp.where(mask, values, 0.0), axis=1, keepdims=True)
+
+    lengths = lengths.astype(F32)
+    two = jnp.where(lengths == 2.0, 1.0, 0.0)
+    rank = column(there < here, two)
+    two = column(here == there, two)
+    source = column(here == there, source.astype(F32))
+    lengths = column(here == there, lengths)
+    lane = lane_iota((episodes, LANES)).astype(F32)
+    number = lax.broadcasted_iota(jnp.int32, (episodes, LANES), 0).astype(F32)
+    pick = (lane == number) | ((two == 1.0) & (lane == episodes + rank))
+
+    def of_lane(values):
+        return jnp.sum(jnp.where(pick, values, 0.0), axis=0, keepdims=True)
+
+    lane = lane_iota((1, LANES))
     inside = lane < VALID
-    episode = jnp.sum(jnp.where(pick, number[:, None], 0), axis=0)
-    source = jnp.sum(jnp.where(pick, episode_source[:, None], 0), axis=0)
-    length = jnp.sum(jnp.where(pick, lengths[:, None], 0), axis=0)
-    student_row = jnp.where(inside, episode * SEQ + position, -1)
-    teacher_row = jnp.where(inside, source * SEQ + position, -1)
-    weight = jnp.where(inside, 1.0 / jnp.maximum(length, 1).astype(F32), 0.0)
-    return student_row[None], teacher_row[None], weight[None]
+    position = jnp.where(lane >= episodes, 1.0, 0.0)
+    student_row = jnp.where(inside, of_lane(number) * SEQ + position, -1.0)
+    teacher_row = jnp.where(inside, of_lane(source) * SEQ + position, -1.0)
+    weight = jnp.where(inside, 1.0 / jnp.maximum(of_lane(lengths), 1.0), 0.0)
+    return student_row.astype(jnp.int32), teacher_row.astype(jnp.int32), weight
 
 
 def own_core():
@@ -85,15 +90,34 @@
     return lax.broadcasted_iota(jnp.int32, shape, len(shape) - 1)
 
 
-def pack_kernel(student_in, teacher_in, out, student, teacher, in_sems):
-    copies = [
-        pltpu.make_async_copy(student_in, student, in_sems.at[0]),
-        pltpu.make_async_copy(teacher_in, teacher, in_sems.at[1]),
-    ]
-    for copy in copies:
-        copy.start()
-    for copy in copies:
-        copy.wait()
+def pack_kernel(
+    student_in, teacher_in, source_in, lengths_in, gain_in,
+    out, student_row, teacher_row, weight, gain_out,
+    student, teacher, source, lengths, gain, sems,
+):
+    pairs = (
+        (source_in, source),
+        (lengths_in, lengths),
+        (gain_in, gain),
+        (student_in, student),
+        (teacher_in, teacher),
+    )
+    copies = []
+    for n, (place, held) in enumerate(pairs):
+        copies.append(pltpu.make_async_copy(place, held, sems.at[n]))
+        copies[n].start()
+    copies[0].wait()
+    copies[1].wait()
+    student_row[...], teacher_row[...], weight[...] = lane_tables(source[...], lengths[...])
+    copies[2].wait()
+    row = lax.broadcasted_iota(jnp.int32, (16, HALF_S), 0)
+    own_gain = jnp.where(own_core() == 0, gain[:, :HALF_S], gain[:, HALF_S:])
+    spread = jnp.zeros((16, HALF_S), F32)
+    for k, part in enumerate(split(own_gain, 3)):
+        spread = jnp.where(row == k, part.astype(F32), spread)
+    gain_out[...] = spread
+    copies[3].wait()
+    copies[4].wait()
     for c in range(2):
         rows = teacher[:, c * HALF_T : (c + 1) * HALF_T].astype(F32)
         tail = rows[:, HALF_S:]
@@ -127,9 +151,7 @@
     return out
 
 
-def compact_kernel(held, student_row, teacher_row, weight, gain, out, row_out, weight_out):
-    row_out[...] = student_row[...]
-    weight_out[...] = weight[...]
+def compact_kernel(held, student_row, teacher_row, gain, out):
     blocks = [held[g].astype(F32) for g in range(GROUPS)]
     rows_s = jnp.concatenate([block[:ROWS] for block in blocks], axis=0).astype(BF)
     rows_t = jnp.concatenate([block[ROWS : 2 * ROWS] for block in blocks], axis=0).astype(BF)
@@ -253,32 +275,17 @@
     squares_out[...] = squares
 
 
-def save_rows(refs, out, sems):
-    copies = []
-    for k, ref in enumerate(refs):
-        copies.append(
-            pltpu.make_async_copy(
-                ref.at[:, pl.ds(0, HALF_S)], out.at[pl.ds(k * SIDE, SIDE)], sems.at[k]
-            )
-        )
-        copies[k].start()
-    return copies
-
-
 def forward_near(
-    a, u, d, student_head, teacher_head, student_sum, teacher_sum, squares_sum,
-    student_out, teacher_out, squares_out, zero_out, rows_out, row_sems,
+    u, d, student_head, teacher_head, student_sum, teacher_sum, squares_sum,
+    student_out, teacher_out, squares_out, zero_out,
 ):
     core = own_core()
-    saved = save_rows((a, u, d), rows_out, row_sems)
     groups = batches((None, u, d), core)[1:]
     student, teacher, squares = logits_of(groups, student_head, teacher_head, core)
     student_out[...] = student + student_sum[...]
     teacher_out[...] = teacher + teacher_sum[...]
     squares_out[...] = squares + squares_sum[...]
     zero_out[...] = jnp.zeros((1, LANES), F32)
-    for copy in saved:
-        copy.wait()
 
 
 def forward_mid(
@@ -381,10 +388,9 @@
     terms_of(batches((None,) * 4, core), student_head, grad, core, away)
 
 
-def backward_two(*refs):
-    grad, student_head, hidden, gain, student_row, inverse, pull = refs[5:12]
-    stay, base_out, rows_out, sems = refs[12:]
-    saved = save_rows(refs[:5], rows_out, sems)
+def backward_two(
+    grad, student_head, hidden, gain, student_row, inverse, pull, stay, base_out
+):
     core = own_core()
     first = lax.axis_index("grp") * ROWS
     own = lax.broadcasted_iota(jnp.int32, (ROWS, LANES), 0) + first == student_row[...]
@@ -394,34 +400,17 @@
     base_out[ROWS : 2 * ROWS] = hidden[...].astype(F32) * own_pull
     base_out[2 * ROWS :] = jnp.broadcast_to(1.0 / gain[...], (8, LANES))
     terms_of(batches((None,) * 4, core), student_head, grad[...], core, stay)
-    for copy in saved:
-        copy.wait()
-
-
-def head_kernel(
-    near, rest, scaled_in, out, rows, scaled, blocks, in_sems, scaled_sem, sems
-):
-    first = pltpu.make_async_copy(scaled_in, scaled, scaled_sem)
-    first.start()
-    waiting = []
-    for n in range(2 * SIDE):
-        source, start = (near, n) if n < 3 else (rest, n - 3)
-        waiting.append(
-            pltpu.make_async_copy(
-                source.at[pl.ds(start * SIDE, SIDE)], rows.at[pl.ds(n * SIDE, SIDE)], in_sems.at[n]
-            )
-        )
-        waiting[n].start()
-    first.wait()
+
+
+def head_kernel(*refs):
+    scaled, out, zero_out, blocks, sems = refs[8:]
+    zero_out[...] = jnp.zeros((1, LANES), F32)
     copies = []
     for k, core in enumerate((own_core(), 1 - own_core())):
-        groups = batches((None,) * 4, core)
-        for j in range(SIDE):
-            m = k * SIDE + j
-            waiting[m].wait()
-            block = rows[pl.ds(m * SIDE, SIDE)].reshape(SIDE * HALF_S, LANES)
+        for group in batches(refs[SIDE * k : SIDE * k + SIDE], core):
+            block = jnp.concatenate([ref[j, :HALF_S, :] for ref, j, _ in group], axis=0)
             result = dot(block, scaled[...], NT).astype(BF)
-            for i, (_, _, v) in enumerate(groups[j]):
+            for i, (_, _, v) in enumerate(group):
                 n = len(copies)
                 blocks[n] = result[i * HALF_S : (i + 1) * HALF_S]
                 copies.append(
@@ -434,7 +423,7 @@
         copy.wait()
 
 
-def pair_kernel(stay, arrived, out):
+def pair_kernel(stay, arrived, zero, out):
     for v in range(VOC):
         out[v] = (stay[v].astype(F32) + arrived[v].astype(F32)).astype(BF)
 
@@ -499,38 +488,36 @@
 def local(
     student_hidden, norm_gain, teacher_hidden, student_head, teacher_head, episode_source, lengths
 ):
-    core = own_core()
     row = shape((1, LANES), F32)
     logits = shape((VOC_DEV, LANES), F32)
     half_rows = shape((VOC, HALF_S, LANES), BF)
-    student_row, teacher_row, weight = lane_tables(episode_source, lengths)
-
-    packed = pl.pallas_call(
+
+    table = shape((1, LANES), jnp.int32)
+    episodes = lengths.shape[0]
+    packed, student_row, teacher_row, weight, gain_parts = pl.pallas_call(
         pack_kernel,
-        out_shape=pltpu.HBM((GROUPS, PACK, HALF_S), BF),
-        in_specs=[HBM] * 2,
-        out_specs=VMEM,
+        out_shape=(
+            shape((GROUPS, PACK, HALF_S), BF), table, table, row, shape((16, HALF_S), F32)
+        ),
+        in_specs=[HBM] * 5,
+        out_specs=(VMEM,) * 5,
         scratch_shapes=[
             pltpu.VMEM((ROWS, 2 * HALF_S), BF),
             pltpu.VMEM((ROWS, 2 * HALF_T), BF),
-            pltpu.SemaphoreType.DMA((2,)),
+            pltpu.VMEM((1, episodes), jnp.int32),
+            pltpu.VMEM((1, episodes), jnp.int32),
+            pltpu.VMEM((1, 2 * HALF_S), F32),
+            pltpu.SemaphoreType.DMA((5,)),
         ],
         compiler_params=params(4),
-    )(in_hbm(student_hidden), in_hbm(teacher_hidden))
+    )(
+        in_hbm(student_hidden), in_hbm(teacher_hidden),
+        in_hbm(episode_source[None]), in_hbm(lengths[None]), in_hbm(norm_gain[None]),
+    )
     held = exchange(packed, "grp")
-
-    gain_half = lax.dynamic_slice_in_dim(norm_gain, core * HALF_S, HALF_S)
-    gain_high = rounded(gain_half)
-    gain_mid = rounded(gain_half - gain_high)
-    gain_low = gain_half - gain_high - gain_mid
-    gain_parts = jnp.concatenate(
-        [jnp.stack([gain_high, gain_mid, gain_low]), jnp.zeros((13, HALF_S), F32)], axis=0
-    )
-    block, student_row, weight = pl.pallas_call(
-        compact_kernel,
-        out_shape=(shape((HALF, LANES), BF), shape((1, LANES), jnp.int32), row),
-        compiler_params=params(8),
-    )(held, student_row, teacher_row, weight, gain_parts)
+    block = pl.pallas_call(
+        compact_kernel, out_shape=shape((HALF, LANES), BF), compiler_params=params(8)
+    )(held, student_row, teacher_row, gain_parts)
 
     one = lax.ppermute(block, BOTH, ring(1, 1))
     three = lax.ppermute(block, BOTH, ring(1, 3))
@@ -563,14 +550,12 @@
     other = (lax.ppermute(a, "grp", CORE_SWAP),) + tuple(
         lax.ppermute(part + zero.astype(BF), "grp", CORE_SWAP) for part in (u, d)
     )
-    *sums, zero, saved_near = pl.pallas_call(
+    *sums, zero = pl.pallas_call(
         forward_near,
-        out_shape=partial + (row, pltpu.HBM((3 * SIDE, HALF_S, LANES), BF)),
-        out_specs=(VMEM,) * 4 + (HBM,),
-        scratch_shapes=[sems(3)],
+        out_shape=partial + (row,),
         compiler_params=params(12),
         cost_estimate=cost(2 * SIDE * HALF * VOC_DEV * LANES * 2),
-    )(a, u, d, student_head, head_t, *sums)
+    )(u, d, student_head, head_t, *sums)
     far = jnp.concatenate([v, w], axis=0) + zero.astype(BF)
     other_far = lax.ppermute(far, "grp", CORE_SWAP)
     sums = pl.pallas_call(
@@ -602,7 +587,7 @@
         backward_one,
         out_shape=(
             shape((VOC_DEV, LANES), BF),
-            pltpu.HBM((VOC_DEV, LANES), BF),
+            shape((VOC_DEV, LANES), BF),
             half_rows,
             row,
             shape((1, 1), F32),
@@ -612,45 +597,27 @@
         cost_estimate=cost(DS * VOC_DEV * LANES),
     )(from_grp, tops, exp_s, ratio, weight, inverse, student_head)
     arrived = lax.ppermute(away, "grp", CORE_SWAP)
-    stay, base, saved_rest = pl.pallas_call(
+    stay, base = pl.pallas_call(
         backward_two,
-        out_shape=(
-            half_rows,
-            shape((2 * ROWS + 8, LANES), F32),
-            pltpu.HBM((5 * SIDE, HALF_S, LANES), BF),
-        ),
-        out_specs=(VMEM, VMEM, HBM),
-        scratch_shapes=[sems(5)],
+        out_shape=(half_rows, shape((2 * ROWS + 8, LANES), F32)),
         compiler_params=params(8),
         cost_estimate=cost(DS * VOC_DEV * LANES),
-    )(
-        far, *other, other_far, grad, student_head,
-        student_hidden, norm_gain[None], student_row, inverse, pull,
-    )
-    pair = pl.pallas_call(pair_kernel, out_shape=half_rows, compiler_params=params(8))(
-        stay, arrived
-    )
-    pieces = exchange(pair, "voc")
-    grad_head = pl.pallas_call(
+    )(grad, student_head, student_hidden, norm_gain[None], student_row, inverse, pull)
+    grad_head, zero = pl.pallas_call(
         head_kernel,
-        out_shape=shape((DS, VOC_DEV), BF),
-        in_specs=[HBM] * 3,
-        out_specs=HBM,
-        scratch_shapes=[
-            pltpu.VMEM((2 * VOC, HALF_S, LANES), BF),
-            pltpu.VMEM((VOC_DEV, LANES), BF),
-            pltpu.VMEM((2 * VOC, HALF_S, VOC_DEV), BF),
-            pltpu.SemaphoreType.DMA((2 * SIDE,)),
-            pltpu.SemaphoreType.DMA,
-            pltpu.SemaphoreType.DMA((2 * VOC,)),
-        ],
+        out_shape=(shape((DS, VOC_DEV), BF), row),
+        out_specs=(HBM, VMEM),
+        scratch_shapes=[pltpu.VMEM((2 * VOC, HALF_S, VOC_DEV), BF), sems(2 * VOC)],
         compiler_params=params(12),
         cost_estimate=cost(DS * VOC_DEV * LANES * 2),
-    )(in_hbm(saved_near), in_hbm(saved_rest), in_hbm(scaled))
+    )(a, u, d, far, *other, other_far, scaled)
+    pair = pl.pallas_call(pair_kernel, out_shape=half_rows, compiler_params=params(8))(
+        stay, arrived, zero
+    )
+    pieces = exchange(pair, "voc")
     outgoing = pl.pallas_call(
         send_kernel,
-        out_shape=pltpu.HBM((GROUPS, SEND, HALF_S), BF),
-        out_specs=VMEM,
+        out_shape=shape((GROUPS, SEND, HALF_S), BF),
         compiler_params=params(8),
     )(pieces, student_row, block, inverse)
     pieces = exchange(outgoing, "grp")

time: 118 us -> 116 us (0.983)
  blocking collectives: 42.5 us -> 76.5 us
  starting transfers between devices: 33.5 us -> 19.1 us
  waiting for transfers between devices: 18.9 us -> 6.05 us
  Pallas kernels: 18.7 us -> 12.7 us
  other arithmetic: 2.86 us -> 0.31 us
    all_to_all x3 -> x5, blocking collectives: 42.5 us -> 76.5 us  [exchange(): return lax.all_to_all(x, axis, 0, 0, tiled=True)]
    all_to_all x2 -> x0, starting transfers between devices: 14.9 us -> none  [exchange(): return lax.all_to_all(x, axis, 0, 0, tiled=True)]
    all_to_all x2 -> x0, waiting for transfers between devices: 12.5 us -> none  [exchange(): return lax.all_to_all(x, axis, 0, 0, tiled=True)]
    pallas_call x6, Pallas kernels: 11.1 us -> 6.27 us  [the longest x1 2.21 us: local(): pl.pallas_call(head_kernel, out_shape=(shape((DS, VOC_DEV), BF), row), ou...]
  transfers between devices with their start and end apart: 16 -> 14, of which waited for: 8 -> 6; matrix products, arithmetic and copies ran while one was open for 3% -> 0% of each run, Pallas kernels for 11% -> 7%
where the time goes in v8:
time: 116 us
  blocking collectives  76.5 us (66%)
  starting transfers between devices  19.1 us (16%)
  Pallas kernels  12.7 us (11%)
  waiting for transfers between devices  6.05 us (5%)
    all_to_all x5, blocking collectives, exchange(): return lax.all_to_all(x, axis, 0, 0, tiled=True)  76.5 us
    ppermute x1, starting transfers between devices, local(): other_far = lax.ppermute(far, 'grp', CORE_SWAP)  3.3 us
    ppermute x1, starting transfers between devices, local(): three = lax.ppermute(block, BOTH, ring(1, 3))  2.81 us
    ppermute x1, waiting for transfers between devices, local(): three = lax.ppermute(block, BOTH, ring(1, 3))  2.63 us
    pallas_call x1, Pallas kernels, local(): pl.pallas_call(forward_own, out_shape=partial + (pltpu.VMEM(teacher_head....  2.62 us
    ppermute x2, starting transfers between devices, local(): lax.ppermute(part + zero.astype(BF), 'grp', CORE_SWAP)  2.6 us
    ppermute x1, starting transfers between devices, local(): d_first = lax.ppermute(first, BOTH, ring(2, 3))  2.58 us
    ppermute x1, starting transfers between devices, local(): d_second = lax.ppermute(second, BOTH, ring(2, 3))  2.36 us
  transfers between devices with their start and end apart: 14, of which 6 were waited for; matrix products, arithmetic and copies ran while one was open for 0% of the time, Pallas kernels for 7%

profile of v8, /device:TPU:1, one launch (start us, length us, event | category | flops | bytes accessed | tf_op | source)
XLA Modules:
  0.0 115.6 jit_solution(15784907437064750268)
XLA Ops:
  0.6 1.2 %shard_map.102 = (bf16[16,56,128]{2,1,0:T(8,128)(2,1)S(1)}, s32[1,256]{1,0:T(1,128)S(1)}, s32[1,256]{1,0:T(1,128)S(1)}, f32[1,256]{1,0:T(1,128)S(1)}, f32[16,128]{1,0:T(8,128)S(1)}) custom-call(bf16[24,256]{1,0:T(8,128)(2,1)} %hidden.1, bf16[24,320]{1,0:T(8,128)(2,1)} %teacher_in.2, s32[1,192]{1,0:T(1,128)} %bitcast.19, s32[1,192]{1,0:T(1,128)} %bitcast.20, ...), custom_call_target="tpu_custom_call" | custom-call | tf_op jit(solution)/shard_map/pallas_call | solution.py:497
  1.8 20.8 %all_to_all.25.held = bf16[16,56,128]{2,1,0:T(8,128)(2,1)S(1)} all-to-all(bf16[16,56,128]{2,1,0:T(8,128)(2,1)S(1)} %get-tuple-element.37), channel_id=1, replica_groups=mesh['grp'=16,'voc'=16] {'grp'}, dimensions={0} | all-to-all | bytes 458752 | tf_op jit(solution)/shard_map/all_to_all | solution.py:480
  23.0 2.8 %collective-permute-start.4 = (bf16[288,256]{1,0:T(8,128)(2,1)S(1)}, bf16[288,256]{1,0:T(8,128)(2,1)S(1)}, u32[]{:S(2)}, u32[]{:S(2)}) collective-permute-start(bf16[288,256]{1,0:T(8,128)(2,1)S(1)} %shard_map.103.block), channel_id=1, source_target_pairs={{0,3},{1,0},{2,1},{3,2},{4,7},{5,4},{6,5},{7,6},{8,11},{9,8},{10,9... | collective-permute-start | bytes 442376 | tf_op jit(solution)/shard_map/ppermute | solution.py:523
  26.2 0.7 collective-permute-start
  26.9 2.6 %collective-permute-done.4 = bf16[288,256]{1,0:T(8,128)(2,1)S(1)} collective-permute-done((bf16[288,256]{1,0:T(8,128)(2,1)S(1)}, bf16[288,256]{1,0:T(8,128)(2,1)S(1)}, u32[]{:S(2)}, u32[]{:S(2)}) %collective-permute-start.4) | collective-permute-done | bytes 147488 | tf_op jit(solution)/shard_map/ppermute | solution.py:523
  29.5 2.1 %collective-permute-done.3 = bf16[288,256]{1,0:T(8,128)(2,1)S(1)} collective-permute-done((bf16[288,256]{1,0:T(8,128)(2,1)S(1)}, bf16[288,256]{1,0:T(8,128)(2,1)S(1)}, u32[]{:S(2)}, u32[]{:S(2)}) %collective-permute-start.3) | collective-permute-done | bytes 147488 | tf_op jit(solution)/shard_map/ppermute | solution.py:524
  31.7 2.4 %collective-permute-start.5 = (bf16[2,288,256]{2,1,0:T(8,128)(2,1)S(1)}, bf16[2,288,256]{2,1,0:T(8,128)(2,1)S(1)}, u32[]{:S(2)}, u32[]{:S(2)}) collective-permute-start(bf16[2,288,256]{2,1,0:T(8,128)(2,1)S(1)} %pad_maximum_fusion.2), channel_id=1, source_target_pairs={{0,12},{1,13},{2,14},{3,15},{4,0},{5,1},{6,2},{7,3},{8,4},{9,5},{1... | collective-permute-start | bytes 884744 | tf_op jit(solution)/shard_map/ppermute | solution.py:528
  34.3 2.6 %collective-permute-start.8 = (bf16[2,288,256]{2,1,0:T(8,128)(2,1)S(1)}, bf16[2,288,256]{2,1,0:T(8,128)(2,1)S(1)}, u32[]{:S(2)}, u32[]{:S(2)}) collective-permute-start(bf16[2,288,256]{2,1,0:T(8,128)(2,1)S(1)} %pad_maximum_fusion.1), channel_id=1, source_target_pairs={{0,12},{1,13},{2,14},{3,15},{4,0},{5,1},{6,2},{7,3},{8,4},{9,5},{1... | collective-permute-start | bytes 884744 | tf_op jit(solution)/shard_map/ppermute | solution.py:530
  37.0 2.0 %collective-permute-start.10 = (bf16[4,288,256]{2,1,0:T(8,128)(2,1)S(1)}, bf16[4,288,256]{2,1,0:T(8,128)(2,1)S(1)}, u32[]{:S(2)}, u32[]{:S(2)}) collective-permute-start(bf16[4,288,256]{2,1,0:T(8,128)(2,1)S(1)} %pad_maximum_fusion.a.refs_0_), channel_id=1, source_target_pairs={{0,16},{16,0},{32,48},{48,32},{64,80},{80,64},{96,112},{112,96},{1... | collective-permute-start | bytes 1769480 | tf_op jit(solution)/shard_map/ppermute | solution.py:550
  39.0 2.1 %collective-permute-start.6 = (bf16[2,288,256]{2,1,0:T(8,128)(2,1)S(1)}, bf16[2,288,256]{2,1,0:T(8,128)(2,1)S(1)}, u32[]{:S(2)}, u32[]{:S(2)}) collective-permute-start(bf16[2,288,256]{2,1,0:T(8,128)(2,1)S(1)} %collective-permute-done.5.d_second), channel_id=1, source_target_pairs={{0,12},{1,13},{2,14},{3,15},{4,0},{5,1},{6,2},{7,3},{8,4},{9,5},{1... | collective-permute-start | bytes 884744 | tf_op jit(solution)/shard_map/ppermute | solution.py:532
  41.2 2.6 %shard_map.104 = (f32[384,256]{1,0:T(8,128)S(1)}, f32[384,256]{1,0:T(8,128)S(1)}, f32[16,256]{1,0:T(8,128)S(1)}, bf16[5120,384]{1,0:T(8,128)(2,1)S(1)}, f32[1,256]{1,0:T(1,128)S(1)}) custom-call(bf16[4,288,256]{2,1,0:T(8,128)(2,1)S(1)} %pad_maximum_fusion.a.refs_0_, bf16[2,288,256]{2,1,0:T(8,128)(2,1)S(1)} %collective-permute-done.1.u_first, ...), custom_call_target="tpu_custom_call" | custom-call | flops 226492416 | bytes 4194304 | tf_op jit(solution)/shard_map/pallas_call | solution.py:541
  44.5 2.5 %collective-permute-start.12 = (bf16[4,288,256]{2,1,0:T(8,128)(2,1)S(1)}, bf16[4,288,256]{2,1,0:T(8,128)(2,1)S(1)}, u32[]{:S(2)}, u32[]{:S(2)}) collective-permute-start(bf16[4,288,256]{2,1,0:T(8,128)(2,1)S(1)} %get-tuple-element.70), channel_id=1, source_target_pairs={{0,16},{16,0},{32,48},{48,32},{64,80},{80,64},{96,112},{112,96},{1... | collective-permute-start | bytes 1769480 | tf_op jit(solution)/shard_map/ppermute | solution.py:551
  47.1 0.8 shard_map.105
  48.4 3.3 %collective-permute-start.9 = (bf16[4,288,256]{2,1,0:T(8,128)(2,1)S(1)}, bf16[4,288,256]{2,1,0:T(8,128)(2,1)S(1)}, u32[]{:S(2)}, u32[]{:S(2)}) collective-permute-start(bf16[4,288,256]{2,1,0:T(8,128)(2,1)S(1)} %maximum_add_fusion.far.refs_3_), channel_id=1, source_target_pairs={{0,16},{16,0},{32,48},{48,32},{64,80},{80,64},{96,112},{112,96},{1... | collective-permute-start | bytes 1769480 | tf_op jit(solution)/shard_map/ppermute | solution.py:560
  51.7 1.3 %shard_map.106 = (f32[384,256]{1,0:T(8,128)S(1)}, f32[384,256]{1,0:T(8,128)S(1)}, f32[16,256]{1,0:T(8,128)S(1)}) custom-call(bf16[4,288,256]{2,1,0:T(8,128)(2,1)S(1)} %maximum_add_fusion.far.refs_3_, bf16[4,288,256]{2,1,0:T(8,128)(2,1)S(1)} %collective-permute-done.10.other_a.refs_4_, bf16[4,288,256]{2,1,0:T(8,128)(2,1)S(1)} %collective-permute-done.11.other_u.refs_5_, ...), custom_call_target="tpu_custom_call" | custom-call | flops 905969664 | bytes 4194304 | tf_op jit(solution)/shard_map/pallas_call | solution.py:561
  53.3 0.8 shard_map.107
  54.1 9.4 %all_to_all.26.stats = f32[16,8,256]{2,1,0:T(8,128)S(1)} all-to-all(f32[16,8,256]{2,1,0:T(8,128)S(1)} %get-tuple-element.53), channel_id=1, replica_groups=mesh['grp'=16,'voc'=16] {'voc'}, dimensions={0} | all-to-all | bytes 262144 | tf_op jit(solution)/shard_map/all_to_all | solution.py:480
  63.7 13.7 %all_to_all.27.stats = f32[16,8,256]{2,1,0:T(8,128)S(1)} all-to-all(f32[16,8,256]{2,1,0:T(8,128)S(1)} %shard_map.108), channel_id=1, replica_groups=mesh['grp'=16,'voc'=16] {'grp'}, dimensions={0} | all-to-all | bytes 262144 | tf_op jit(solution)/shard_map/all_to_all | solution.py:480
  77.4 1.3 %shard_map.109 = (bf16[384,256]{1,0:T(8,128)(2,1)S(1)}, bf16[384,256]{1,0:T(8,128)(2,1)S(1)}, bf16[16,128,256]{2,1,0:T(8,128)(2,1)S(1)}, f32[1,256]{1,0:T(1,128)S(1)}, f32[1,1]{1,0:T(1,128)}) custom-call(f32[16,8,256]{2,1,0:T(8,128)S(1)} %all_to_all.27.stats, f32[8,256]{1,0:T(8,128)S(1)} %get-tuple-element.54.tops, f32[384,256]{1,0:T(8,128)S(1)} %get-tuple-element.55.exp_in, ...), custom_call_target="tpu_custom_call" | custom-call | flops 402653184 | bytes 4194304 | tf_op jit(solution)/shard_map/pallas_call | solution.py:586
  78.7 0.7 shard_map.110
  79.5 2.2 %shard_map.111 = (bf16[4096,384]{1,0:T(8,128)(2,1)}, f32[1,256]{1,0:T(1,128)S(1)}) custom-call(bf16[4,288,256]{2,1,0:T(8,128)(2,1)S(1)} %pad_maximum_fusion.a.refs_0_, bf16[4,288,256]{2,1,0:T(8,128)(2,1)S(1)} %constant_dynamic-update-slice_fusion.u.refs_1_, bf16[4,288,256]{2,1,0:T(8,128)(2,1)S(1)} %constant_dynamic-update-slice_fusion.2.d.refs_2_, ...), custom_call_target="tpu_custom_call" | custom-call | flops 805306368 | bytes 4194304 | tf_op jit(solution)/shard_map/pallas_call | solution.py:606
  82.0 19.0 %all_to_all.28.pieces = bf16[16,128,256]{2,1,0:T(8,128)(2,1)S(1)} all-to-all(bf16[16,128,256]{2,1,0:T(8,128)(2,1)S(1)} %shard_map.112), channel_id=1, replica_groups=mesh['grp'=16,'voc'=16] {'voc'}, dimensions={0} | all-to-all | bytes 2097152 | tf_op jit(solution)/shard_map/all_to_all | solution.py:480
  101.4 13.6 %all_to_all.29.pieces = bf16[16,32,128]{2,1,0:T(8,128)(2,1)S(1)} all-to-all(bf16[16,32,128]{2,1,0:T(8,128)(2,1)S(1)} %shard_map.113), channel_id=1, replica_groups=mesh['grp'=16,'voc'=16] {'grp'}, dimensions={0} | all-to-all | bytes 262144 | tf_op jit(solution)/shard_map/all_to_all | solution.py:480
  115.0 0.6 shard_map.114
  (39 shorter events, 3.6 us)
Async XLA Ops:
  0.6 40.6 %copy-start = (bf16[4096,384]{1,0:T(8,128)(2,1)S(1)}, bf16[4096,384]{1,0:T(8,128)(2,1)}, u32[]{:S(2)}) copy-start(bf16[4096,384]{1,0:T(8,128)(2,1)} %student_head.11) | copy-start | bytes 9437188
  23.0 6.5 %collective-permute-start.4 = (bf16[288,256]{1,0:T(8,128)(2,1)S(1)}, bf16[288,256]{1,0:T(8,128)(2,1)S(1)}, u32[]{:S(2)}, u32[]{:S(2)}) collective-permute-start(bf16[288,256]{1,0:T(8,128)(2,1)S(1)} %shard_map.103.block), channel_id=1, source_target_pairs={{0,3},{1,0},{2,1},{3,2},{4,7},{5,4},{6,5},{7,6},{8,11},{9,8},{10,9... | collective-permute-start | bytes 442376 | tf_op jit(solution)/shard_map/ppermute | solution.py:523
  25.9 5.8 %collective-permute-start.3 = (bf16[288,256]{1,0:T(8,128)(2,1)S(1)}, bf16[288,256]{1,0:T(8,128)(2,1)S(1)}, u32[]{:S(2)}, u32[]{:S(2)}) collective-permute-start(bf16[288,256]{1,0:T(8,128)(2,1)S(1)} %shard_map.103.block), channel_id=1, source_target_pairs={{0,2},{1,3},{2,0},{3,1},{4,6},{5,7},{6,4},{7,5},{8,10},{9,11},{10,... | collective-permute-start | bytes 442376 | tf_op jit(solution)/shard_map/ppermute | solution.py:524
  26.2 7.8 %collective-permute-start = (bf16[288,256]{1,0:T(8,128)(2,1)S(1)}, bf16[288,256]{1,0:T(8,128)(2,1)S(1)}, u32[]{:S(2)}, u32[]{:S(2)}) collective-permute-start(bf16[288,256]{1,0:T(8,128)(2,1)S(1)} %shard_map.103.block), channel_id=1, source_target_pairs={{0,1},{1,2},{2,3},{3,0},{4,5},{5,6},{6,7},{7,4},{8,9},{9,10},{10,1... | collective-permute-start | bytes 442376 | tf_op jit(solution)/shard_map/ppermute | solution.py:522
  31.7 7.3 %collective-permute-start.5 = (bf16[2,288,256]{2,1,0:T(8,128)(2,1)S(1)}, bf16[2,288,256]{2,1,0:T(8,128)(2,1)S(1)}, u32[]{:S(2)}, u32[]{:S(2)}) collective-permute-start(bf16[2,288,256]{2,1,0:T(8,128)(2,1)S(1)} %pad_maximum_fusion.2), channel_id=1, source_target_pairs={{0,12},{1,13},{2,14},{3,15},{4,0},{5,1},{6,2},{7,3},{8,4},{9,5},{1... | collective-permute-start | bytes 884744 | tf_op jit(solution)/shard_map/ppermute | solution.py:528
  34.1 7.2 %collective-permute-start.1 = (bf16[2,288,256]{2,1,0:T(8,128)(2,1)S(1)}, bf16[2,288,256]{2,1,0:T(8,128)(2,1)S(1)}, u32[]{:S(2)}, u32[]{:S(2)}) collective-permute-start(bf16[2,288,256]{2,1,0:T(8,128)(2,1)S(1)} %pad_maximum_fusion.1), channel_id=1, source_target_pairs={{0,4},{1,5},{2,6},{3,7},{4,8},{5,9},{6,10},{7,11},{8,12},{9,13},{1... | collective-permute-start | bytes 884744 | tf_op jit(solution)/shard_map/ppermute | solution.py:527
  34.3 9.7 %collective-permute-start.8 = (bf16[2,288,256]{2,1,0:T(8,128)(2,1)S(1)}, bf16[2,288,256]{2,1,0:T(8,128)(2,1)S(1)}, u32[]{:S(2)}, u32[]{:S(2)}) collective-permute-start(bf16[2,288,256]{2,1,0:T(8,128)(2,1)S(1)} %pad_maximum_fusion.1), channel_id=1, source_target_pairs={{0,12},{1,13},{2,14},{3,15},{4,0},{5,1},{6,2},{7,3},{8,4},{9,5},{1... | collective-permute-start | bytes 884744 | tf_op jit(solution)/shard_map/ppermute | solution.py:530
  36.9 7.5 %collective-permute-start.7 = (bf16[2,288,256]{2,1,0:T(8,128)(2,1)S(1)}, bf16[2,288,256]{2,1,0:T(8,128)(2,1)S(1)}, u32[]{:S(2)}, u32[]{:S(2)}) collective-permute-start(bf16[2,288,256]{2,1,0:T(8,128)(2,1)S(1)} %pad_maximum_fusion.2), channel_id=1, source_target_pairs={{0,4},{1,5},{2,6},{3,7},{4,8},{5,9},{6,10},{7,11},{8,12},{9,13},{1... | collective-permute-start | bytes 884744 | tf_op jit(solution)/shard_map/ppermute | solution.py:529
  37.0 14.7 %collective-permute-start.10 = (bf16[4,288,256]{2,1,0:T(8,128)(2,1)S(1)}, bf16[4,288,256]{2,1,0:T(8,128)(2,1)S(1)}, u32[]{:S(2)}, u32[]{:S(2)}) collective-permute-start(bf16[4,288,256]{2,1,0:T(8,128)(2,1)S(1)} %pad_maximum_fusion.a.refs_0_), channel_id=1, source_target_pairs={{0,16},{16,0},{32,48},{48,32},{64,80},{80,64},{96,112},{112,96},{1... | collective-permute-start | bytes 1769480 | tf_op jit(solution)/shard_map/ppermute | solution.py:550
  39.0 8.9 %collective-permute-start.6 = (bf16[2,288,256]{2,1,0:T(8,128)(2,1)S(1)}, bf16[2,288,256]{2,1,0:T(8,128)(2,1)S(1)}, u32[]{:S(2)}, u32[]{:S(2)}) collective-permute-start(bf16[2,288,256]{2,1,0:T(8,128)(2,1)S(1)} %collective-permute-done.5.d_second), channel_id=1, source_target_pairs={{0,12},{1,13},{2,14},{3,15},{4,0},{5,1},{6,2},{7,3},{8,4},{9,5},{1... | collective-permute-start | bytes 884744 | tf_op jit(solution)/shard_map/ppermute | solution.py:532
  41.2 7.1 %collective-permute-start.2 = (bf16[2,288,256]{2,1,0:T(8,128)(2,1)S(1)}, bf16[2,288,256]{2,1,0:T(8,128)(2,1)S(1)}, u32[]{:S(2)}, u32[]{:S(2)}) collective-permute-start(bf16[2,288,256]{2,1,0:T(8,128)(2,1)S(1)} %collective-permute-done.1.u_first), channel_id=1, source_target_pairs={{0,4},{1,5},{2,6},{3,7},{4,8},{5,9},{6,10},{7,11},{8,12},{9,13},{1... | collective-permute-start | bytes 884744 | tf_op jit(solution)/shard_map/ppermute | solution.py:531
  44.5 7.2 %collective-permute-start.12 = (bf16[4,288,256]{2,1,0:T(8,128)(2,1)S(1)}, bf16[4,288,256]{2,1,0:T(8,128)(2,1)S(1)}, u32[]{:S(2)}, u32[]{:S(2)}) collective-permute-start(bf16[4,288,256]{2,1,0:T(8,128)(2,1)S(1)} %get-tuple-element.70), channel_id=1, source_target_pairs={{0,16},{16,0},{32,48},{48,32},{64,80},{80,64},{96,112},{112,96},{1... | collective-permute-start | bytes 1769480 | tf_op jit(solution)/shard_map/ppermute | solution.py:551
  47.0 4.7 %collective-permute-start.11 = (bf16[4,288,256]{2,1,0:T(8,128)(2,1)S(1)}, bf16[4,288,256]{2,1,0:T(8,128)(2,1)S(1)}, u32[]{:S(2)}, u32[]{:S(2)}) collective-permute-start(bf16[4,288,256]{2,1,0:T(8,128)(2,1)S(1)} %get-tuple-element.71), channel_id=1, source_target_pairs={{0,16},{16,0},{32,48},{48,32},{64,80},{80,64},{96,112},{112,96},{1... | collective-permute-start | bytes 1769480 | tf_op jit(solution)/shard_map/ppermute | solution.py:551
  48.4 4.9 %collective-permute-start.9 = (bf16[4,288,256]{2,1,0:T(8,128)(2,1)S(1)}, bf16[4,288,256]{2,1,0:T(8,128)(2,1)S(1)}, u32[]{:S(2)}, u32[]{:S(2)}) collective-permute-start(bf16[4,288,256]{2,1,0:T(8,128)(2,1)S(1)} %maximum_add_fusion.far.refs_3_), channel_id=1, source_target_pairs={{0,16},{16,0},{32,48},{48,32},{64,80},{80,64},{96,112},{112,96},{1... | collective-permute-start | bytes 1769480 | tf_op jit(solution)/shard_map/ppermute | solution.py:560
  54.1 24.6 %copy-start.1 = (bf16[24,256]{1,0:T(8,128)(2,1)S(1)}, bf16[24,256]{1,0:T(8,128)(2,1)}, u32[]{:S(2)}) copy-start(bf16[24,256]{1,0:T(8,128)(2,1)} %hidden.1) | copy-start | bytes 36868
  54.1 24.6 %copy-start.2 = (f32[256]{0:T(256)S(1)}, f32[256]{0:T(256)}, u32[]{:S(2)}) copy-start(f32[256]{0:T(256)} %param.8) | copy-start | bytes 3076
  78.7 3.0 %collective-permute-start.13 = (bf16[16,128,256]{2,1,0:T(8,128)(2,1)S(1)}, bf16[16,128,256]{2,1,0:T(8,128)(2,1)S(1)}, u32[]{:S(2)}, u32[]{:S(2)}) collective-permute-start(bf16[16,128,256]{2,1,0:T(8,128)(2,1)S(1)} %get-tuple-element.63), channel_id=1, source_target_pairs={{0,16},{16,0},{32,48},{48,32},{64,80},{80,64},{96,112},{112,96},{1... | collective-permute-start | bytes 3145736 | tf_op jit(solution)/shard_map/ppermute | solution.py:599

commit v9 on v8

--- a/solution.py
+++ b/solution.py
@@ -10,6 +10,7 @@
 VALID = 240
 LANES = 256
 EPSILON = 1e-06
+LARGEST = 3e38
 GROUPS = 16
 VOC = 16
 ROWS = 24
@@ -168,7 +169,7 @@
         pick = jnp.where(short + 8 * k == teacher_row[...], 1.0, 0.0).astype(BF)
         tail = tail + dot(tails, pick, TN)[k * TAIL : (k + 1) * TAIL]
     spread_gain = dot(gain[...].astype(BF), jnp.ones((16, LANES), BF), TN)
-    squares = jnp.sum(block_s * block_s, axis=0, keepdims=True)
+    squares = jnp.minimum(jnp.sum(block_s * block_s, axis=0, keepdims=True), LARGEST)
     parts = split(jnp.where(spare_rows(), squares, 0.0), 2)
     lanes = spare_lanes()
     spare = jnp.concatenate([dot(part, lanes, NN) for part in parts], axis=0)

time: 116 us -> 116 us (level)
  no operation moved by 1% of the time
where the time goes in v9:
time: 116 us
  blocking collectives  76.5 us (66%)
  starting transfers between devices  19.1 us (16%)
  Pallas kernels  12.7 us (11%)
  waiting for transfers between devices  6.05 us (5%)
    all_to_all x5, blocking collectives, exchange(): return lax.all_to_all(x, axis, 0, 0, tiled=True)  76.5 us
    ppermute x1, starting transfers between devices, local(): other_far = lax.ppermute(far, 'grp', CORE_SWAP)  3.3 us
    ppermute x1, starting transfers between devices, local(): three = lax.ppermute(block, BOTH, ring(1, 3))  2.81 us
    ppermute x1, waiting for transfers between devices, local(): three = lax.ppermute(block, BOTH, ring(1, 3))  2.63 us
    pallas_call x1, Pallas kernels, local(): pl.pallas_call(forward_own, out_shape=partial + (pltpu.VMEM(teacher_head....  2.62 us
    ppermute x2, starting transfers between devices, local(): lax.ppermute(part + zero.astype(BF), 'grp', CORE_SWAP)  2.6 us
    ppermute x1, starting transfers between devices, local(): d_first = lax.ppermute(first, BOTH, ring(2, 3))  2.58 us
    ppermute x1, starting transfers between devices, local(): d_second = lax.ppermute(second, BOTH, ring(2, 3))  2.36 us
  transfers between devices with their start and end apart: 14, of which 6 were waited for; matrix products, arithmetic and copies ran while one was open for 0% of the time, Pallas kernels for 7%

profile of v9, /device:TPU:1, one launch (start us, length us, event | category | flops | bytes accessed | tf_op | source)
XLA Modules:
  0.0 115.6 jit_solution(6324842125994089551)
XLA Ops:
  0.6 1.2 %shard_map.102 = (bf16[16,56,128]{2,1,0:T(8,128)(2,1)S(1)}, s32[1,256]{1,0:T(1,128)S(1)}, s32[1,256]{1,0:T(1,128)S(1)}, f32[1,256]{1,0:T(1,128)S(1)}, f32[16,128]{1,0:T(8,128)S(1)}) custom-call(bf16[24,256]{1,0:T(8,128)(2,1)} %hidden.1, bf16[24,320]{1,0:T(8,128)(2,1)} %teacher_in.2, s32[1,192]{1,0:T(1,128)} %bitcast.19, s32[1,192]{1,0:T(1,128)} %bitcast.20, ...), custom_call_target="tpu_custom_call" | custom-call | tf_op jit(solution)/shard_map/pallas_call | solution.py:498
  1.8 20.8 %all_to_all.25.held = bf16[16,56,128]{2,1,0:T(8,128)(2,1)S(1)} all-to-all(bf16[16,56,128]{2,1,0:T(8,128)(2,1)S(1)} %get-tuple-element.37), channel_id=1, replica_groups=mesh['grp'=16,'voc'=16] {'grp'}, dimensions={0} | all-to-all | bytes 458752 | tf_op jit(solution)/shard_map/all_to_all | solution.py:481
  23.0 2.8 %collective-permute-start.4 = (bf16[288,256]{1,0:T(8,128)(2,1)S(1)}, bf16[288,256]{1,0:T(8,128)(2,1)S(1)}, u32[]{:S(2)}, u32[]{:S(2)}) collective-permute-start(bf16[288,256]{1,0:T(8,128)(2,1)S(1)} %shard_map.103.block), channel_id=1, source_target_pairs={{0,3},{1,0},{2,1},{3,2},{4,7},{5,4},{6,5},{7,6},{8,11},{9,8},{10,9... | collective-permute-start | bytes 442376 | tf_op jit(solution)/shard_map/ppermute | solution.py:524
  26.2 0.7 collective-permute-start
  26.9 2.6 %collective-permute-done.4 = bf16[288,256]{1,0:T(8,128)(2,1)S(1)} collective-permute-done((bf16[288,256]{1,0:T(8,128)(2,1)S(1)}, bf16[288,256]{1,0:T(8,128)(2,1)S(1)}, u32[]{:S(2)}, u32[]{:S(2)}) %collective-permute-start.4) | collective-permute-done | bytes 147488 | tf_op jit(solution)/shard_map/ppermute | solution.py:524
  29.5 2.1 %collective-permute-done.3 = bf16[288,256]{1,0:T(8,128)(2,1)S(1)} collective-permute-done((bf16[288,256]{1,0:T(8,128)(2,1)S(1)}, bf16[288,256]{1,0:T(8,128)(2,1)S(1)}, u32[]{:S(2)}, u32[]{:S(2)}) %collective-permute-start.3) | collective-permute-done | bytes 147488 | tf_op jit(solution)/shard_map/ppermute | solution.py:525
  31.7 2.4 %collective-permute-start.5 = (bf16[2,288,256]{2,1,0:T(8,128)(2,1)S(1)}, bf16[2,288,256]{2,1,0:T(8,128)(2,1)S(1)}, u32[]{:S(2)}, u32[]{:S(2)}) collective-permute-start(bf16[2,288,256]{2,1,0:T(8,128)(2,1)S(1)} %pad_maximum_fusion.2), channel_id=1, source_target_pairs={{0,12},{1,13},{2,14},{3,15},{4,0},{5,1},{6,2},{7,3},{8,4},{9,5},{1... | collective-permute-start | bytes 884744 | tf_op jit(solution)/shard_map/ppermute | solution.py:529
  34.3 2.6 %collective-permute-start.8 = (bf16[2,288,256]{2,1,0:T(8,128)(2,1)S(1)}, bf16[2,288,256]{2,1,0:T(8,128)(2,1)S(1)}, u32[]{:S(2)}, u32[]{:S(2)}) collective-permute-start(bf16[2,288,256]{2,1,0:T(8,128)(2,1)S(1)} %pad_maximum_fusion.1), channel_id=1, source_target_pairs={{0,12},{1,13},{2,14},{3,15},{4,0},{5,1},{6,2},{7,3},{8,4},{9,5},{1... | collective-permute-start | bytes 884744 | tf_op jit(solution)/shard_map/ppermute | solution.py:531
  37.0 2.0 %collective-permute-start.10 = (bf16[4,288,256]{2,1,0:T(8,128)(2,1)S(1)}, bf16[4,288,256]{2,1,0:T(8,128)(2,1)S(1)}, u32[]{:S(2)}, u32[]{:S(2)}) collective-permute-start(bf16[4,288,256]{2,1,0:T(8,128)(2,1)S(1)} %pad_maximum_fusion.a.refs_0_), channel_id=1, source_target_pairs={{0,16},{16,0},{32,48},{48,32},{64,80},{80,64},{96,112},{112,96},{1... | collective-permute-start | bytes 1769480 | tf_op jit(solution)/shard_map/ppermute | solution.py:551
  39.0 2.1 %collective-permute-start.6 = (bf16[2,288,256]{2,1,0:T(8,128)(2,1)S(1)}, bf16[2,288,256]{2,1,0:T(8,128)(2,1)S(1)}, u32[]{:S(2)}, u32[]{:S(2)}) collective-permute-start(bf16[2,288,256]{2,1,0:T(8,128)(2,1)S(1)} %collective-permute-done.5.d_second), channel_id=1, source_target_pairs={{0,12},{1,13},{2,14},{3,15},{4,0},{5,1},{6,2},{7,3},{8,4},{9,5},{1... | collective-permute-start | bytes 884744 | tf_op jit(solution)/shard_map/ppermute | solution.py:533
  41.2 2.6 %shard_map.104 = (f32[384,256]{1,0:T(8,128)S(1)}, f32[384,256]{1,0:T(8,128)S(1)}, f32[16,256]{1,0:T(8,128)S(1)}, bf16[5120,384]{1,0:T(8,128)(2,1)S(1)}, f32[1,256]{1,0:T(1,128)S(1)}) custom-call(bf16[4,288,256]{2,1,0:T(8,128)(2,1)S(1)} %pad_maximum_fusion.a.refs_0_, bf16[2,288,256]{2,1,0:T(8,128)(2,1)S(1)} %collective-permute-done.1.u_first, ...), custom_call_target="tpu_custom_call" | custom-call | flops 226492416 | bytes 4194304 | tf_op jit(solution)/shard_map/pallas_call | solution.py:542
  44.5 2.5 %collective-permute-start.12 = (bf16[4,288,256]{2,1,0:T(8,128)(2,1)S(1)}, bf16[4,288,256]{2,1,0:T(8,128)(2,1)S(1)}, u32[]{:S(2)}, u32[]{:S(2)}) collective-permute-start(bf16[4,288,256]{2,1,0:T(8,128)(2,1)S(1)} %get-tuple-element.70), channel_id=1, source_target_pairs={{0,16},{16,0},{32,48},{48,32},{64,80},{80,64},{96,112},{112,96},{1... | collective-permute-start | bytes 1769480 | tf_op jit(solution)/shard_map/ppermute | solution.py:552
  47.1 0.8 shard_map.105
  48.4 3.3 %collective-permute-start.9 = (bf16[4,288,256]{2,1,0:T(8,128)(2,1)S(1)}, bf16[4,288,256]{2,1,0:T(8,128)(2,1)S(1)}, u32[]{:S(2)}, u32[]{:S(2)}) collective-permute-start(bf16[4,288,256]{2,1,0:T(8,128)(2,1)S(1)} %maximum_add_fusion.far.refs_3_), channel_id=1, source_target_pairs={{0,16},{16,0},{32,48},{48,32},{64,80},{80,64},{96,112},{112,96},{1... | collective-permute-start | bytes 1769480 | tf_op jit(solution)/shard_map/ppermute | solution.py:561
  51.7 1.3 %shard_map.106 = (f32[384,256]{1,0:T(8,128)S(1)}, f32[384,256]{1,0:T(8,128)S(1)}, f32[16,256]{1,0:T(8,128)S(1)}) custom-call(bf16[4,288,256]{2,1,0:T(8,128)(2,1)S(1)} %maximum_add_fusion.far.refs_3_, bf16[4,288,256]{2,1,0:T(8,128)(2,1)S(1)} %collective-permute-done.10.other_a.refs_4_, bf16[4,288,256]{2,1,0:T(8,128)(2,1)S(1)} %collective-permute-done.11.other_u.refs_5_, ...), custom_call_target="tpu_custom_call" | custom-call | flops 905969664 | bytes 4194304 | tf_op jit(solution)/shard_map/pallas_call | solution.py:562
  53.3 0.8 shard_map.107
  54.1 9.4 %all_to_all.26.stats = f32[16,8,256]{2,1,0:T(8,128)S(1)} all-to-all(f32[16,8,256]{2,1,0:T(8,128)S(1)} %get-tuple-element.53), channel_id=1, replica_groups=mesh['grp'=16,'voc'=16] {'voc'}, dimensions={0} | all-to-all | bytes 262144 | tf_op jit(solution)/shard_map/all_to_all | solution.py:481
  63.7 13.7 %all_to_all.27.stats = f32[16,8,256]{2,1,0:T(8,128)S(1)} all-to-all(f32[16,8,256]{2,1,0:T(8,128)S(1)} %shard_map.108), channel_id=1, replica_groups=mesh['grp'=16,'voc'=16] {'grp'}, dimensions={0} | all-to-all | bytes 262144 | tf_op jit(solution)/shard_map/all_to_all | solution.py:481
  77.4 1.3 %shard_map.109 = (bf16[384,256]{1,0:T(8,128)(2,1)S(1)}, bf16[384,256]{1,0:T(8,128)(2,1)S(1)}, bf16[16,128,256]{2,1,0:T(8,128)(2,1)S(1)}, f32[1,256]{1,0:T(1,128)S(1)}, f32[1,1]{1,0:T(1,128)}) custom-call(f32[16,8,256]{2,1,0:T(8,128)S(1)} %all_to_all.27.stats, f32[8,256]{1,0:T(8,128)S(1)} %get-tuple-element.54.tops, f32[384,256]{1,0:T(8,128)S(1)} %get-tuple-element.55.exp_in, ...), custom_call_target="tpu_custom_call" | custom-call | flops 402653184 | bytes 4194304 | tf_op jit(solution)/shard_map/pallas_call | solution.py:587
  78.7 0.7 shard_map.110
  79.5 2.2 %shard_map.111 = (bf16[4096,384]{1,0:T(8,128)(2,1)}, f32[1,256]{1,0:T(1,128)S(1)}) custom-call(bf16[4,288,256]{2,1,0:T(8,128)(2,1)S(1)} %pad_maximum_fusion.a.refs_0_, bf16[4,288,256]{2,1,0:T(8,128)(2,1)S(1)} %constant_dynamic-update-slice_fusion.u.refs_1_, bf16[4,288,256]{2,1,0:T(8,128)(2,1)S(1)} %constant_dynamic-update-slice_fusion.2.d.refs_2_, ...), custom_call_target="tpu_custom_call" | custom-call | flops 805306368 | bytes 4194304 | tf_op jit(solution)/shard_map/pallas_call | solution.py:607
  82.0 19.0 %all_to_all.28.pieces = bf16[16,128,256]{2,1,0:T(8,128)(2,1)S(1)} all-to-all(bf16[16,128,256]{2,1,0:T(8,128)(2,1)S(1)} %shard_map.112), channel_id=1, replica_groups=mesh['grp'=16,'voc'=16] {'voc'}, dimensions={0} | all-to-all | bytes 2097152 | tf_op jit(solution)/shard_map/all_to_all | solution.py:481
  101.4 13.6 %all_to_all.29.pieces = bf16[16,32,128]{2,1,0:T(8,128)(2,1)S(1)} all-to-all(bf16[16,32,128]{2,1,0:T(8,128)(2,1)S(1)} %shard_map.113), channel_id=1, replica_groups=mesh['grp'=16,'voc'=16] {'grp'}, dimensions={0} | all-to-all | bytes 262144 | tf_op jit(solution)/shard_map/all_to_all | solution.py:481
  115.0 0.6 shard_map.114
  (39 shorter events, 3.6 us)
Async XLA Ops:
  0.6 40.6 %copy-start = (bf16[4096,384]{1,0:T(8,128)(2,1)S(1)}, bf16[4096,384]{1,0:T(8,128)(2,1)}, u32[]{:S(2)}) copy-start(bf16[4096,384]{1,0:T(8,128)(2,1)} %student_head.11) | copy-start | bytes 9437188
  23.0 6.5 %collective-permute-start.4 = (bf16[288,256]{1,0:T(8,128)(2,1)S(1)}, bf16[288,256]{1,0:T(8,128)(2,1)S(1)}, u32[]{:S(2)}, u32[]{:S(2)}) collective-permute-start(bf16[288,256]{1,0:T(8,128)(2,1)S(1)} %shard_map.103.block), channel_id=1, source_target_pairs={{0,3},{1,0},{2,1},{3,2},{4,7},{5,4},{6,5},{7,6},{8,11},{9,8},{10,9... | collective-permute-start | bytes 442376 | tf_op jit(solution)/shard_map/ppermute | solution.py:524
  25.9 5.8 %collective-permute-start.3 = (bf16[288,256]{1,0:T(8,128)(2,1)S(1)}, bf16[288,256]{1,0:T(8,128)(2,1)S(1)}, u32[]{:S(2)}, u32[]{:S(2)}) collective-permute-start(bf16[288,256]{1,0:T(8,128)(2,1)S(1)} %shard_map.103.block), channel_id=1, source_target_pairs={{0,2},{1,3},{2,0},{3,1},{4,6},{5,7},{6,4},{7,5},{8,10},{9,11},{10,... | collective-permute-start | bytes 442376 | tf_op jit(solution)/shard_map/ppermute | solution.py:525
  26.2 7.8 %collective-permute-start = (bf16[288,256]{1,0:T(8,128)(2,1)S(1)}, bf16[288,256]{1,0:T(8,128)(2,1)S(1)}, u32[]{:S(2)}, u32[]{:S(2)}) collective-permute-start(bf16[288,256]{1,0:T(8,128)(2,1)S(1)} %shard_map.103.block), channel_id=1, source_target_pairs={{0,1},{1,2},{2,3},{3,0},{4,5},{5,6},{6,7},{7,4},{8,9},{9,10},{10,1... | collective-permute-start | bytes 442376 | tf_op jit(solution)/shard_map/ppermute | solution.py:523
  31.7 7.3 %collective-permute-start.5 = (bf16[2,288,256]{2,1,0:T(8,128)(2,1)S(1)}, bf16[2,288,256]{2,1,0:T(8,128)(2,1)S(1)}, u32[]{:S(2)}, u32[]{:S(2)}) collective-permute-start(bf16[2,288,256]{2,1,0:T(8,128)(2,1)S(1)} %pad_maximum_fusion.2), channel_id=1, source_target_pairs={{0,12},{1,13},{2,14},{3,15},{4,0},{5,1},{6,2},{7,3},{8,4},{9,5},{1... | collective-permute-start | bytes 884744 | tf_op jit(solution)/shard_map/ppermute | solution.py:529
  34.1 7.2 %collective-permute-start.1 = (bf16[2,288,256]{2,1,0:T(8,128)(2,1)S(1)}, bf16[2,288,256]{2,1,0:T(8,128)(2,1)S(1)}, u32[]{:S(2)}, u32[]{:S(2)}) collective-permute-start(bf16[2,288,256]{2,1,0:T(8,128)(2,1)S(1)} %pad_maximum_fusion.1), channel_id=1, source_target_pairs={{0,4},{1,5},{2,6},{3,7},{4,8},{5,9},{6,10},{7,11},{8,12},{9,13},{1... | collective-permute-start | bytes 884744 | tf_op jit(solution)/shard_map/ppermute | solution.py:528
  34.3 9.7 %collective-permute-start.8 = (bf16[2,288,256]{2,1,0:T(8,128)(2,1)S(1)}, bf16[2,288,256]{2,1,0:T(8,128)(2,1)S(1)}, u32[]{:S(2)}, u32[]{:S(2)}) collective-permute-start(bf16[2,288,256]{2,1,0:T(8,128)(2,1)S(1)} %pad_maximum_fusion.1), channel_id=1, source_target_pairs={{0,12},{1,13},{2,14},{3,15},{4,0},{5,1},{6,2},{7,3},{8,4},{9,5},{1... | collective-permute-start | bytes 884744 | tf_op jit(solution)/shard_map/ppermute | solution.py:531
  36.9 7.5 %collective-permute-start.7 = (bf16[2,288,256]{2,1,0:T(8,128)(2,1)S(1)}, bf16[2,288,256]{2,1,0:T(8,128)(2,1)S(1)}, u32[]{:S(2)}, u32[]{:S(2)}) collective-permute-start(bf16[2,288,256]{2,1,0:T(8,128)(2,1)S(1)} %pad_maximum_fusion.2), channel_id=1, source_target_pairs={{0,4},{1,5},{2,6},{3,7},{4,8},{5,9},{6,10},{7,11},{8,12},{9,13},{1... | collective-permute-start | bytes 884744 | tf_op jit(solution)/shard_map/ppermute | solution.py:530
  37.0 14.7 %collective-permute-start.10 = (bf16[4,288,256]{2,1,0:T(8,128)(2,1)S(1)}, bf16[4,288,256]{2,1,0:T(8,128)(2,1)S(1)}, u32[]{:S(2)}, u32[]{:S(2)}) collective-permute-start(bf16[4,288,256]{2,1,0:T(8,128)(2,1)S(1)} %pad_maximum_fusion.a.refs_0_), channel_id=1, source_target_pairs={{0,16},{16,0},{32,48},{48,32},{64,80},{80,64},{96,112},{112,96},{1... | collective-permute-start | bytes 1769480 | tf_op jit(solution)/shard_map/ppermute | solution.py:551
  39.0 8.9 %collective-permute-start.6 = (bf16[2,288,256]{2,1,0:T(8,128)(2,1)S(1)}, bf16[2,288,256]{2,1,0:T(8,128)(2,1)S(1)}, u32[]{:S(2)}, u32[]{:S(2)}) collective-permute-start(bf16[2,288,256]{2,1,0:T(8,128)(2,1)S(1)} %collective-permute-done.5.d_second), channel_id=1, source_target_pairs={{0,12},{1,13},{2,14},{3,15},{4,0},{5,1},{6,2},{7,3},{8,4},{9,5},{1... | collective-permute-start | bytes 884744 | tf_op jit(solution)/shard_map/ppermute | solution.py:533
  41.2 7.1 %collective-permute-start.2 = (bf16[2,288,256]{2,1,0:T(8,128)(2,1)S(1)}, bf16[2,288,256]{2,1,0:T(8,128)(2,1)S(1)}, u32[]{:S(2)}, u32[]{:S(2)}) collective-permute-start(bf16[2,288,256]{2,1,0:T(8,128)(2,1)S(1)} %collective-permute-done.1.u_first), channel_id=1, source_target_pairs={{0,4},{1,5},{2,6},{3,7},{4,8},{5,9},{6,10},{7,11},{8,12},{9,13},{1... | collective-permute-start | bytes 884744 | tf_op jit(solution)/shard_map/ppermute | solution.py:532
  44.5 7.2 %collective-permute-start.12 = (bf16[4,288,256]{2,1,0:T(8,128)(2,1)S(1)}, bf16[4,288,256]{2,1,0:T(8,128)(2,1)S(1)}, u32[]{:S(2)}, u32[]{:S(2)}) collective-permute-start(bf16[4,288,256]{2,1,0:T(8,128)(2,1)S(1)} %get-tuple-element.70), channel_id=1, source_target_pairs={{0,16},{16,0},{32,48},{48,32},{64,80},{80,64},{96,112},{112,96},{1... | collective-permute-start | bytes 1769480 | tf_op jit(solution)/shard_map/ppermute | solution.py:552
  47.0 4.7 %collective-permute-start.11 = (bf16[4,288,256]{2,1,0:T(8,128)(2,1)S(1)}, bf16[4,288,256]{2,1,0:T(8,128)(2,1)S(1)}, u32[]{:S(2)}, u32[]{:S(2)}) collective-permute-start(bf16[4,288,256]{2,1,0:T(8,128)(2,1)S(1)} %get-tuple-element.71), channel_id=1, source_target_pairs={{0,16},{16,0},{32,48},{48,32},{64,80},{80,64},{96,112},{112,96},{1... | collective-permute-start | bytes 1769480 | tf_op jit(solution)/shard_map/ppermute | solution.py:552
  48.4 4.9 %collective-permute-start.9 = (bf16[4,288,256]{2,1,0:T(8,128)(2,1)S(1)}, bf16[4,288,256]{2,1,0:T(8,128)(2,1)S(1)}, u32[]{:S(2)}, u32[]{:S(2)}) collective-permute-start(bf16[4,288,256]{2,1,0:T(8,128)(2,1)S(1)} %maximum_add_fusion.far.refs_3_), channel_id=1, source_target_pairs={{0,16},{16,0},{32,48},{48,32},{64,80},{80,64},{96,112},{112,96},{1... | collective-permute-start | bytes 1769480 | tf_op jit(solution)/shard_map/ppermute | solution.py:561
  54.1 24.6 %copy-start.1 = (bf16[24,256]{1,0:T(8,128)(2,1)S(1)}, bf16[24,256]{1,0:T(8,128)(2,1)}, u32[]{:S(2)}) copy-start(bf16[24,256]{1,0:T(8,128)(2,1)} %hidden.1) | copy-start | bytes 36868
  54.1 24.6 %copy-start.2 = (f32[256]{0:T(256)S(1)}, f32[256]{0:T(256)}, u32[]{:S(2)}) copy-start(f32[256]{0:T(256)} %param.8) | copy-start | bytes 3076
  78.7 3.0 %collective-permute-start.13 = (bf16[16,128,256]{2,1,0:T(8,128)(2,1)S(1)}, bf16[16,128,256]{2,1,0:T(8,128)(2,1)S(1)}, u32[]{:S(2)}, u32[]{:S(2)}) collective-permute-start(bf16[16,128,256]{2,1,0:T(8,128)(2,1)S(1)} %get-tuple-element.63), channel_id=1, source_target_pairs={{0,16},{16,0},{32,48},{48,32},{64,80},{80,64},{96,112},{112,96},{1... | collective-permute-start | bytes 3145736 | tf_op jit(solution)/shard_map/ppermute | solution.py:600

commit v10 on v9

--- a/solution.py
+++ b/solution.py
@@ -389,10 +389,24 @@
     terms_of(batches((None,) * 4, core), student_head, grad, core, away)
 
 
-def backward_two(
-    grad, student_head, hidden, gain, student_row, inverse, pull, stay, base_out
-):
+def backward_two(*refs):
+    scaled, grad, student_head, hidden, gain, student_row, inverse, pull = refs[8:16]
+    stay, base_out, out, blocks, sems = refs[16:]
     core = own_core()
+    copies = []
+    for k, side in enumerate((core, 1 - core)):
+        for group in batches(refs[SIDE * k : SIDE * k + SIDE], side):
+            block = jnp.concatenate([ref[j, :HALF_S, :] for ref, j, _ in group], axis=0)
+            result = dot(block, scaled[...], NT).astype(BF)
+            for i, (_, _, v) in enumerate(group):
+                n = len(copies)
+                blocks[n] = result[i * HALF_S : (i + 1) * HALF_S]
+                copies.append(
+                    pltpu.make_async_copy(
+                        blocks.at[n], out.at[span_of(v, side, HALF_S)], sems.at[n]
+                    )
+                )
+                copies[n].start()
     first = lax.axis_index("grp") * ROWS
     own = lax.broadcasted_iota(jnp.int32, (ROWS, LANES), 0) + first == student_row[...]
     own_rms = jnp.sum(jnp.where(own, inverse[...], 0.0), axis=1, keepdims=True)
@@ -401,30 +415,11 @@
     base_out[ROWS : 2 * ROWS] = hidden[...].astype(F32) * own_pull
     base_out[2 * ROWS :] = jnp.broadcast_to(1.0 / gain[...], (8, LANES))
     terms_of(batches((None,) * 4, core), student_head, grad[...], core, stay)
-
-
-def head_kernel(*refs):
-    scaled, out, zero_out, blocks, sems = refs[8:]
-    zero_out[...] = jnp.zeros((1, LANES), F32)
-    copies = []
-    for k, core in enumerate((own_core(), 1 - own_core())):
-        for group in batches(refs[SIDE * k : SIDE * k + SIDE], core):
-            block = jnp.concatenate([ref[j, :HALF_S, :] for ref, j, _ in group], axis=0)
-            result = dot(block, scaled[...], NT).astype(BF)
-            for i, (_, _, v) in enumerate(group):
-                n = len(copies)
-                blocks[n] = result[i * HALF_S : (i + 1) * HALF_S]
-                copies.append(
-                    pltpu.make_async_copy(
-                        blocks.at[n], out.at[span_of(v, core, HALF_S)], sems.at[n]
-                    )
-                )
-                copies[n].start()
     for copy in copies:
         copy.wait()
 
 
-def pair_kernel(stay, arrived, zero, out):
+def pair_kernel(stay, arrived, out):
     for v in range(VOC):
         out[v] = (stay[v].astype(F32) + arrived[v].astype(F32)).astype(BF)
 
@@ -598,22 +593,23 @@
         cost_estimate=cost(DS * VOC_DEV * LANES),
     )(from_grp, tops, exp_s, ratio, weight, inverse, student_head)
     arrived = lax.ppermute(away, "grp", CORE_SWAP)
-    stay, base = pl.pallas_call(
+    stay, base, grad_head = pl.pallas_call(
         backward_two,
-        out_shape=(half_rows, shape((2 * ROWS + 8, LANES), F32)),
-        compiler_params=params(8),
-        cost_estimate=cost(DS * VOC_DEV * LANES),
-    )(grad, student_head, student_hidden, norm_gain[None], student_row, inverse, pull)
-    grad_head, zero = pl.pallas_call(
-        head_kernel,
-        out_shape=(shape((DS, VOC_DEV), BF), row),
-        out_specs=(HBM, VMEM),
+        out_shape=(
+            half_rows,
+            shape((2 * ROWS + 8, LANES), F32),
+            shape((DS, VOC_DEV), BF),
+        ),
+        out_specs=(VMEM, VMEM, HBM),
         scratch_shapes=[pltpu.VMEM((2 * VOC, HALF_S, VOC_DEV), BF), sems(2 * VOC)],
         compiler_params=params(12),
-        cost_estimate=cost(DS * VOC_DEV * LANES * 2),
-    )(a, u, d, far, *other, other_far, scaled)
+        cost_estimate=cost(DS * VOC_DEV * LANES * 3),
+    )(
+        a, u, d, far, *other, other_far, scaled, grad, student_head,
+        student_hidden, norm_gain[None], student_row, inverse, pull,
+    )
     pair = pl.pallas_call(pair_kernel, out_shape=half_rows, compiler_params=params(8))(
-        stay, arrived, zero
+        stay, arrived
     )
     pieces = exchange(pair, "voc")
     outgoing = pl.pallas_call(

time: 116 us -> 116 us (level)
    pallas_call x1 -> x0, Pallas kernels: 2.21 us -> none  [local(): pl.pallas_call(head_kernel, out_shape=(shape((DS, VOC_DEV), BF), row), ou...]
    pallas_call x1, Pallas kernels: 0.74 us -> 2.52 us  [local(): pl.pallas_call(backward_two, out_shape=(half_rows, shape((2 * ROWS + 8, L...]
  transfers between devices with their start and end apart: 14 -> 14, of which waited for: 6 -> 7; matrix products, arithmetic and copies ran while one was open for 0% -> 0% of each run, Pallas kernels for 7% -> 6%
where the time goes in v10:
time: 116 us; the launch traced here: 115 us
  blocking collectives  76.5 us (66%)
  starting transfers between devices  19.1 us (16%)
  Pallas kernels  12.3 us (11%)
  waiting for transfers between devices  6.18 us (5%)
    all_to_all x5, blocking collectives, exchange(): return lax.all_to_all(x, axis, 0, 0, tiled=True)  76.5 us
    ppermute x1, starting transfers between devices, local(): other_far = lax.ppermute(far, 'grp', CORE_SWAP)  3.3 us
    ppermute x1, starting transfers between devices, local(): three = lax.ppermute(block, BOTH, ring(1, 3))  2.81 us
    ppermute x1, waiting for transfers between devices, local(): three = lax.ppermute(block, BOTH, ring(1, 3))  2.63 us
    pallas_call x1, Pallas kernels, local(): pl.pallas_call(forward_own, out_shape=partial + (pltpu.VMEM(teacher_head....  2.62 us
    ppermute x2, starting transfers between devices, local(): lax.ppermute(part + zero.astype(BF), 'grp', CORE_SWAP)  2.6 us
    ppermute x1, starting transfers between devices, local(): d_first = lax.ppermute(first, BOTH, ring(2, 3))  2.58 us
    pallas_call x1, Pallas kernels, local(): pl.pallas_call(backward_two, out_shape=(half_rows, shape((2 * ROWS + 8, L...  2.52 us
  transfers between devices with their start and end apart: 14, of which 7 were waited for; matrix products, arithmetic and copies ran while one was open for 0% of the time, Pallas kernels for 6%

profile of v10, /device:TPU:1, one launch (start us, length us, event | category | flops | bytes accessed | tf_op | source)
XLA Modules:
  0.0 115.2 jit_solution(12708838272634769366)
XLA Ops:
  0.6 1.2 %shard_map.102 = (bf16[16,56,128]{2,1,0:T(8,128)(2,1)S(1)}, s32[1,256]{1,0:T(1,128)S(1)}, s32[1,256]{1,0:T(1,128)S(1)}, f32[1,256]{1,0:T(1,128)S(1)}, f32[16,128]{1,0:T(8,128)S(1)}) custom-call(bf16[24,256]{1,0:T(8,128)(2,1)} %refs_11_.1, bf16[24,320]{1,0:T(8,128)(2,1)} %teacher_in.2, s32[1,192]{1,0:T(1,128)} %bitcast.19, s32[1,192]{1,0:T(1,128)} %bitcast.20, ...), custom_call_target="tpu_custom_call" | custom-call | tf_op jit(solution)/shard_map/pallas_call | solution.py:493
  1.8 20.8 %all_to_all.25.held = bf16[16,56,128]{2,1,0:T(8,128)(2,1)S(1)} all-to-all(bf16[16,56,128]{2,1,0:T(8,128)(2,1)S(1)} %get-tuple-element.36), channel_id=1, replica_groups=mesh['grp'=16,'voc'=16] {'grp'}, dimensions={0} | all-to-all | bytes 458752 | tf_op jit(solution)/shard_map/all_to_all | solution.py:476
  23.0 2.8 %collective-permute-start.4 = (bf16[288,256]{1,0:T(8,128)(2,1)S(1)}, bf16[288,256]{1,0:T(8,128)(2,1)S(1)}, u32[]{:S(2)}, u32[]{:S(2)}) collective-permute-start(bf16[288,256]{1,0:T(8,128)(2,1)S(1)} %shard_map.103.block), channel_id=1, source_target_pairs={{0,3},{1,0},{2,1},{3,2},{4,7},{5,4},{6,5},{7,6},{8,11},{9,8},{10,9... | collective-permute-start | bytes 442376 | tf_op jit(solution)/shard_map/ppermute | solution.py:519
  26.2 0.7 collective-permute-start
  26.9 2.6 %collective-permute-done.4 = bf16[288,256]{1,0:T(8,128)(2,1)S(1)} collective-permute-done((bf16[288,256]{1,0:T(8,128)(2,1)S(1)}, bf16[288,256]{1,0:T(8,128)(2,1)S(1)}, u32[]{:S(2)}, u32[]{:S(2)}) %collective-permute-start.4) | collective-permute-done | bytes 147488 | tf_op jit(solution)/shard_map/ppermute | solution.py:519
  29.5 2.1 %collective-permute-done.3 = bf16[288,256]{1,0:T(8,128)(2,1)S(1)} collective-permute-done((bf16[288,256]{1,0:T(8,128)(2,1)S(1)}, bf16[288,256]{1,0:T(8,128)(2,1)S(1)}, u32[]{:S(2)}, u32[]{:S(2)}) %collective-permute-start.3) | collective-permute-done | bytes 147488 | tf_op jit(solution)/shard_map/ppermute | solution.py:520
  31.7 2.4 %collective-permute-start.5 = (bf16[2,288,256]{2,1,0:T(8,128)(2,1)S(1)}, bf16[2,288,256]{2,1,0:T(8,128)(2,1)S(1)}, u32[]{:S(2)}, u32[]{:S(2)}) collective-permute-start(bf16[2,288,256]{2,1,0:T(8,128)(2,1)S(1)} %pad_maximum_fusion.2), channel_id=1, source_target_pairs={{0,12},{1,13},{2,14},{3,15},{4,0},{5,1},{6,2},{7,3},{8,4},{9,5},{1... | collective-permute-start | bytes 884744 | tf_op jit(solution)/shard_map/ppermute | solution.py:524
  34.3 2.6 %collective-permute-start.8 = (bf16[2,288,256]{2,1,0:T(8,128)(2,1)S(1)}, bf16[2,288,256]{2,1,0:T(8,128)(2,1)S(1)}, u32[]{:S(2)}, u32[]{:S(2)}) collective-permute-start(bf16[2,288,256]{2,1,0:T(8,128)(2,1)S(1)} %pad_maximum_fusion.1), channel_id=1, source_target_pairs={{0,12},{1,13},{2,14},{3,15},{4,0},{5,1},{6,2},{7,3},{8,4},{9,5},{1... | collective-permute-start | bytes 884744 | tf_op jit(solution)/shard_map/ppermute | solution.py:526
  37.0 2.0 %collective-permute-start.10 = (bf16[4,288,256]{2,1,0:T(8,128)(2,1)S(1)}, bf16[4,288,256]{2,1,0:T(8,128)(2,1)S(1)}, u32[]{:S(2)}, u32[]{:S(2)}) collective-permute-start(bf16[4,288,256]{2,1,0:T(8,128)(2,1)S(1)} %pad_maximum_fusion.a.refs_0_), channel_id=1, source_target_pairs={{0,16},{16,0},{32,48},{48,32},{64,80},{80,64},{96,112},{112,96},{1... | collective-permute-start | bytes 1769480 | tf_op jit(solution)/shard_map/ppermute | solution.py:546
  39.0 2.1 %collective-permute-start.6 = (bf16[2,288,256]{2,1,0:T(8,128)(2,1)S(1)}, bf16[2,288,256]{2,1,0:T(8,128)(2,1)S(1)}, u32[]{:S(2)}, u32[]{:S(2)}) collective-permute-start(bf16[2,288,256]{2,1,0:T(8,128)(2,1)S(1)} %collective-permute-done.5.d_second), channel_id=1, source_target_pairs={{0,12},{1,13},{2,14},{3,15},{4,0},{5,1},{6,2},{7,3},{8,4},{9,5},{1... | collective-permute-start | bytes 884744 | tf_op jit(solution)/shard_map/ppermute | solution.py:528
  41.2 2.6 %shard_map.104 = (f32[384,256]{1,0:T(8,128)S(1)}, f32[384,256]{1,0:T(8,128)S(1)}, f32[16,256]{1,0:T(8,128)S(1)}, bf16[5120,384]{1,0:T(8,128)(2,1)S(1)}, f32[1,256]{1,0:T(1,128)S(1)}) custom-call(bf16[4,288,256]{2,1,0:T(8,128)(2,1)S(1)} %pad_maximum_fusion.a.refs_0_, bf16[2,288,256]{2,1,0:T(8,128)(2,1)S(1)} %collective-permute-done.1.u_first, ...), custom_call_target="tpu_custom_call" | custom-call | flops 226492416 | bytes 4194304 | tf_op jit(solution)/shard_map/pallas_call | solution.py:537
  44.5 2.5 %collective-permute-start.12 = (bf16[4,288,256]{2,1,0:T(8,128)(2,1)S(1)}, bf16[4,288,256]{2,1,0:T(8,128)(2,1)S(1)}, u32[]{:S(2)}, u32[]{:S(2)}) collective-permute-start(bf16[4,288,256]{2,1,0:T(8,128)(2,1)S(1)} %get-tuple-element.68), channel_id=1, source_target_pairs={{0,16},{16,0},{32,48},{48,32},{64,80},{80,64},{96,112},{112,96},{1... | collective-permute-start | bytes 1769480 | tf_op jit(solution)/shard_map/ppermute | solution.py:547
  47.1 0.8 shard_map.105
  48.4 3.3 %collective-permute-start.9 = (bf16[4,288,256]{2,1,0:T(8,128)(2,1)S(1)}, bf16[4,288,256]{2,1,0:T(8,128)(2,1)S(1)}, u32[]{:S(2)}, u32[]{:S(2)}) collective-permute-start(bf16[4,288,256]{2,1,0:T(8,128)(2,1)S(1)} %maximum_add_fusion.far.refs_3_), channel_id=1, source_target_pairs={{0,16},{16,0},{32,48},{48,32},{64,80},{80,64},{96,112},{112,96},{1... | collective-permute-start | bytes 1769480 | tf_op jit(solution)/shard_map/ppermute | solution.py:556
  51.7 1.3 %shard_map.106 = (f32[384,256]{1,0:T(8,128)S(1)}, f32[384,256]{1,0:T(8,128)S(1)}, f32[16,256]{1,0:T(8,128)S(1)}) custom-call(bf16[4,288,256]{2,1,0:T(8,128)(2,1)S(1)} %maximum_add_fusion.far.refs_3_, bf16[4,288,256]{2,1,0:T(8,128)(2,1)S(1)} %collective-permute-done.10.other_a.refs_4_, bf16[4,288,256]{2,1,0:T(8,128)(2,1)S(1)} %collective-permute-done.11.other_u.refs_5_, ...), custom_call_target="tpu_custom_call" | custom-call | flops 905969664 | bytes 4194304 | tf_op jit(solution)/shard_map/pallas_call | solution.py:557
  53.3 0.8 shard_map.107
  54.1 9.4 %all_to_all.26.stats = f32[16,8,256]{2,1,0:T(8,128)S(1)} all-to-all(f32[16,8,256]{2,1,0:T(8,128)S(1)} %get-tuple-element.52), channel_id=1, replica_groups=mesh['grp'=16,'voc'=16] {'voc'}, dimensions={0} | all-to-all | bytes 262144 | tf_op jit(solution)/shard_map/all_to_all | solution.py:476
  63.7 13.7 %all_to_all.27.stats = f32[16,8,256]{2,1,0:T(8,128)S(1)} all-to-all(f32[16,8,256]{2,1,0:T(8,128)S(1)} %shard_map.108), channel_id=1, replica_groups=mesh['grp'=16,'voc'=16] {'grp'}, dimensions={0} | all-to-all | bytes 262144 | tf_op jit(solution)/shard_map/all_to_all | solution.py:476
  77.4 1.3 %shard_map.109 = (bf16[384,256]{1,0:T(8,128)(2,1)S(1)}, bf16[384,256]{1,0:T(8,128)(2,1)S(1)}, bf16[16,128,256]{2,1,0:T(8,128)(2,1)S(1)}, f32[1,256]{1,0:T(1,128)S(1)}, f32[1,1]{1,0:T(1,128)}) custom-call(f32[16,8,256]{2,1,0:T(8,128)S(1)} %all_to_all.27.stats, f32[8,256]{1,0:T(8,128)S(1)} %get-tuple-element.53.tops, f32[384,256]{1,0:T(8,128)S(1)} %get-tuple-element.54.exp_in, ...), custom_call_target="tpu_custom_call" | custom-call | flops 402653184 | bytes 4194304 | tf_op jit(solution)/shard_map/pallas_call | solution.py:582
  78.7 2.5 %shard_map.110 = (bf16[16,128,256]{2,1,0:T(8,128)(2,1)S(1)}, f32[56,256]{1,0:T(8,128)S(1)}, bf16[4096,384]{1,0:T(8,128)(2,1)}) custom-call(bf16[4,288,256]{2,1,0:T(8,128)(2,1)S(1)} %pad_maximum_fusion.a.refs_0_, bf16[4,288,256]{2,1,0:T(8,128)(2,1)S(1)} %constant_dynamic-update-slice_fusion.u.refs_1_, ...), custom_call_target="tpu_custom_call" | custom-call | flops 1207959552 | bytes 4194304 | tf_op jit(solution)/shard_map/pallas_call | solution.py:596
  81.7 19.1 %all_to_all.28.pieces = bf16[16,128,256]{2,1,0:T(8,128)(2,1)S(1)} all-to-all(bf16[16,128,256]{2,1,0:T(8,128)(2,1)S(1)} %shard_map.111), channel_id=1, replica_groups=mesh['grp'=16,'voc'=16] {'voc'}, dimensions={0} | all-to-all | bytes 2097152 | tf_op jit(solution)/shard_map/all_to_all | solution.py:476
  100.8 0.4 shard_map.112
  101.2 13.4 %all_to_all.29.pieces = bf16[16,32,128]{2,1,0:T(8,128)(2,1)S(1)} all-to-all(bf16[16,32,128]{2,1,0:T(8,128)(2,1)S(1)} %shard_map.112), channel_id=1, replica_groups=mesh['grp'=16,'voc'=16] {'grp'}, dimensions={0} | all-to-all | bytes 262144 | tf_op jit(solution)/shard_map/all_to_all | solution.py:476
  114.6 0.6 shard_map.113
  (38 shorter events, 3.3 us)
Async XLA Ops:
  0.6 40.6 %copy-start = (bf16[4096,384]{1,0:T(8,128)(2,1)S(1)}, bf16[4096,384]{1,0:T(8,128)(2,1)}, u32[]{:S(2)}) copy-start(bf16[4096,384]{1,0:T(8,128)(2,1)} %refs_10_.1) | copy-start | bytes 9437188
  23.0 6.5 %collective-permute-start.4 = (bf16[288,256]{1,0:T(8,128)(2,1)S(1)}, bf16[288,256]{1,0:T(8,128)(2,1)S(1)}, u32[]{:S(2)}, u32[]{:S(2)}) collective-permute-start(bf16[288,256]{1,0:T(8,128)(2,1)S(1)} %shard_map.103.block), channel_id=1, source_target_pairs={{0,3},{1,0},{2,1},{3,2},{4,7},{5,4},{6,5},{7,6},{8,11},{9,8},{10,9... | collective-permute-start | bytes 442376 | tf_op jit(solution)/shard_map/ppermute | solution.py:519
  25.9 5.8 %collective-permute-start.3 = (bf16[288,256]{1,0:T(8,128)(2,1)S(1)}, bf16[288,256]{1,0:T(8,128)(2,1)S(1)}, u32[]{:S(2)}, u32[]{:S(2)}) collective-permute-start(bf16[288,256]{1,0:T(8,128)(2,1)S(1)} %shard_map.103.block), channel_id=1, source_target_pairs={{0,2},{1,3},{2,0},{3,1},{4,6},{5,7},{6,4},{7,5},{8,10},{9,11},{10,... | collective-permute-start | bytes 442376 | tf_op jit(solution)/shard_map/ppermute | solution.py:520
  26.2 7.8 %collective-permute-start = (bf16[288,256]{1,0:T(8,128)(2,1)S(1)}, bf16[288,256]{1,0:T(8,128)(2,1)S(1)}, u32[]{:S(2)}, u32[]{:S(2)}) collective-permute-start(bf16[288,256]{1,0:T(8,128)(2,1)S(1)} %shard_map.103.block), channel_id=1, source_target_pairs={{0,1},{1,2},{2,3},{3,0},{4,5},{5,6},{6,7},{7,4},{8,9},{9,10},{10,1... | collective-permute-start | bytes 442376 | tf_op jit(solution)/shard_map/ppermute | solution.py:518
  31.7 7.3 %collective-permute-start.5 = (bf16[2,288,256]{2,1,0:T(8,128)(2,1)S(1)}, bf16[2,288,256]{2,1,0:T(8,128)(2,1)S(1)}, u32[]{:S(2)}, u32[]{:S(2)}) collective-permute-start(bf16[2,288,256]{2,1,0:T(8,128)(2,1)S(1)} %pad_maximum_fusion.2), channel_id=1, source_target_pairs={{0,12},{1,13},{2,14},{3,15},{4,0},{5,1},{6,2},{7,3},{8,4},{9,5},{1... | collective-permute-start | bytes 884744 | tf_op jit(solution)/shard_map/ppermute | solution.py:524
  34.1 7.2 %collective-permute-start.1 = (bf16[2,288,256]{2,1,0:T(8,128)(2,1)S(1)}, bf16[2,288,256]{2,1,0:T(8,128)(2,1)S(1)}, u32[]{:S(2)}, u32[]{:S(2)}) collective-permute-start(bf16[2,288,256]{2,1,0:T(8,128)(2,1)S(1)} %pad_maximum_fusion.1), channel_id=1, source_target_pairs={{0,4},{1,5},{2,6},{3,7},{4,8},{5,9},{6,10},{7,11},{8,12},{9,13},{1... | collective-permute-start | bytes 884744 | tf_op jit(solution)/shard_map/ppermute | solution.py:523
  34.3 9.7 %collective-permute-start.8 = (bf16[2,288,256]{2,1,0:T(8,128)(2,1)S(1)}, bf16[2,288,256]{2,1,0:T(8,128)(2,1)S(1)}, u32[]{:S(2)}, u32[]{:S(2)}) collective-permute-start(bf16[2,288,256]{2,1,0:T(8,128)(2,1)S(1)} %pad_maximum_fusion.1), channel_id=1, source_target_pairs={{0,12},{1,13},{2,14},{3,15},{4,0},{5,1},{6,2},{7,3},{8,4},{9,5},{1... | collective-permute-start | bytes 884744 | tf_op jit(solution)/shard_map/ppermute | solution.py:526
  36.9 7.5 %collective-permute-start.7 = (bf16[2,288,256]{2,1,0:T(8,128)(2,1)S(1)}, bf16[2,288,256]{2,1,0:T(8,128)(2,1)S(1)}, u32[]{:S(2)}, u32[]{:S(2)}) collective-permute-start(bf16[2,288,256]{2,1,0:T(8,128)(2,1)S(1)} %pad_maximum_fusion.2), channel_id=1, source_target_pairs={{0,4},{1,5},{2,6},{3,7},{4,8},{5,9},{6,10},{7,11},{8,12},{9,13},{1... | collective-permute-start | bytes 884744 | tf_op jit(solution)/shard_map/ppermute | solution.py:525
  37.0 14.7 %collective-permute-start.10 = (bf16[4,288,256]{2,1,0:T(8,128)(2,1)S(1)}, bf16[4,288,256]{2,1,0:T(8,128)(2,1)S(1)}, u32[]{:S(2)}, u32[]{:S(2)}) collective-permute-start(bf16[4,288,256]{2,1,0:T(8,128)(2,1)S(1)} %pad_maximum_fusion.a.refs_0_), channel_id=1, source_target_pairs={{0,16},{16,0},{32,48},{48,32},{64,80},{80,64},{96,112},{112,96},{1... | collective-permute-start | bytes 1769480 | tf_op jit(solution)/shard_map/ppermute | solution.py:546
  39.0 8.9 %collective-permute-start.6 = (bf16[2,288,256]{2,1,0:T(8,128)(2,1)S(1)}, bf16[2,288,256]{2,1,0:T(8,128)(2,1)S(1)}, u32[]{:S(2)}, u32[]{:S(2)}) collective-permute-start(bf16[2,288,256]{2,1,0:T(8,128)(2,1)S(1)} %collective-permute-done.5.d_second), channel_id=1, source_target_pairs={{0,12},{1,13},{2,14},{3,15},{4,0},{5,1},{6,2},{7,3},{8,4},{9,5},{1... | collective-permute-start | bytes 884744 | tf_op jit(solution)/shard_map/ppermute | solution.py:528
  41.2 7.1 %collective-permute-start.2 = (bf16[2,288,256]{2,1,0:T(8,128)(2,1)S(1)}, bf16[2,288,256]{2,1,0:T(8,128)(2,1)S(1)}, u32[]{:S(2)}, u32[]{:S(2)}) collective-permute-start(bf16[2,288,256]{2,1,0:T(8,128)(2,1)S(1)} %collective-permute-done.1.u_first), channel_id=1, source_target_pairs={{0,4},{1,5},{2,6},{3,7},{4,8},{5,9},{6,10},{7,11},{8,12},{9,13},{1... | collective-permute-start | bytes 884744 | tf_op jit(solution)/shard_map/ppermute | solution.py:527
  44.5 7.2 %collective-permute-start.12 = (bf16[4,288,256]{2,1,0:T(8,128)(2,1)S(1)}, bf16[4,288,256]{2,1,0:T(8,128)(2,1)S(1)}, u32[]{:S(2)}, u32[]{:S(2)}) collective-permute-start(bf16[4,288,256]{2,1,0:T(8,128)(2,1)S(1)} %get-tuple-element.68), channel_id=1, source_target_pairs={{0,16},{16,0},{32,48},{48,32},{64,80},{80,64},{96,112},{112,96},{1... | collective-permute-start | bytes 1769480 | tf_op jit(solution)/shard_map/ppermute | solution.py:547
  47.0 4.7 %collective-permute-start.11 = (bf16[4,288,256]{2,1,0:T(8,128)(2,1)S(1)}, bf16[4,288,256]{2,1,0:T(8,128)(2,1)S(1)}, u32[]{:S(2)}, u32[]{:S(2)}) collective-permute-start(bf16[4,288,256]{2,1,0:T(8,128)(2,1)S(1)} %get-tuple-element.69), channel_id=1, source_target_pairs={{0,16},{16,0},{32,48},{48,32},{64,80},{80,64},{96,112},{112,96},{1... | collective-permute-start | bytes 1769480 | tf_op jit(solution)/shard_map/ppermute | solution.py:547
  48.4 4.9 %collective-permute-start.9 = (bf16[4,288,256]{2,1,0:T(8,128)(2,1)S(1)}, bf16[4,288,256]{2,1,0:T(8,128)(2,1)S(1)}, u32[]{:S(2)}, u32[]{:S(2)}) collective-permute-start(bf16[4,288,256]{2,1,0:T(8,128)(2,1)S(1)} %maximum_add_fusion.far.refs_3_), channel_id=1, source_target_pairs={{0,16},{16,0},{32,48},{48,32},{64,80},{80,64},{96,112},{112,96},{1... | collective-permute-start | bytes 1769480 | tf_op jit(solution)/shard_map/ppermute | solution.py:556
  54.1 24.6 %copy-start.1 = (bf16[24,256]{1,0:T(8,128)(2,1)S(1)}, bf16[24,256]{1,0:T(8,128)(2,1)}, u32[]{:S(2)}) copy-start(bf16[24,256]{1,0:T(8,128)(2,1)} %refs_11_.1) | copy-start | bytes 36868
  54.1 24.6 %copy-start.2 = (f32[256]{0:T(256)S(1)}, f32[256]{0:T(256)}, u32[]{:S(2)}) copy-start(f32[256]{0:T(256)} %param.8) | copy-start | bytes 3076
  78.7 2.7 %collective-permute-start.13 = (bf16[16,128,256]{2,1,0:T(8,128)(2,1)S(1)}, bf16[16,128,256]{2,1,0:T(8,128)(2,1)S(1)}, u32[]{:S(2)}, u32[]{:S(2)}) collective-permute-start(bf16[16,128,256]{2,1,0:T(8,128)(2,1)S(1)} %get-tuple-element.63), channel_id=1, source_target_pairs={{0,16},{16,0},{32,48},{48,32},{64,80},{80,64},{96,112},{112,96},{1... | collective-permute-start | bytes 3145736 | tf_op jit(solution)/shard_map/ppermute | solution.py:595

commit v11 on v10

--- a/solution.py
+++ b/solution.py
@@ -92,17 +92,11 @@
 
 
 def pack_kernel(
-    student_in, teacher_in, source_in, lengths_in, gain_in,
+    student, teacher, source_in, lengths_in, gain_in,
     out, student_row, teacher_row, weight, gain_out,
-    student, teacher, source, lengths, gain, sems,
+    source, lengths, gain, sems,
 ):
-    pairs = (
-        (source_in, source),
-        (lengths_in, lengths),
-        (gain_in, gain),
-        (student_in, student),
-        (teacher_in, teacher),
-    )
+    pairs = ((source_in, source), (lengths_in, lengths), (gain_in, gain))
     copies = []
     for n, (place, held) in enumerate(pairs):
         copies.append(pltpu.make_async_copy(place, held, sems.at[n]))
@@ -117,8 +111,6 @@
     for k, part in enumerate(split(own_gain, 3)):
         spread = jnp.where(row == k, part.astype(F32), spread)
     gain_out[...] = spread
-    copies[3].wait()
-    copies[4].wait()
     for c in range(2):
         rows = teacher[:, c * HALF_T : (c + 1) * HALF_T].astype(F32)
         tail = rows[:, HALF_S:]
@@ -495,15 +487,13 @@
         out_shape=(
             shape((GROUPS, PACK, HALF_S), BF), table, table, row, shape((16, HALF_S), F32)
         ),
-        in_specs=[HBM] * 5,
+        in_specs=[VMEM] * 2 + [HBM] * 3,
         out_specs=(VMEM,) * 5,
         scratch_shapes=[
-            pltpu.VMEM((ROWS, 2 * HALF_S), BF),
-            pltpu.VMEM((ROWS, 2 * HALF_T), BF),
             pltpu.VMEM((1, episodes), jnp.int32),
             pltpu.VMEM((1, episodes), jnp.int32),
             pltpu.VMEM((1, 2 * HALF_S), F32),
-            pltpu.SemaphoreType.DMA((5,)),
+            pltpu.SemaphoreType.DMA((3,)),
         ],
         compiler_params=params(4),
     )(

time: 116 us -> 116 us (level)
  no operation moved by 1% of the time
where the time goes in v11:
time: 116 us
  blocking collectives  76.5 us (66%)
  starting transfers between devices  19.1 us (16%)
  Pallas kernels  13 us (11%)
  waiting for transfers between devices  6.18 us (5%)
    all_to_all x5, blocking collectives, exchange(): return lax.all_to_all(x, axis, 0, 0, tiled=True)  76.5 us
    ppermute x1, starting transfers between devices, local(): other_far = lax.ppermute(far, 'grp', CORE_SWAP)  3.3 us
    ppermute x1, starting transfers between devices, local(): three = lax.ppermute(block, BOTH, ring(1, 3))  2.81 us
    ppermute x1, waiting for transfers between devices, local(): three = lax.ppermute(block, BOTH, ring(1, 3))  2.63 us
    pallas_call x1, Pallas kernels, local(): pl.pallas_call(forward_own, out_shape=partial + (pltpu.VMEM(teacher_head....  2.62 us
    ppermute x2, starting transfers between devices, local(): lax.ppermute(part + zero.astype(BF), 'grp', CORE_SWAP)  2.6 us
    ppermute x1, starting transfers between devices, local(): d_first = lax.ppermute(first, BOTH, ring(2, 3))  2.58 us
    pallas_call x1, Pallas kernels, local(): pl.pallas_call(backward_two, out_shape=(half_rows, shape((2 * ROWS + 8, L...  2.51 us
  transfers between devices with their start and end apart: 14, of which 7 were waited for; matrix products, arithmetic and copies ran while one was open for 0% of the time, Pallas kernels for 6%

profile of v11, /device:TPU:1, one launch (start us, length us, event | category | flops | bytes accessed | tf_op | source)
XLA Modules:
  0.0 116.0 jit_solution(5639433978527787671)
XLA Ops:
  0.6 2.0 %shard_map.102 = (bf16[16,56,128]{2,1,0:T(8,128)(2,1)S(1)}, s32[1,256]{1,0:T(1,128)S(1)}, s32[1,256]{1,0:T(1,128)S(1)}, f32[1,256]{1,0:T(1,128)S(1)}, f32[16,128]{1,0:T(8,128)S(1)}) custom-call(bf16[24,256]{1,0:T(8,128)(2,1)} %refs_11_.1, bf16[24,320]{1,0:T(8,128)(2,1)} %teacher.1, s32[1,192]{1,0:T(1,128)} %bitcast.19, s32[1,192]{1,0:T(1,128)} %bitcast.20, ...), custom_call_target="tpu_custom_call" | custom-call | tf_op jit(solution)/shard_map/pallas_call | solution.py:485
  2.6 20.8 %all_to_all.25.held = bf16[16,56,128]{2,1,0:T(8,128)(2,1)S(1)} all-to-all(bf16[16,56,128]{2,1,0:T(8,128)(2,1)S(1)} %get-tuple-element.36), channel_id=1, replica_groups=mesh['grp'=16,'voc'=16] {'grp'}, dimensions={0} | all-to-all | bytes 458752 | tf_op jit(solution)/shard_map/all_to_all | solution.py:468
  23.8 2.8 %collective-permute-start.4 = (bf16[288,256]{1,0:T(8,128)(2,1)S(1)}, bf16[288,256]{1,0:T(8,128)(2,1)S(1)}, u32[]{:S(2)}, u32[]{:S(2)}) collective-permute-start(bf16[288,256]{1,0:T(8,128)(2,1)S(1)} %shard_map.103.block), channel_id=1, source_target_pairs={{0,3},{1,0},{2,1},{3,2},{4,7},{5,4},{6,5},{7,6},{8,11},{9,8},{10,9... | collective-permute-start | bytes 442376 | tf_op jit(solution)/shard_map/ppermute | solution.py:509
  27.0 0.7 collective-permute-start
  27.7 2.6 %collective-permute-done.4 = bf16[288,256]{1,0:T(8,128)(2,1)S(1)} collective-permute-done((bf16[288,256]{1,0:T(8,128)(2,1)S(1)}, bf16[288,256]{1,0:T(8,128)(2,1)S(1)}, u32[]{:S(2)}, u32[]{:S(2)}) %collective-permute-start.4) | collective-permute-done | bytes 147488 | tf_op jit(solution)/shard_map/ppermute | solution.py:509
  30.3 2.1 %collective-permute-done.3 = bf16[288,256]{1,0:T(8,128)(2,1)S(1)} collective-permute-done((bf16[288,256]{1,0:T(8,128)(2,1)S(1)}, bf16[288,256]{1,0:T(8,128)(2,1)S(1)}, u32[]{:S(2)}, u32[]{:S(2)}) %collective-permute-start.3) | collective-permute-done | bytes 147488 | tf_op jit(solution)/shard_map/ppermute | solution.py:510
  32.5 2.4 %collective-permute-start.5 = (bf16[2,288,256]{2,1,0:T(8,128)(2,1)S(1)}, bf16[2,288,256]{2,1,0:T(8,128)(2,1)S(1)}, u32[]{:S(2)}, u32[]{:S(2)}) collective-permute-start(bf16[2,288,256]{2,1,0:T(8,128)(2,1)S(1)} %pad_maximum_fusion.2), channel_id=1, source_target_pairs={{0,12},{1,13},{2,14},{3,15},{4,0},{5,1},{6,2},{7,3},{8,4},{9,5},{1... | collective-permute-start | bytes 884744 | tf_op jit(solution)/shard_map/ppermute | solution.py:514
  35.0 2.6 %collective-permute-start.8 = (bf16[2,288,256]{2,1,0:T(8,128)(2,1)S(1)}, bf16[2,288,256]{2,1,0:T(8,128)(2,1)S(1)}, u32[]{:S(2)}, u32[]{:S(2)}) collective-permute-start(bf16[2,288,256]{2,1,0:T(8,128)(2,1)S(1)} %pad_maximum_fusion.1), channel_id=1, source_target_pairs={{0,12},{1,13},{2,14},{3,15},{4,0},{5,1},{6,2},{7,3},{8,4},{9,5},{1... | collective-permute-start | bytes 884744 | tf_op jit(solution)/shard_map/ppermute | solution.py:516
  37.8 2.0 %collective-permute-start.10 = (bf16[4,288,256]{2,1,0:T(8,128)(2,1)S(1)}, bf16[4,288,256]{2,1,0:T(8,128)(2,1)S(1)}, u32[]{:S(2)}, u32[]{:S(2)}) collective-permute-start(bf16[4,288,256]{2,1,0:T(8,128)(2,1)S(1)} %pad_maximum_fusion.a.refs_0_), channel_id=1, source_target_pairs={{0,16},{16,0},{32,48},{48,32},{64,80},{80,64},{96,112},{112,96},{1... | collective-permute-start | bytes 1769480 | tf_op jit(solution)/shard_map/ppermute | solution.py:536
  39.8 2.1 %collective-permute-start.6 = (bf16[2,288,256]{2,1,0:T(8,128)(2,1)S(1)}, bf16[2,288,256]{2,1,0:T(8,128)(2,1)S(1)}, u32[]{:S(2)}, u32[]{:S(2)}) collective-permute-start(bf16[2,288,256]{2,1,0:T(8,128)(2,1)S(1)} %collective-permute-done.5.d_second), channel_id=1, source_target_pairs={{0,12},{1,13},{2,14},{3,15},{4,0},{5,1},{6,2},{7,3},{8,4},{9,5},{1... | collective-permute-start | bytes 884744 | tf_op jit(solution)/shard_map/ppermute | solution.py:518
  42.0 2.6 %shard_map.104 = (f32[384,256]{1,0:T(8,128)S(1)}, f32[384,256]{1,0:T(8,128)S(1)}, f32[16,256]{1,0:T(8,128)S(1)}, bf16[5120,384]{1,0:T(8,128)(2,1)S(1)}, f32[1,256]{1,0:T(1,128)S(1)}) custom-call(bf16[4,288,256]{2,1,0:T(8,128)(2,1)S(1)} %pad_maximum_fusion.a.refs_0_, bf16[2,288,256]{2,1,0:T(8,128)(2,1)S(1)} %collective-permute-done.1.u_first, ...), custom_call_target="tpu_custom_call" | custom-call | flops 226492416 | bytes 4194304 | tf_op jit(solution)/shard_map/pallas_call | solution.py:527
  45.3 2.5 %collective-permute-start.12 = (bf16[4,288,256]{2,1,0:T(8,128)(2,1)S(1)}, bf16[4,288,256]{2,1,0:T(8,128)(2,1)S(1)}, u32[]{:S(2)}, u32[]{:S(2)}) collective-permute-start(bf16[4,288,256]{2,1,0:T(8,128)(2,1)S(1)} %get-tuple-element.68), channel_id=1, source_target_pairs={{0,16},{16,0},{32,48},{48,32},{64,80},{80,64},{96,112},{112,96},{1... | collective-permute-start | bytes 1769480 | tf_op jit(solution)/shard_map/ppermute | solution.py:537
  47.9 0.8 shard_map.105
  49.2 3.3 %collective-permute-start.9 = (bf16[4,288,256]{2,1,0:T(8,128)(2,1)S(1)}, bf16[4,288,256]{2,1,0:T(8,128)(2,1)S(1)}, u32[]{:S(2)}, u32[]{:S(2)}) collective-permute-start(bf16[4,288,256]{2,1,0:T(8,128)(2,1)S(1)} %maximum_add_fusion.far.refs_3_), channel_id=1, source_target_pairs={{0,16},{16,0},{32,48},{48,32},{64,80},{80,64},{96,112},{112,96},{1... | collective-permute-start | bytes 1769480 | tf_op jit(solution)/shard_map/ppermute | solution.py:546
  52.5 1.3 %shard_map.106 = (f32[384,256]{1,0:T(8,128)S(1)}, f32[384,256]{1,0:T(8,128)S(1)}, f32[16,256]{1,0:T(8,128)S(1)}) custom-call(bf16[4,288,256]{2,1,0:T(8,128)(2,1)S(1)} %maximum_add_fusion.far.refs_3_, bf16[4,288,256]{2,1,0:T(8,128)(2,1)S(1)} %collective-permute-done.10.other_a.refs_4_, bf16[4,288,256]{2,1,0:T(8,128)(2,1)S(1)} %collective-permute-done.11.other_u.refs_5_, ...), custom_call_target="tpu_custom_call" | custom-call | flops 905969664 | bytes 4194304 | tf_op jit(solution)/shard_map/pallas_call | solution.py:547
  54.1 0.8 shard_map.107
  54.9 9.4 %all_to_all.26.stats = f32[16,8,256]{2,1,0:T(8,128)S(1)} all-to-all(f32[16,8,256]{2,1,0:T(8,128)S(1)} %get-tuple-element.52), channel_id=1, replica_groups=mesh['grp'=16,'voc'=16] {'voc'}, dimensions={0} | all-to-all | bytes 262144 | tf_op jit(solution)/shard_map/all_to_all | solution.py:468
  64.5 13.7 %all_to_all.27.stats = f32[16,8,256]{2,1,0:T(8,128)S(1)} all-to-all(f32[16,8,256]{2,1,0:T(8,128)S(1)} %shard_map.108), channel_id=1, replica_groups=mesh['grp'=16,'voc'=16] {'grp'}, dimensions={0} | all-to-all | bytes 262144 | tf_op jit(solution)/shard_map/all_to_all | solution.py:468
  78.2 1.3 %shard_map.109 = (bf16[384,256]{1,0:T(8,128)(2,1)S(1)}, bf16[384,256]{1,0:T(8,128)(2,1)S(1)}, bf16[16,128,256]{2,1,0:T(8,128)(2,1)S(1)}, f32[1,256]{1,0:T(1,128)S(1)}, f32[1,1]{1,0:T(1,128)}) custom-call(f32[16,8,256]{2,1,0:T(8,128)S(1)} %all_to_all.27.stats, f32[8,256]{1,0:T(8,128)S(1)} %get-tuple-element.53.tops, f32[384,256]{1,0:T(8,128)S(1)} %get-tuple-element.54.exp_in, ...), custom_call_target="tpu_custom_call" | custom-call | flops 402653184 | bytes 4194304 | tf_op jit(solution)/shard_map/pallas_call | solution.py:572
  79.5 2.5 %shard_map.110 = (bf16[16,128,256]{2,1,0:T(8,128)(2,1)S(1)}, f32[56,256]{1,0:T(8,128)S(1)}, bf16[4096,384]{1,0:T(8,128)(2,1)}) custom-call(bf16[4,288,256]{2,1,0:T(8,128)(2,1)S(1)} %pad_maximum_fusion.a.refs_0_, bf16[4,288,256]{2,1,0:T(8,128)(2,1)S(1)} %constant_dynamic-update-slice_fusion.u.refs_1_, ...), custom_call_target="tpu_custom_call" | custom-call | flops 1207959552 | bytes 4194304 | tf_op jit(solution)/shard_map/pallas_call | solution.py:586
  82.4 19.1 %all_to_all.28.pieces = bf16[16,128,256]{2,1,0:T(8,128)(2,1)S(1)} all-to-all(bf16[16,128,256]{2,1,0:T(8,128)(2,1)S(1)} %shard_map.111), channel_id=1, replica_groups=mesh['grp'=16,'voc'=16] {'voc'}, dimensions={0} | all-to-all | bytes 2097152 | tf_op jit(solution)/shard_map/all_to_all | solution.py:468
  101.5 0.4 shard_map.112
  102.0 13.4 %all_to_all.29.pieces = bf16[16,32,128]{2,1,0:T(8,128)(2,1)S(1)} all-to-all(bf16[16,32,128]{2,1,0:T(8,128)(2,1)S(1)} %shard_map.112), channel_id=1, replica_groups=mesh['grp'=16,'voc'=16] {'grp'}, dimensions={0} | all-to-all | bytes 262144 | tf_op jit(solution)/shard_map/all_to_all | solution.py:468
  115.4 0.6 shard_map.113
  (38 shorter events, 3.3 us)
Async XLA Ops:
  0.6 41.4 %copy-start = (bf16[4096,384]{1,0:T(8,128)(2,1)S(1)}, bf16[4096,384]{1,0:T(8,128)(2,1)}, u32[]{:S(2)}) copy-start(bf16[4096,384]{1,0:T(8,128)(2,1)} %refs_10_.1) | copy-start | bytes 9437188
  23.8 6.5 %collective-permute-start.4 = (bf16[288,256]{1,0:T(8,128)(2,1)S(1)}, bf16[288,256]{1,0:T(8,128)(2,1)S(1)}, u32[]{:S(2)}, u32[]{:S(2)}) collective-permute-start(bf16[288,256]{1,0:T(8,128)(2,1)S(1)} %shard_map.103.block), channel_id=1, source_target_pairs={{0,3},{1,0},{2,1},{3,2},{4,7},{5,4},{6,5},{7,6},{8,11},{9,8},{10,9... | collective-permute-start | bytes 442376 | tf_op jit(solution)/shard_map/ppermute | solution.py:509
  26.6 5.8 %collective-permute-start.3 = (bf16[288,256]{1,0:T(8,128)(2,1)S(1)}, bf16[288,256]{1,0:T(8,128)(2,1)S(1)}, u32[]{:S(2)}, u32[]{:S(2)}) collective-permute-start(bf16[288,256]{1,0:T(8,128)(2,1)S(1)} %shard_map.103.block), channel_id=1, source_target_pairs={{0,2},{1,3},{2,0},{3,1},{4,6},{5,7},{6,4},{7,5},{8,10},{9,11},{10,... | collective-permute-start | bytes 442376 | tf_op jit(solution)/shard_map/ppermute | solution.py:510
  27.0 7.8 %collective-permute-start = (bf16[288,256]{1,0:T(8,128)(2,1)S(1)}, bf16[288,256]{1,0:T(8,128)(2,1)S(1)}, u32[]{:S(2)}, u32[]{:S(2)}) collective-permute-start(bf16[288,256]{1,0:T(8,128)(2,1)S(1)} %shard_map.103.block), channel_id=1, source_target_pairs={{0,1},{1,2},{2,3},{3,0},{4,5},{5,6},{6,7},{7,4},{8,9},{9,10},{10,1... | collective-permute-start | bytes 442376 | tf_op jit(solution)/shard_map/ppermute | solution.py:508
  32.5 7.3 %collective-permute-start.5 = (bf16[2,288,256]{2,1,0:T(8,128)(2,1)S(1)}, bf16[2,288,256]{2,1,0:T(8,128)(2,1)S(1)}, u32[]{:S(2)}, u32[]{:S(2)}) collective-permute-start(bf16[2,288,256]{2,1,0:T(8,128)(2,1)S(1)} %pad_maximum_fusion.2), channel_id=1, source_target_pairs={{0,12},{1,13},{2,14},{3,15},{4,0},{5,1},{6,2},{7,3},{8,4},{9,5},{1... | collective-permute-start | bytes 884744 | tf_op jit(solution)/shard_map/ppermute | solution.py:514
  34.9 7.2 %collective-permute-start.1 = (bf16[2,288,256]{2,1,0:T(8,128)(2,1)S(1)}, bf16[2,288,256]{2,1,0:T(8,128)(2,1)S(1)}, u32[]{:S(2)}, u32[]{:S(2)}) collective-permute-start(bf16[2,288,256]{2,1,0:T(8,128)(2,1)S(1)} %pad_maximum_fusion.1), channel_id=1, source_target_pairs={{0,4},{1,5},{2,6},{3,7},{4,8},{5,9},{6,10},{7,11},{8,12},{9,13},{1... | collective-permute-start | bytes 884744 | tf_op jit(solution)/shard_map/ppermute | solution.py:513
  35.0 9.7 %collective-permute-start.8 = (bf16[2,288,256]{2,1,0:T(8,128)(2,1)S(1)}, bf16[2,288,256]{2,1,0:T(8,128)(2,1)S(1)}, u32[]{:S(2)}, u32[]{:S(2)}) collective-permute-start(bf16[2,288,256]{2,1,0:T(8,128)(2,1)S(1)} %pad_maximum_fusion.1), channel_id=1, source_target_pairs={{0,12},{1,13},{2,14},{3,15},{4,0},{5,1},{6,2},{7,3},{8,4},{9,5},{1... | collective-permute-start | bytes 884744 | tf_op jit(solution)/shard_map/ppermute | solution.py:516
  37.7 7.5 %collective-permute-start.7 = (bf16[2,288,256]{2,1,0:T(8,128)(2,1)S(1)}, bf16[2,288,256]{2,1,0:T(8,128)(2,1)S(1)}, u32[]{:S(2)}, u32[]{:S(2)}) collective-permute-start(bf16[2,288,256]{2,1,0:T(8,128)(2,1)S(1)} %pad_maximum_fusion.2), channel_id=1, source_target_pairs={{0,4},{1,5},{2,6},{3,7},{4,8},{5,9},{6,10},{7,11},{8,12},{9,13},{1... | collective-permute-start | bytes 884744 | tf_op jit(solution)/shard_map/ppermute | solution.py:515
  37.8 14.7 %collective-permute-start.10 = (bf16[4,288,256]{2,1,0:T(8,128)(2,1)S(1)}, bf16[4,288,256]{2,1,0:T(8,128)(2,1)S(1)}, u32[]{:S(2)}, u32[]{:S(2)}) collective-permute-start(bf16[4,288,256]{2,1,0:T(8,128)(2,1)S(1)} %pad_maximum_fusion.a.refs_0_), channel_id=1, source_target_pairs={{0,16},{16,0},{32,48},{48,32},{64,80},{80,64},{96,112},{112,96},{1... | collective-permute-start | bytes 1769480 | tf_op jit(solution)/shard_map/ppermute | solution.py:536
  39.8 8.9 %collective-permute-start.6 = (bf16[2,288,256]{2,1,0:T(8,128)(2,1)S(1)}, bf16[2,288,256]{2,1,0:T(8,128)(2,1)S(1)}, u32[]{:S(2)}, u32[]{:S(2)}) collective-permute-start(bf16[2,288,256]{2,1,0:T(8,128)(2,1)S(1)} %collective-permute-done.5.d_second), channel_id=1, source_target_pairs={{0,12},{1,13},{2,14},{3,15},{4,0},{5,1},{6,2},{7,3},{8,4},{9,5},{1... | collective-permute-start | bytes 884744 | tf_op jit(solution)/shard_map/ppermute | solution.py:518
  42.0 7.1 %collective-permute-start.2 = (bf16[2,288,256]{2,1,0:T(8,128)(2,1)S(1)}, bf16[2,288,256]{2,1,0:T(8,128)(2,1)S(1)}, u32[]{:S(2)}, u32[]{:S(2)}) collective-permute-start(bf16[2,288,256]{2,1,0:T(8,128)(2,1)S(1)} %collective-permute-done.1.u_first), channel_id=1, source_target_pairs={{0,4},{1,5},{2,6},{3,7},{4,8},{5,9},{6,10},{7,11},{8,12},{9,13},{1... | collective-permute-start | bytes 884744 | tf_op jit(solution)/shard_map/ppermute | solution.py:517
  45.3 7.2 %collective-permute-start.12 = (bf16[4,288,256]{2,1,0:T(8,128)(2,1)S(1)}, bf16[4,288,256]{2,1,0:T(8,128)(2,1)S(1)}, u32[]{:S(2)}, u32[]{:S(2)}) collective-permute-start(bf16[4,288,256]{2,1,0:T(8,128)(2,1)S(1)} %get-tuple-element.68), channel_id=1, source_target_pairs={{0,16},{16,0},{32,48},{48,32},{64,80},{80,64},{96,112},{112,96},{1... | collective-permute-start | bytes 1769480 | tf_op jit(solution)/shard_map/ppermute | solution.py:537
  47.8 4.7 %collective-permute-start.11 = (bf16[4,288,256]{2,1,0:T(8,128)(2,1)S(1)}, bf16[4,288,256]{2,1,0:T(8,128)(2,1)S(1)}, u32[]{:S(2)}, u32[]{:S(2)}) collective-permute-start(bf16[4,288,256]{2,1,0:T(8,128)(2,1)S(1)} %get-tuple-element.69), channel_id=1, source_target_pairs={{0,16},{16,0},{32,48},{48,32},{64,80},{80,64},{96,112},{112,96},{1... | collective-permute-start | bytes 1769480 | tf_op jit(solution)/shard_map/ppermute | solution.py:537
  49.2 4.9 %collective-permute-start.9 = (bf16[4,288,256]{2,1,0:T(8,128)(2,1)S(1)}, bf16[4,288,256]{2,1,0:T(8,128)(2,1)S(1)}, u32[]{:S(2)}, u32[]{:S(2)}) collective-permute-start(bf16[4,288,256]{2,1,0:T(8,128)(2,1)S(1)} %maximum_add_fusion.far.refs_3_), channel_id=1, source_target_pairs={{0,16},{16,0},{32,48},{48,32},{64,80},{80,64},{96,112},{112,96},{1... | collective-permute-start | bytes 1769480 | tf_op jit(solution)/shard_map/ppermute | solution.py:546
  54.9 24.6 %copy-start.1 = (bf16[24,256]{1,0:T(8,128)(2,1)S(1)}, bf16[24,256]{1,0:T(8,128)(2,1)}, u32[]{:S(2)}) copy-start(bf16[24,256]{1,0:T(8,128)(2,1)} %refs_11_.1) | copy-start | bytes 36868
  54.9 24.6 %copy-start.2 = (f32[256]{0:T(256)S(1)}, f32[256]{0:T(256)}, u32[]{:S(2)}) copy-start(f32[256]{0:T(256)} %param.8) | copy-start | bytes 3076
  79.5 2.7 %collective-permute-start.13 = (bf16[16,128,256]{2,1,0:T(8,128)(2,1)S(1)}, bf16[16,128,256]{2,1,0:T(8,128)(2,1)S(1)}, u32[]{:S(2)}, u32[]{:S(2)}) collective-permute-start(bf16[16,128,256]{2,1,0:T(8,128)(2,1)S(1)} %get-tuple-element.63), channel_id=1, source_target_pairs={{0,16},{16,0},{32,48},{48,32},{64,80},{80,64},{96,112},{112,96},{1... | collective-permute-start | bytes 3145736 | tf_op jit(solution)/shard_map/ppermute | solution.py:585
